TPU v7x, 32 devices: a whole 2x2x4 slice. The times are simulated.
32 devices in a mesh: group: 2 (over y), node: 4 (over z), local: 2 (over x), pair: 2 (over core).
Axes of the slice: x: 2, y: 2, z: 4, core: 2. Of those that a mesh axis runs over, the one named last changes fastest.
Arguments:
- tokens: bfloat16 [512, 3584], P(('group', 'node', 'local', 'pair')), parts along dimension 0, may hold values from -6 to 6
- expert_ids: int32 [512, 8], P(('group', 'node', 'local', 'pair')), parts along dimension 0, may hold values from 0 to 15, all different within a row; in each aligned block of 16 rows (0 to 15, 16 to 31, ...) at most 16 rows name the same one
- combine_weights: bfloat16 [512, 8], P(('group', 'node', 'local', 'pair')), parts along dimension 0, may hold values from 0.099609375 to 1
- expert_weight: bfloat16 [16, 3584, 1024], P(('node', 'local', 'pair')), may hold values from -0.09375 to 0.09375
- query_latent: bfloat16 [512, 64, 512], P(('group', 'node', 'local', 'pair')), parts along dimension 0
- query_rope: bfloat16 [512, 4096], P(('group', 'node', 'local', 'pair')), parts along dimension 0
- cache_latent: bfloat16 [512, 128, 512], P(('group', 'node', 'local', 'pair')), parts along dimension 0
- cache_rope: bfloat16 [512, 64, 128], P(('group', 'node', 'local', 'pair')), parts along dimension 0
- lengths: int32 [512], P(('group', 'node', 'local', 'pair')), parts along dimension 0, may hold values from 2 to 128, as said below
Outputs:
- expert_mix: bfloat16 [512, 1024], P(('group', 'node', 'local', 'pair')), parts along dimension 0
- attended: bfloat16 [512, 64, 512], P(('group', 'node', 'local', 'pair')), parts along dimension 0
There are 2 independent parts, one for each index of `group`. A program takes and returns all parts, laid end to end along the dimension named above; an argument that names none is the same for every part. Nothing has to cross between parts.
Inputs may be any that keep to these rules, and one draw needn't show every extreme that they name: `expert_ids`: each row names 8 different experts; in each aligned block of 16 rows (one device's tokens) no expert is named by more than 16 rows, a bound that some block reaches. `lengths`: some sequence holds exactly 128 positions.
All inputs are finite; a program needn't handle non-finite values.
Results may differ from a plain program's by a relative error of at most 0.0085.
Values may be sent and summed in bfloat16 or wider, within the bound.
No kernel may reach another device: no remote copies, remote signals or barrier semaphores. Data moves between devices by JAX's collectives and lax.ppermute only.
A program may use at most 64 MiB of HBM per device.

v0:
```python
import jax
import jax.numpy as jnp
from jax import lax
from jax.sharding import PartitionSpec as P

score_scale = 192.0 ** (-0.5)


def slot_tables(picked, weights, experts, capacity):
    row_count, choose = picked.shape
    flat_picks = picked.reshape(-1)
    matches = (flat_picks[:, None] == jnp.arange(experts, dtype=jnp.int32)[None, :]).astype(
        jnp.int32
    )
    earlier = jnp.cumsum(matches, axis=0) - matches
    position = jnp.sum(earlier * matches, axis=1)
    slot_index = flat_picks * capacity + position
    slot_hits = (
        slot_index[:, None] == jnp.arange(experts * capacity, dtype=jnp.int32)[None, :]
    ).astype(jnp.float32)
    owner = (
        jnp.arange(row_count * choose, dtype=jnp.int32)[:, None] // choose
        == jnp.arange(row_count, dtype=jnp.int32)[None, :]
    ).astype(jnp.float32)
    dispatch = jnp.dot(slot_hits.T, owner, precision=lax.Precision.HIGHEST)
    combine = jnp.dot(
        owner.T,
        slot_hits * weights.astype(jnp.float32).reshape(-1)[:, None],
        precision=lax.Precision.HIGHEST,
    )
    return (dispatch, combine)


def attend(query_latent, query_rope, cache_latent, cache_rope, lengths):
    row_count, head_count, latent_size = query_latent.shape
    rope_size = cache_rope.shape[1]
    context = cache_rope.shape[2]
    rotary = query_rope.reshape(row_count, head_count, rope_size)
    scores = jnp.einsum(
        "rhc,rlc->rhl", query_latent, cache_latent, preferred_element_type=jnp.float32
    )
    scores = scores + jnp.einsum(
        "rhc,rcl->rhl", rotary, cache_rope, preferred_element_type=jnp.float32
    )
    scores = scores * score_scale
    visible = jnp.arange(context, dtype=jnp.int32)[None, None, :] < lengths[:, None, None]
    scores = jnp.where(visible, scores, -1e30)
    highest = jnp.max(scores, axis=2, keepdims=True)
    exponent = jnp.exp(scores - highest)
    weights_bf = (exponent / jnp.sum(exponent, axis=2, keepdims=True)).astype(jnp.bfloat16)
    return jnp.einsum(
        "rhl,rlc->rhc", weights_bf, cache_latent, preferred_element_type=jnp.float32
    ).astype(jnp.bfloat16)


def expert_part(tokens, expert_ids, combine_weights, expert_weight):
    row_count, model_width = tokens.shape
    choose = expert_ids.shape[1]
    experts = lax.axis_size(("node", "local", "pair"))
    capacity = min(row_count, 3 * max(1, (row_count * choose + experts - 1) // experts))
    matrix = expert_weight[0]
    dispatch, combine = slot_tables(expert_ids, combine_weights, experts, capacity)
    outgoing = jnp.dot(
        dispatch.astype(jnp.bfloat16), tokens, preferred_element_type=jnp.float32
    ).astype(jnp.bfloat16)
    outgoing = outgoing.reshape(experts, capacity, model_width)
    received = lax.all_to_all(
        outgoing, ("node", "local", "pair"), split_axis=0, concat_axis=0, tiled=True
    )
    hidden = jnp.dot(received.reshape(-1, model_width), matrix, preferred_element_type=jnp.float32)
    returned = lax.all_to_all(
        jax.nn.silu(hidden).astype(jnp.bfloat16).reshape(received.shape[:-1] + (matrix.shape[1],)),
        ("node", "local", "pair"),
        split_axis=0,
        concat_axis=0,
        tiled=True,
    )
    returned = returned.reshape(experts * capacity, -1).astype(jnp.float32)
    mixture = jnp.dot(combine, returned, precision=lax.Precision.HIGHEST)
    return mixture.astype(jnp.bfloat16)


def body(
    tokens,
    expert_ids,
    combine_weights,
    expert_weight,
    query_latent,
    query_rope,
    cache_latent,
    cache_rope,
    lengths,
):
    attended = attend(query_latent, query_rope, cache_latent, cache_rope, lengths)
    expert_mix = expert_part(tokens, expert_ids, combine_weights, expert_weight)
    return (expert_mix, attended)


def solution(mesh):
    return jax.shard_map(
        body,
        mesh=mesh,
        in_specs=(
            P(("group", "node", "local", "pair"), None),
            P(("group", "node", "local", "pair"), None),
            P(("group", "node", "local", "pair"), None),
            P(("node", "local", "pair"), None, None),
            P(("group", "node", "local", "pair"), None, None),
            P(("group", "node", "local", "pair"), None),
            P(("group", "node", "local", "pair"), None, None),
            P(("group", "node", "local", "pair"), None, None),
            P(("group", "node", "local", "pair")),
        ),
        out_specs=(
            P(("group", "node", "local", "pair"), None),
            P(("group", "node", "local", "pair"), None, None),
        ),
        check_vma=False,
    )
```

profile of v0, /device:TPU:0, one launch (start us, length us, event | category | flops | bytes accessed | tf_op | source)
XLA Modules:
  0.0 81.5 jit_solution(7248996533377026528)
XLA Ops:
  0.6 0.0 copy-start
  0.6 0.9 %copy.13 = s32[16,8]{1,0:T(8,128)S(1)} copy(s32[16,8]{0,1:T(8,128)} %param.10) | data formatting | bytes 1024 | tf_op args[1]
  1.6 0.1 reshape.92
  1.6 0.1 fusion.16
  1.7 0.2 reduce_window_sum.11
  1.9 0.2 select_reduce_fusion
  2.1 0.3 convolution_convert_fusion.2
  2.4 2.7 %convolution_convert_fusion = bf16[256,3584]{1,0:T(8,128)(2,1)} fusion(bf16[256,16]{1,0:T(8,128)(2,1)S(1)} %convolution_convert_fusion.2, bf16[16,3584]{1,0:T(8,128)(2,1)} %param.9), kind=kOutput, calls=%fused_computation.3 | convolution fusion | flops 30277632 | bytes 1957888 | tf_op jit(solution)/shard_map/dot_general | solution.py:63
  5.1 0.0 copy-start.4
  5.1 0.0 copy-start.3
  5.1 7.5 %all-to-all-start = ((bf16[16,16,3584]{2,1,0:T(8,128)(2,1)}), bf16[16,16,3584]{2,1,0:T(8,128)(2,1)}, u32[]{:S(2)}, u32[]{:S(2)}) async-start(bf16[16,16,3584]{2,1,0:T(8,128)(2,1)} %bitcast.21), calls=%async_computation | async-start | bytes 3670016 | tf_op jit(solution)/shard_map/all_to_all | solution.py:67
  12.7 0.0 copy-done.4
  12.7 0.1 copy.14
  12.8 0.1 reshape.98
  12.9 0.0 copy-done.3
  12.9 0.2 reshape.97
  13.1 0.0 copy-done.5
  13.1 0.1 iota_compare_fusion.7
  13.2 0.0 copy-done.2
  13.2 0.2 fusion.22
  13.4 35.9 %all-to-all-done = bf16[16,16,3584]{2,1,0:T(8,128)(2,1)} async-done(((bf16[16,16,3584]{2,1,0:T(8,128)(2,1)}), bf16[16,16,3584]{2,1,0:T(8,128)(2,1)}, u32[]{:S(2)}, u32[]{:S(2)}) %all-to-all-start) | async-done | bytes 1835040 | tf_op jit(solution)/shard_map/all_to_all | solution.py:67
  49.3 6.6 %multiply_convert_fusion = bf16[256,1024]{1,0:T(8,128)(2,1)} fusion(bf16[256,3584]{1,0:T(8,128)(2,1)} %bitcast.1, bf16[1,3584,1024]{2,1,0:T(8,128)(2,1)} %param.12), kind=kOutput, calls=%fused_computation.12 | convolution fusion | flops 1880358912 | bytes 9699328 | tf_op jit(solution)/shard_map/dot_general | solution.py:70
  55.9 10.2 %all-to-all-start.1 = ((bf16[16,16,1024]{2,1,0:T(8,128)(2,1)}), bf16[16,16,1024]{2,1,0:T(8,128)(2,1)S(1)}, u32[]{:S(2)}, u32[]{:S(2)}) async-start(bf16[16,16,1024]{2,1,0:T(8,128)(2,1)} %bitcast.23), calls=%async_computation.1 | async-start | bytes 1048576 | tf_op jit(solution)/shard_map/all_to_all | solution.py:71
  66.1 0.0 copy-done
  66.1 2.1 %fusion.6 = f32[16,64,128]{2,1,0:T(8,128)S(1)} fusion(f32[16,64,128]{2,1,0:T(8,128)S(1)} %fusion.22, bf16[16,64,512]{2,1,0:T(8,128)(2,1)} %param.13, bf16[16,128,512]{2,1,0:T(8,128)(2,1)S(1)} %copy-done, pred[16,128]{1,0:T(8,128)(4,1)S(1)} %iota_compare_fusion.7), kind=kOutput, calls=%fused_computation.9 | convolution fusion | flops 134610944 | bytes 4196352 | tf_op jit(solution)/shard_map/rhc,rlc->rhl/dot_general | solution.py:39
  68.1 0.0 copy-start.1
  68.2 0.8 copy-done.1
  68.9 0.3 fusion.21
  69.3 0.3 fusion.10
  69.6 4.1 %convolution_convert_fusion.1 = bf16[16,64,512]{2,1,0:T(8,128)(2,1)} fusion(bf16[16,128,512]{2,1,0:T(8,128)(2,1)S(1)} %copy-done, f32[16,64]{1,0:T(8,128)S(1)} %fusion.21, f32[16,64,128]{2,1,0:T(8,128)} %copy-done.1), kind=kOutput, calls=%fused_computation.4 | convolution fusion | flops 135136384 | bytes 3674112 | tf_op jit(solution)/shard_map/rhl,rlc->rhc/dot_general | solution.py:51
  73.7 6.9 %all-to-all-done.1 = bf16[16,16,1024]{2,1,0:T(8,128)(2,1)S(1)} async-done(((bf16[16,16,1024]{2,1,0:T(8,128)(2,1)}), bf16[16,16,1024]{2,1,0:T(8,128)(2,1)S(1)}, u32[]{:S(2)}, u32[]{:S(2)}) %all-to-all-start.1) | async-done | bytes 524320 | tf_op jit(solution)/shard_map/all_to_all | solution.py:71
  80.5 0.9 %convolution_convert_fusion.3 = bf16[16,1024]{1,0:T(8,128)(2,1)} fusion(f32[16,256]{1,0:T(8,128)S(1)} %fusion.10, bf16[256,1024]{1,0:T(8,128)(2,1)S(1)} %bitcast.22), kind=kOutput, calls=%fused_computation.11 | convolution fusion | flops 50348032 | bytes 573440 | tf_op jit(solution)/shard_map/dot_general | solution.py:79
  (3 shorter events, 0.0 us)
Async XLA Ops:
  0.6 65.4 %copy-start = (bf16[16,128,512]{2,1,0:T(8,128)(2,1)S(1)}, bf16[16,128,512]{2,1,0:T(8,128)(2,1)}, u32[]{:S(2)}) copy-start(bf16[16,128,512]{2,1,0:T(8,128)(2,1)} %param.15) | copy-start | bytes 6291460
  5.1 7.6 %copy-start.4 = (bf16[16,8]{0,1:T(8,128)(2,1)S(1)}, bf16[16,8]{0,1:T(8,128)(2,1)}, u32[]{:S(2)}) copy-start(bf16[16,8]{0,1:T(8,128)(2,1)} %param.11) | copy-start | bytes 772
  5.1 7.7 %copy-start.3 = (bf16[16,4096]{1,0:T(8,128)(2,1)S(1)}, bf16[16,4096]{1,0:T(8,128)(2,1)}, u32[]{:S(2)}) copy-start(bf16[16,4096]{1,0:T(8,128)(2,1)} %param.14) | copy-start | bytes 393220
  5.1 8.0 %copy-start.5 = (s32[16]{0:T(128)S(1)}, s32[16]{0:T(128)}, u32[]{:S(2)}) copy-start(s32[16]{0:T(128)} %param.17) | copy-start | bytes 196
  5.1 8.1 %copy-start.2 = (bf16[16,64,128]{2,1,0:T(8,128)(2,1)S(1)}, bf16[16,64,128]{2,1,0:T(8,128)(2,1)}, u32[]{:S(2)}) copy-start(bf16[16,64,128]{2,1,0:T(8,128)(2,1)} %param.16) | copy-start | bytes 786436
  5.1 44.2 %all-to-all-start = ((bf16[16,16,3584]{2,1,0:T(8,128)(2,1)}), bf16[16,16,3584]{2,1,0:T(8,128)(2,1)}, u32[]{:S(2)}, u32[]{:S(2)}) async-start(bf16[16,16,3584]{2,1,0:T(8,128)(2,1)} %bitcast.21), calls=%async_computation | async-start | bytes 3670016 | tf_op jit(solution)/shard_map/all_to_all | solution.py:67
  55.9 24.6 %all-to-all-start.1 = ((bf16[16,16,1024]{2,1,0:T(8,128)(2,1)}), bf16[16,16,1024]{2,1,0:T(8,128)(2,1)S(1)}, u32[]{:S(2)}, u32[]{:S(2)}) async-start(bf16[16,16,1024]{2,1,0:T(8,128)(2,1)} %bitcast.23), calls=%async_computation.1 | async-start | bytes 1048576 | tf_op jit(solution)/shard_map/all_to_all | solution.py:71
  68.1 0.8 copy-start.1
where the time goes:
time: 81.9 us; the launch traced here: 81.5 us
  waiting for transfers between devices  42.7 us (52%)
  starting transfers between devices  17.7 us (22%)
  matrix products  17.2 us (21%)
  local copies, waits for them, and re-layouts  2.21 us (3%)
  other arithmetic  0.85 us (1%)
    all_to_all x1, waiting for transfers between devices, expert_part(): lax.all_to_all(outgoing, ('node', 'local', 'pair'), split_axis=0, concat_...  35.9 us
    all_to_all x1, starting transfers between devices, expert_part(): lax.all_to_all(jax.nn.silu(hidden).astype(jnp.bfloat16).reshape(received....  10.2 us
    all_to_all x1, starting transfers between devices, expert_part(): lax.all_to_all(outgoing, ('node', 'local', 'pair'), split_axis=0, concat_...  7.54 us
    all_to_all x1, waiting for transfers between devices, expert_part(): lax.all_to_all(jax.nn.silu(hidden).astype(jnp.bfloat16).reshape(received....  6.86 us
    dot_general x1, matrix products, expert_part(): jnp.dot(received.reshape(-1, model_width), matrix, preferred_element_type...  6.61 us
    dot_general x1, matrix products, attend(): jnp.einsum('rhl,rlc->rhc', weights_bf, cache_latent, preferred_element_ty...  4.1 us
    dot_general x1, matrix products, expert_part(): jnp.dot(dispatch.astype(jnp.bfloat16), tokens, preferred_element_type=jnp...  2.74 us
    dot_general x1, matrix products, attend(): jnp.einsum('rhc,rlc->rhl', query_latent, cache_latent, preferred_element_...  2.07 us
  transfers between devices with their start and end apart: 2, of which 2 were waited for; matrix products, arithmetic and copies ran while one was open for 9% of the time, Pallas kernels for 0%

commit v1 on v0

v1 whole, which is shorter than its diff:
```python
import functools

import jax
import jax.numpy as jnp
from jax import lax
from jax.experimental import pallas as pl
from jax.experimental.pallas import tpu as pltpu
from jax.sharding import PartitionSpec as P

score_scale = 192.0 ** (-0.5)
EXPERT_AXES = ("node", "local", "pair")
LANES = 128


def slot_tables(picked, weights, experts, capacity):
    row_count, choose = picked.shape
    flat_picks = picked.reshape(-1)
    matches = (flat_picks[:, None] == jnp.arange(experts, dtype=jnp.int32)[None, :]).astype(
        jnp.int32
    )
    earlier = jnp.cumsum(matches, axis=0) - matches
    position = jnp.sum(earlier * matches, axis=1)
    slot_index = flat_picks * capacity + position
    slot_hits = (
        slot_index[:, None] == jnp.arange(experts * capacity, dtype=jnp.int32)[None, :]
    ).astype(jnp.float32)
    owner = (
        jnp.arange(row_count * choose, dtype=jnp.int32)[:, None] // choose
        == jnp.arange(row_count, dtype=jnp.int32)[None, :]
    ).astype(jnp.float32)
    dispatch = jnp.dot(slot_hits.T, owner, precision=lax.Precision.HIGHEST)
    combine = jnp.dot(
        owner.T,
        slot_hits * weights.astype(jnp.float32).reshape(-1)[:, None],
        precision=lax.Precision.HIGHEST,
    )
    return (dispatch, combine)


def attend_kernel(lengths_ref, ql_ref, qr_ref, cl_ref, cr_ref, out_ref):
    rows, heads, _ = ql_ref.shape
    context = cr_ref.shape[2]
    first = pl.program_id(0) * rows
    place = lax.broadcasted_iota(jnp.int32, (heads, context), 1)
    for r in range(rows):
        cached = cl_ref[r]
        scores = lax.dot_general(
            ql_ref[r], cached, (((1,), (1,)), ((), ())), preferred_element_type=jnp.float32
        )
        scores = scores + jnp.dot(qr_ref[r], cr_ref[r], preferred_element_type=jnp.float32)
        scores = jnp.where(place < lengths_ref[first + r], scores * score_scale, -1e30)
        exponent = jnp.exp(scores - jnp.max(scores, axis=1, keepdims=True))
        probs = (exponent / jnp.sum(exponent, axis=1, keepdims=True)).astype(jnp.bfloat16)
        out_ref[r] = jnp.dot(probs, cached, preferred_element_type=jnp.float32).astype(
            out_ref.dtype
        )


def attend(query_latent, query_rope, cache_latent, cache_rope, lengths):
    row_count, heads, latent = query_latent.shape
    rope, context = cache_rope.shape[1:]
    rotary = query_rope.reshape(row_count, heads, rope)
    step = 4 if row_count % 4 == 0 else 1

    def block(*tail):
        return pl.BlockSpec((step,) + tail, lambda i, lengths_ref: (i, 0, 0))

    flops = 2 * row_count * heads * context * (2 * latent + rope)
    return pl.pallas_call(
        attend_kernel,
        out_shape=jax.ShapeDtypeStruct((row_count, heads, latent), jnp.bfloat16),
        grid_spec=pltpu.PrefetchScalarGridSpec(
            num_scalar_prefetch=1,
            grid=(row_count // step,),
            in_specs=[
                block(heads, latent),
                block(heads, rope),
                block(context, latent),
                block(rope, context),
            ],
            out_specs=block(heads, latent),
        ),
        compiler_params=pltpu.CompilerParams(vmem_limit_bytes=24 * 2**20),
        cost_estimate=pl.CostEstimate(
            flops=flops,
            bytes_accessed=2 * row_count * (latent * (2 * heads + context) + rope * (heads + context)),
            transcendentals=row_count * heads * context,
        ),
    )(lengths, query_latent, rotary, cache_latent, cache_rope)


def expert_by_slots(tokens, expert_ids, combine_weights, expert_weight):
    row_count, model_width = tokens.shape
    choose = expert_ids.shape[1]
    experts = lax.axis_size(EXPERT_AXES)
    capacity = min(row_count, 3 * max(1, (row_count * choose + experts - 1) // experts))
    matrix = expert_weight[0]
    dispatch, combine = slot_tables(expert_ids, combine_weights, experts, capacity)
    outgoing = jnp.dot(
        dispatch.astype(jnp.bfloat16), tokens, preferred_element_type=jnp.float32
    ).astype(jnp.bfloat16)
    outgoing = outgoing.reshape(experts, capacity, model_width)
    received = lax.all_to_all(outgoing, EXPERT_AXES, split_axis=0, concat_axis=0, tiled=True)
    hidden = jnp.dot(received.reshape(-1, model_width), matrix, preferred_element_type=jnp.float32)
    returned = lax.all_to_all(
        jax.nn.silu(hidden).astype(jnp.bfloat16).reshape(received.shape[:-1] + (matrix.shape[1],)),
        EXPERT_AXES,
        split_axis=0,
        concat_axis=0,
        tiled=True,
    )
    returned = returned.reshape(experts * capacity, -1).astype(jnp.float32)
    mixture = jnp.dot(combine, returned, precision=lax.Precision.HIGHEST)
    return mixture.astype(jnp.bfloat16)


def payload_kernel(ids_ref, weights_ref, tokens_ref, out_ref):
    choose, rows = ids_ref.shape
    width = tokens_ref.shape[1]
    expert = lax.broadcasted_iota(jnp.int32, (LANES, rows), 0)
    table = jnp.zeros((LANES, rows), jnp.float32)
    for k in range(choose):
        table = table + jnp.where(
            expert == ids_ref[pl.ds(k, 1), :], weights_ref[pl.ds(k, 1), :].astype(jnp.float32), 0.0
        )
    eye = (
        lax.broadcasted_iota(jnp.int32, (rows, rows), 0)
        == lax.broadcasted_iota(jnp.int32, (rows, rows), 1)
    ).astype(jnp.bfloat16)
    out_ref[:, :width] = tokens_ref[...]
    out_ref[:, width:] = lax.dot_general(
        eye,
        table.astype(jnp.bfloat16),
        (((1,), (1,)), ((), ())),
        preferred_element_type=jnp.float32,
    ).astype(jnp.bfloat16)


def make_payload(tokens, expert_ids, combine_weights):
    rows, width = tokens.shape
    return pl.pallas_call(
        payload_kernel,
        out_shape=jax.ShapeDtypeStruct((rows, width + LANES), jnp.bfloat16),
        compiler_params=pltpu.CompilerParams(vmem_limit_bytes=4 * 2**20),
        cost_estimate=pl.CostEstimate(
            flops=0, bytes_accessed=4 * rows * width, transcendentals=0
        ),
    )(expert_ids.T, combine_weights.T, tokens)


def expert_kernel(count, scalar_ref, *refs):
    blocks, (own_ref, other_ref), outs = refs[:count], refs[count : count + 2], refs[count + 2 :]
    rows = jnp.concatenate([block[...] for block in blocks], axis=0) if count > 1 else blocks[0][...]
    width = own_ref.shape[0]
    features, shares = rows[:, :width], rows[:, width:].astype(jnp.float32)
    lane = lax.broadcasted_iota(jnp.int32, shares.shape, 1)
    total = None
    for which, matrix_ref in ((0, own_ref), (1, other_ref)):
        share = jnp.sum(jnp.where(lane == scalar_ref[which], shares, 0.0), axis=1, keepdims=True)
        hidden = jnp.dot(features, matrix_ref[...], preferred_element_type=jnp.float32)
        term = share * (hidden / (1.0 + jnp.exp(-hidden)))
        total = term if total is None else total + term
    total = total.astype(jnp.bfloat16)
    step = blocks[0].shape[0]
    for i, out_ref in enumerate(outs):
        out_ref[...] = total[i * step : (i + 1) * step]


def serve(blocks, own, other, experts_here):
    count = len(blocks)
    rows, padded = blocks[0].shape
    width, hidden = own.shape
    tile = 256
    weight_spec = pl.BlockSpec((width, tile), lambda n, s: (0, n))
    return pl.pallas_call(
        functools.partial(expert_kernel, count),
        out_shape=[jax.ShapeDtypeStruct((rows, hidden), jnp.bfloat16)] * count,
        grid_spec=pltpu.PrefetchScalarGridSpec(
            num_scalar_prefetch=1,
            grid=(hidden // tile,),
            in_specs=[pl.BlockSpec((rows, padded), lambda n, s: (0, 0))] * count
            + [weight_spec, weight_spec],
            out_specs=[pl.BlockSpec((rows, tile), lambda n, s: (0, n))] * count,
        ),
        compiler_params=pltpu.CompilerParams(vmem_limit_bytes=24 * 2**20),
        cost_estimate=pl.CostEstimate(
            flops=4 * count * rows * width * hidden,
            bytes_accessed=4 * width * hidden,
            transcendentals=2 * count * rows * hidden,
        ),
    )(experts_here, *blocks, own, other)


def swap(value, axis, size, mask):
    return lax.ppermute(value, axis, [(i, i ^ mask) for i in range(size)])


def expert_by_gather(tokens, expert_ids, combine_weights, expert_weight):
    nodes, locals_, pairs = (lax.axis_size(axis) for axis in EXPERT_AXES)
    own = expert_weight[0]
    other = swap(own, "pair", pairs, 1)
    here = lax.axis_index(EXPERT_AXES).astype(jnp.int32)
    experts_here = jnp.stack([here, here ^ 1])

    mine = make_payload(tokens, expert_ids, combine_weights)
    near = {0: mine}
    for n in range(nodes - 1, 0, -1):
        near[n] = swap(mine, "node", nodes, n)
    names = [(n, l) for l in range(locals_) for n in range(nodes)]
    blocks = [
        near[n] if l == 0 else swap(near[n], ("local"), locals_, l) for n, l in names
    ]
    parts = dict(zip(names, serve(blocks, own, other, experts_here)))
    total = parts[(0, 0)].astype(jnp.float32)
    for n, l in names[1:]:
        came = swap(parts[(n, l)], ("node", "local"), nodes * locals_, n * locals_ + l)
        total = total + came.astype(jnp.float32)
    return total.astype(jnp.bfloat16)


def expert_part(tokens, expert_ids, combine_weights, expert_weight):
    sizes = tuple(lax.axis_size(axis) for axis in EXPERT_AXES)
    rows, choose = tokens.shape[0], expert_ids.shape[1]
    experts = lax.axis_size(EXPERT_AXES)
    if sizes == (4, 2, 2) and rows * choose * 2 >= rows * experts and experts <= LANES:
        return expert_by_gather(tokens, expert_ids, combine_weights, expert_weight)
    return expert_by_slots(tokens, expert_ids, combine_weights, expert_weight)


def body(
    tokens,
    expert_ids,
    combine_weights,
    expert_weight,
    query_latent,
    query_rope,
    cache_latent,
    cache_rope,
    lengths,
):
    attended = attend(query_latent, query_rope, cache_latent, cache_rope, lengths)
    expert_mix = expert_part(tokens, expert_ids, combine_weights, expert_weight)
    return (expert_mix, attended)


def solution(mesh):
    rows = ("group",) + EXPERT_AXES
    return jax.shard_map(
        body,
        mesh=mesh,
        in_specs=(
            P(rows, None),
            P(rows, None),
            P(rows, None),
            P(EXPERT_AXES, None, None),
            P(rows, None, None),
            P(rows, None),
            P(rows, None, None),
            P(rows, None, None),
            P(rows),
        ),
        out_specs=(P(rows, None), P(rows, None, None)),
        check_vma=False,
    )
```

time: 81.9 us -> 63 us (0.77)
  waiting for transfers between devices: 42.7 us -> 7.75 us
  matrix products: 17.2 us -> 0 us
  Pallas kernels: 0 us -> 14.9 us
  local copies, waits for them, and re-layouts: 2.21 us -> 15.2 us
  starting transfers between devices: 17.7 us -> 22.3 us
    all_to_all x2 -> x0, waiting for transfers between devices: 42.7 us -> none  [the longest x1 35.9 us: expert_part(): lax.all_to_all(outgoing, ('node', 'local', 'pair'), split_axis=0, concat_...]
    ppermute x0 -> x15, starting transfers between devices: none -> 22.3 us  [swap(): return lax.ppermute(value, axis, [(i, i ^ mask) for i in range(size)])]
    all_to_all x2 -> x0, starting transfers between devices: 17.7 us -> none  [the longest x1 10.2 us: expert_part(): lax.all_to_all(jax.nn.silu(hidden).astype(jnp.bfloat16).reshape(received....]
    dot_general x8 -> x0, matrix products: 17.2 us -> none  [the longest x1 6.61 us: expert_part(): jnp.dot(received.reshape(-1, model_width), matrix, preferred_element_type...]
    pallas_call x0 -> x3, Pallas kernels: none -> 14.9 us  [the longest x1 7.4 us: serve(): pl.pallas_call(functools.partial(expert_kernel, count), out_shape=[jax.Sh...]
    unnamed x13 -> x36, local copies, waits for them, and re-layouts: 1.72 us -> 14.1 us
    ppermute x0 -> x15, waiting for transfers between devices: none -> 7.75 us  [swap(): return lax.ppermute(value, axis, [(i, i ^ mask) for i in range(size)])]
    convert_element_type x1, other arithmetic: 0.09 us -> 1.48 us  [expert_by_gather(): return total.astype(jnp.bfloat16)]
  transfers between devices with their start and end apart: 2 -> 15, of which waited for: 2 -> 4; matrix products, arithmetic and copies ran while one was open for 9% -> 2% of each run, Pallas kernels for 0% -> 12%
where the time goes in v1:
time: 63 us; the launch traced here: 62.5 us
  starting transfers between devices  22.3 us (35%)
  local copies, waits for them, and re-layouts  15.2 us (24%)
  Pallas kernels  14.9 us (24%)
  waiting for transfers between devices  7.75 us (12%)
  other arithmetic  1.56 us (2%)
  between operations  0.72 us (1%)
    ppermute x15, starting transfers between devices, swap(): return lax.ppermute(value, axis, [(i, i ^ mask) for i in range(size)])  22.3 us
    unnamed x36, local copies, waits for them, and re-layouts  14.1 us
    ppermute x15, waiting for transfers between devices, swap(): return lax.ppermute(value, axis, [(i, i ^ mask) for i in range(size)])  7.75 us
    pallas_call x1, Pallas kernels, serve(): pl.pallas_call(functools.partial(expert_kernel, count), out_shape=[jax.Sh...  7.4 us
    pallas_call x1, Pallas kernels, attend(): pl.pallas_call(attend_kernel, out_shape=jax.ShapeDtypeStruct((row_count,...  7.33 us
    convert_element_type x1, other arithmetic, expert_by_gather(): return total.astype(jnp.bfloat16)  1.48 us
  transfers between devices with their start and end apart: 15, of which 4 were waited for; matrix products, arithmetic and copies ran while one was open for 2% of the time, Pallas kernels for 12%

profile of v1, /device:TPU:0, one launch (start us, length us, event | category | flops | bytes accessed | tf_op | source)
XLA Modules:
  0.0 62.5 jit_solution(15610488525449615836)
XLA Ops:
  1.1 0.9 %copy-done.14 = bf16[16,3584]{1,0:T(8,128)(2,1)S(1)} copy-done((bf16[16,3584]{1,0:T(8,128)(2,1)S(1)}, bf16[16,3584]{1,0:T(8,128)(2,1)}, u32[]{:S(2)}) %copy-start.14) | copy-done | bytes 114712
  2.0 0.7 %copy-done.15 = s32[16,8]{0,1:T(8,128)S(1)} copy-done((s32[16,8]{0,1:T(8,128)S(1)}, s32[16,8]{0,1:T(8,128)}, u32[]{:S(2)}) %copy-start.15) | copy-done | bytes 536
  2.7 0.7 %copy-done.16 = bf16[16,8]{0,1:T(8,128)(2,1)S(1)} copy-done((bf16[16,8]{0,1:T(8,128)(2,1)S(1)}, bf16[16,8]{0,1:T(8,128)(2,1)}, u32[]{:S(2)}) %copy-start.16) | copy-done | bytes 280
  3.6 2.6 %collective-permute-start = (bf16[16,3712]{1,0:T(8,128)(2,1)S(1)}, bf16[16,3712]{1,0:T(8,128)(2,1)S(1)}, u32[]{:S(2)}, u32[]{:S(2)}) collective-permute-start(bf16[16,3712]{1,0:T(8,128)(2,1)S(1)} %shard_map.104.refs_0_), channel_id=1, source_target_pairs={{0,4},{4,0},{8,12},{12,8},{1,5},{5,1},{9,13},{13,9},{2,6},{6,2},{1... | collective-permute-start | bytes 356360 | tf_op jit(solution)/shard_map/ppermute | solution.py:195
  6.2 2.6 %collective-permute-start.1 = (bf16[16,3712]{1,0:T(8,128)(2,1)S(1)}, bf16[16,3712]{1,0:T(8,128)(2,1)S(1)}, u32[]{:S(2)}, u32[]{:S(2)}) collective-permute-start(bf16[16,3712]{1,0:T(8,128)(2,1)S(1)} %shard_map.104.refs_0_), channel_id=1, source_target_pairs={{0,8},{4,12},{8,0},{12,4},{1,9},{5,13},{9,1},{13,5},{2,10},{6,14},... | collective-permute-start | bytes 356360 | tf_op jit(solution)/shard_map/ppermute | solution.py:195
  8.8 1.7 %collective-permute-start.3 = (bf16[16,3712]{1,0:T(8,128)(2,1)S(1)}, bf16[16,3712]{1,0:T(8,128)(2,1)S(1)}, u32[]{:S(2)}, u32[]{:S(2)}) collective-permute-start(bf16[16,3712]{1,0:T(8,128)(2,1)S(1)} %shard_map.104.refs_0_), channel_id=1, source_target_pairs={{0,2},{2,0},{1,3},{3,1},{4,6},{6,4},{5,7},{7,5},{8,10},{10,8},{9,1... | collective-permute-start | bytes 356360 | tf_op jit(solution)/shard_map/ppermute | solution.py:195
  10.5 1.5 %collective-permute-done.refs_1_ = bf16[16,3712]{1,0:T(8,128)(2,1)S(1)} collective-permute-done((bf16[16,3712]{1,0:T(8,128)(2,1)S(1)}, bf16[16,3712]{1,0:T(8,128)(2,1)S(1)}, u32[]{:S(2)}, u32[]{:S(2)}) %collective-permute-start) | collective-permute-done | bytes 118816 | tf_op jit(solution)/shard_map/ppermute | solution.py:195
  12.0 1.7 %collective-permute-start.4 = (bf16[16,3712]{1,0:T(8,128)(2,1)S(1)}, bf16[16,3712]{1,0:T(8,128)(2,1)S(1)}, u32[]{:S(2)}, u32[]{:S(2)}) collective-permute-start(bf16[16,3712]{1,0:T(8,128)(2,1)S(1)} %collective-permute-done.refs_1_), channel_id=1, source_target_pairs={{0,2},{2,0},{1,3},{3,1},{4,6},{6,4},{5,7},{7,5},{8,10},{10,8},{9,1... | collective-permute-start | bytes 356360 | tf_op jit(solution)/shard_map/ppermute | solution.py:195
  13.7 4.6 %collective-permute-done.1.refs_2_ = bf16[16,3712]{1,0:T(8,128)(2,1)S(1)} collective-permute-done((bf16[16,3712]{1,0:T(8,128)(2,1)S(1)}, bf16[16,3712]{1,0:T(8,128)(2,1)S(1)}, u32[]{:S(2)}, u32[]{:S(2)}) %collective-permute-start.1) | collective-permute-done | bytes 118816 | tf_op jit(solution)/shard_map/ppermute | solution.py:195
  18.3 1.5 %collective-permute-start.5 = (bf16[16,3712]{1,0:T(8,128)(2,1)S(1)}, bf16[16,3712]{1,0:T(8,128)(2,1)S(1)}, u32[]{:S(2)}, u32[]{:S(2)}) collective-permute-start(bf16[16,3712]{1,0:T(8,128)(2,1)S(1)} %collective-permute-done.1.refs_2_), channel_id=1, source_target_pairs={{0,2},{2,0},{1,3},{3,1},{4,6},{6,4},{5,7},{7,5},{8,10},{10,8},{9,1... | collective-permute-start | bytes 356360 | tf_op jit(solution)/shard_map/ppermute | solution.py:195
  20.3 0.6 %copy-done.4 = bf16[16,3712]{1,0:T(8,128)(2,1)} copy-done((bf16[16,3712]{1,0:T(8,128)(2,1)}, bf16[16,3712]{1,0:T(8,128)(2,1)S(1)}, u32[]{:S(2)}) %copy-start.4) | copy-done | bytes 118808
  21.7 0.6 %copy-done.8 = bf16[16,3712]{1,0:T(8,128)(2,1)} copy-done((bf16[16,3712]{1,0:T(8,128)(2,1)}, bf16[16,3712]{1,0:T(8,128)(2,1)S(1)}, u32[]{:S(2)}) %copy-start.8) | copy-done | bytes 118808
  22.3 0.8 %collective-permute-done.5.refs_6_ = bf16[16,3712]{1,0:T(8,128)(2,1)S(1)} collective-permute-done((bf16[16,3712]{1,0:T(8,128)(2,1)S(1)}, bf16[16,3712]{1,0:T(8,128)(2,1)S(1)}, u32[]{:S(2)}, u32[]{:S(2)}) %collective-permute-start.5) | collective-permute-done | bytes 118816 | tf_op jit(solution)/shard_map/ppermute | solution.py:195
  23.1 0.6 %copy-done.10 = bf16[16,3712]{1,0:T(8,128)(2,1)} copy-done((bf16[16,3712]{1,0:T(8,128)(2,1)}, bf16[16,3712]{1,0:T(8,128)(2,1)S(1)}, u32[]{:S(2)}) %copy-start.10) | copy-done | bytes 118808
  23.8 0.9 %collective-permute-done.6.refs_7_ = bf16[16,3712]{1,0:T(8,128)(2,1)S(1)} collective-permute-done((bf16[16,3712]{1,0:T(8,128)(2,1)S(1)}, bf16[16,3712]{1,0:T(8,128)(2,1)S(1)}, u32[]{:S(2)}, u32[]{:S(2)}) %collective-permute-start.6) | collective-permute-done | bytes 118816 | tf_op jit(solution)/shard_map/ppermute | solution.py:195
  24.6 0.7 %copy-done.12 = bf16[16,3712]{1,0:T(8,128)(2,1)} copy-done((bf16[16,3712]{1,0:T(8,128)(2,1)}, bf16[16,3712]{1,0:T(8,128)(2,1)S(1)}, u32[]{:S(2)}) %copy-start.12) | copy-done | bytes 118808
  25.3 3.1 %copy-done = bf16[1,3584,1024]{2,1,0:T(8,128)(2,1)S(1)} copy-done((bf16[1,3584,1024]{2,1,0:T(8,128)(2,1)S(1)}, bf16[1,3584,1024]{2,1,0:T(8,128)(2,1)}, u32[]{:S(2)}) %copy-start) | copy-done | bytes 7340056
  28.4 0.9 %copy-done.5 = bf16[16,3712]{1,0:T(8,128)(2,1)S(1)} copy-done((bf16[16,3712]{1,0:T(8,128)(2,1)S(1)}, bf16[16,3712]{1,0:T(8,128)(2,1)}, u32[]{:S(2)}) %copy-start.5) | copy-done | bytes 118808
  29.3 0.9 %copy-done.7 = bf16[16,3712]{1,0:T(8,128)(2,1)S(1)} copy-done((bf16[16,3712]{1,0:T(8,128)(2,1)S(1)}, bf16[16,3712]{1,0:T(8,128)(2,1)}, u32[]{:S(2)}) %copy-start.7) | copy-done | bytes 118808
  30.2 0.9 %copy-done.9 = bf16[16,3712]{1,0:T(8,128)(2,1)S(1)} copy-done((bf16[16,3712]{1,0:T(8,128)(2,1)S(1)}, bf16[16,3712]{1,0:T(8,128)(2,1)}, u32[]{:S(2)}) %copy-start.9) | copy-done | bytes 118808
  31.1 0.9 %copy-done.11 = bf16[16,3712]{1,0:T(8,128)(2,1)S(1)} copy-done((bf16[16,3712]{1,0:T(8,128)(2,1)S(1)}, bf16[16,3712]{1,0:T(8,128)(2,1)}, u32[]{:S(2)}) %copy-start.11) | copy-done | bytes 118808
  32.0 0.9 %copy-done.13 = bf16[16,3712]{1,0:T(8,128)(2,1)S(1)} copy-done((bf16[16,3712]{1,0:T(8,128)(2,1)S(1)}, bf16[16,3712]{1,0:T(8,128)(2,1)}, u32[]{:S(2)}) %copy-start.13) | copy-done | bytes 118808
  32.9 7.4 %shard_map.105 = (bf16[16,1024]{1,0:T(8,128)(2,1)S(1)}, bf16[16,1024]{1,0:T(8,128)(2,1)}, bf16[16,1024]{1,0:T(8,128)(2,1)}, bf16[16,1024]{1,0:T(8,128)(2,1)S(1)}...) custom-call(s32[2]{0:T(128)S(1)} %pad_add_fusion.scalar_ref, ...), custom_call_target="tpu_custom_call" | custom-call | flops 1879048192 | bytes 14680064 | tf_op jit(solution)/shard_map/pallas_call | solution.py:175
  40.3 2.6 %collective-permute-start.10 = (bf16[16,1024]{1,0:T(8,128)(2,1)S(1)}, bf16[16,1024]{1,0:T(8,128)(2,1)S(1)}, u32[]{:S(2)}, u32[]{:S(2)}) collective-permute-start(bf16[16,1024]{1,0:T(8,128)(2,1)S(1)} %get-tuple-element.13), channel_id=1, source_target_pairs={{0,12},{2,14},{4,8},{6,10},{8,4},{10,6},{12,0},{14,2},{1,13},{3,15... | collective-permute-start | bytes 98312 | tf_op jit(solution)/shard_map/ppermute | solution.py:195
  42.9 1.5 %collective-permute-start.11 = (bf16[16,1024]{1,0:T(8,128)(2,1)S(1)}, bf16[16,1024]{1,0:T(8,128)(2,1)S(1)}, u32[]{:S(2)}, u32[]{:S(2)}) collective-permute-start(bf16[16,1024]{1,0:T(8,128)(2,1)S(1)} %get-tuple-element.14), channel_id=1, source_target_pairs={{0,2},{2,0},{4,6},{6,4},{8,10},{10,8},{12,14},{14,12},{1,3},{3,1},... | collective-permute-start | bytes 98312 | tf_op jit(solution)/shard_map/ppermute | solution.py:195
  44.3 2.6 %collective-permute-start.13 = (bf16[16,1024]{1,0:T(8,128)(2,1)}, bf16[16,1024]{1,0:T(8,128)(2,1)}, u32[]{:S(2)}, u32[]{:S(2)}) collective-permute-start(bf16[16,1024]{1,0:T(8,128)(2,1)} %get-tuple-element.16), channel_id=1, source_target_pairs={{0,10},{2,8},{4,14},{6,12},{8,2},{10,0},{12,6},{14,4},{1,11},{3,9}... | collective-permute-start | bytes 98312 | tf_op jit(solution)/shard_map/ppermute | solution.py:195
  46.9 2.7 %collective-permute-start.14 = (bf16[16,1024]{1,0:T(8,128)(2,1)}, bf16[16,1024]{1,0:T(8,128)(2,1)}, u32[]{:S(2)}, u32[]{:S(2)}) collective-permute-start(bf16[16,1024]{1,0:T(8,128)(2,1)} %get-tuple-element.17), channel_id=1, source_target_pairs={{0,14},{2,12},{4,10},{6,8},{8,6},{10,4},{12,2},{14,0},{1,15},{3,13... | collective-permute-start | bytes 98312 | tf_op jit(solution)/shard_map/ppermute | solution.py:195
  49.6 1.9 %collective-permute-start.9 = (bf16[16,1024]{1,0:T(8,128)(2,1)}, bf16[16,1024]{1,0:T(8,128)(2,1)}, u32[]{:S(2)}, u32[]{:S(2)}) collective-permute-start(bf16[16,1024]{1,0:T(8,128)(2,1)} %get-tuple-element.12), channel_id=1, source_target_pairs={{0,8},{2,10},{4,12},{6,14},{8,0},{10,2},{12,4},{14,6},{1,9},{3,11}... | collective-permute-start | bytes 98312 | tf_op jit(solution)/shard_map/ppermute | solution.py:195
  51.5 1.2 %reshape.7.qr_ref = bf16[16,64,64]{2,1,0:T(8,128)(2,1)S(1)} reshape(bf16[16,4096]{1,0:T(8,128)(2,1)} %param.14) | data formatting | bytes 262144 | tf_op jit(solution)/shard_map/reshape | solution.py:62
  52.7 0.9 %copy-done.3 = bf16[16,64,128]{2,1,0:T(8,128)(2,1)S(1)} copy-done((bf16[16,64,128]{2,1,0:T(8,128)(2,1)S(1)}, bf16[16,64,128]{2,1,0:T(8,128)(2,1)}, u32[]{:S(2)}) %copy-start.3) | copy-done | bytes 262168
  53.7 7.3 %shard_map.106 = bf16[16,64,512]{2,1,0:T(8,128)(2,1)} custom-call(s32[16]{0:T(128)S(1)} %copy-done.17, bf16[16,64,512]{2,1,0:T(8,128)(2,1)S(1)} %copy-done.2, bf16[16,64,64]{2,1,0:T(8,128)(2,1)S(1)} %reshape.7.qr_ref, bf16[16,128,512]{2,1,0:T(8,128)(2,1)S(1)} %copy-done.1, bf16[16,64,128]{2,1,0:T(8,128)(2,1)S(1)} %copy-done.3), custom_call_target="tpu_custom_call" | custom-call | flops 285212672 | bytes 4587520 | tf_op jit(solution)/shard_map/pallas_call | solution.py:69
  61.0 1.5 %add_convert_fusion = bf16[16,1024]{1,0:T(8,128)(2,1)} fusion(bf16[16,1024]{1,0:T(8,128)(2,1)} %collective-permute-done.14, bf16[16,1024]{1,0:T(8,128)(2,1)} %collective-permute-done.13, bf16[16,1024]{1,0:T(8,128)(2,1)} %collective-permute-done.12, bf16[16,1024]{1,0:T(8,128)(2,1)S(1)} %collective-permute-done.11, ...), kind=kLoop, calls=%fused_computation | loop fusion | flops 262144 | bytes 294912 | tf_op jit(solution)/shard_map/convert_element_type | solution.py:218
  (40 shorter events, 2.0 us)
Async XLA Ops:
  0.6 24.7 %collective-permute-start.7 = (bf16[3584,1024]{1,0:T(8,128)(2,1)}, bf16[3584,1024]{1,0:T(8,128)(2,1)}, u32[]{:S(2)}, u32[]{:S(2)}) collective-permute-start(bf16[3584,1024]{1,0:T(8,128)(2,1)} %bitcast.5), channel_id=1, source_target_pairs={{0,1},{1,0},{2,3},{3,2},{4,5},{5,4},{6,7},{7,6},{8,9},{9,8},{10,11... | collective-permute-start | bytes 22020104 | tf_op jit(solution)/shard_map/ppermute | solution.py:195
  1.1 0.9 %copy-start.14 = (bf16[16,3584]{1,0:T(8,128)(2,1)S(1)}, bf16[16,3584]{1,0:T(8,128)(2,1)}, u32[]{:S(2)}) copy-start(bf16[16,3584]{1,0:T(8,128)(2,1)} %tokens_ref.1) | copy-start | bytes 344068
  2.0 0.7 %copy-start.15 = (s32[16,8]{0,1:T(8,128)S(1)}, s32[16,8]{0,1:T(8,128)}, u32[]{:S(2)}) copy-start(s32[16,8]{0,1:T(8,128)} %param.10) | copy-start | bytes 1540
  2.7 0.7 %copy-start.16 = (bf16[16,8]{0,1:T(8,128)(2,1)S(1)}, bf16[16,8]{0,1:T(8,128)(2,1)}, u32[]{:S(2)}) copy-start(bf16[16,8]{0,1:T(8,128)(2,1)} %param.11) | copy-start | bytes 772
  3.6 8.4 %collective-permute-start = (bf16[16,3712]{1,0:T(8,128)(2,1)S(1)}, bf16[16,3712]{1,0:T(8,128)(2,1)S(1)}, u32[]{:S(2)}, u32[]{:S(2)}) collective-permute-start(bf16[16,3712]{1,0:T(8,128)(2,1)S(1)} %shard_map.104.refs_0_), channel_id=1, source_target_pairs={{0,4},{4,0},{8,12},{12,8},{1,5},{5,1},{9,13},{13,9},{2,6},{6,2},{1... | collective-permute-start | bytes 356360 | tf_op jit(solution)/shard_map/ppermute | solution.py:195
  6.2 12.1 %collective-permute-start.1 = (bf16[16,3712]{1,0:T(8,128)(2,1)S(1)}, bf16[16,3712]{1,0:T(8,128)(2,1)S(1)}, u32[]{:S(2)}, u32[]{:S(2)}) collective-permute-start(bf16[16,3712]{1,0:T(8,128)(2,1)S(1)} %shard_map.104.refs_0_), channel_id=1, source_target_pairs={{0,8},{4,12},{8,0},{12,4},{1,9},{5,13},{9,1},{13,5},{2,10},{6,14},... | collective-permute-start | bytes 356360 | tf_op jit(solution)/shard_map/ppermute | solution.py:195
  8.8 11.0 %collective-permute-start.2 = (bf16[16,3712]{1,0:T(8,128)(2,1)S(1)}, bf16[16,3712]{1,0:T(8,128)(2,1)S(1)}, u32[]{:S(2)}, u32[]{:S(2)}) collective-permute-start(bf16[16,3712]{1,0:T(8,128)(2,1)S(1)} %shard_map.104.refs_0_), channel_id=1, source_target_pairs={{0,12},{4,8},{8,4},{12,0},{1,13},{5,9},{9,5},{13,1},{2,14},{6,10},... | collective-permute-start | bytes 356360 | tf_op jit(solution)/shard_map/ppermute | solution.py:195
  8.8 12.3 %collective-permute-start.3 = (bf16[16,3712]{1,0:T(8,128)(2,1)S(1)}, bf16[16,3712]{1,0:T(8,128)(2,1)S(1)}, u32[]{:S(2)}, u32[]{:S(2)}) collective-permute-start(bf16[16,3712]{1,0:T(8,128)(2,1)S(1)} %shard_map.104.refs_0_), channel_id=1, source_target_pairs={{0,2},{2,0},{1,3},{3,1},{4,6},{6,4},{5,7},{7,5},{8,10},{10,8},{9,1... | collective-permute-start | bytes 356360 | tf_op jit(solution)/shard_map/ppermute | solution.py:195
  12.0 9.7 %collective-permute-start.4 = (bf16[16,3712]{1,0:T(8,128)(2,1)S(1)}, bf16[16,3712]{1,0:T(8,128)(2,1)S(1)}, u32[]{:S(2)}, u32[]{:S(2)}) collective-permute-start(bf16[16,3712]{1,0:T(8,128)(2,1)S(1)} %collective-permute-done.refs_1_), channel_id=1, source_target_pairs={{0,2},{2,0},{1,3},{3,1},{4,6},{6,4},{5,7},{7,5},{8,10},{10,8},{9,1... | collective-permute-start | bytes 356360 | tf_op jit(solution)/shard_map/ppermute | solution.py:195
  18.3 4.8 %collective-permute-start.5 = (bf16[16,3712]{1,0:T(8,128)(2,1)S(1)}, bf16[16,3712]{1,0:T(8,128)(2,1)S(1)}, u32[]{:S(2)}, u32[]{:S(2)}) collective-permute-start(bf16[16,3712]{1,0:T(8,128)(2,1)S(1)} %collective-permute-done.1.refs_2_), channel_id=1, source_target_pairs={{0,2},{2,0},{1,3},{3,1},{4,6},{6,4},{5,7},{7,5},{8,10},{10,8},{9,1... | collective-permute-start | bytes 356360 | tf_op jit(solution)/shard_map/ppermute | solution.py:195
  19.8 4.8 %collective-permute-start.6 = (bf16[16,3712]{1,0:T(8,128)(2,1)S(1)}, bf16[16,3712]{1,0:T(8,128)(2,1)S(1)}, u32[]{:S(2)}, u32[]{:S(2)}) collective-permute-start(bf16[16,3712]{1,0:T(8,128)(2,1)S(1)} %collective-permute-done.2.refs_3_), channel_id=1, source_target_pairs={{0,2},{2,0},{1,3},{3,1},{4,6},{6,4},{5,7},{7,5},{8,10},{10,8},{9,1... | collective-permute-start | bytes 356360 | tf_op jit(solution)/shard_map/ppermute | solution.py:195
  20.3 0.6 %copy-start.4 = (bf16[16,3712]{1,0:T(8,128)(2,1)}, bf16[16,3712]{1,0:T(8,128)(2,1)S(1)}, u32[]{:S(2)}) copy-start(bf16[16,3712]{1,0:T(8,128)(2,1)S(1)} %collective-permute-done.2.refs_3_) | copy-start | bytes 356356
  21.0 31.7 %copy-start.17 = (s32[16]{0:T(128)S(1)}, s32[16]{0:T(128)}, u32[]{:S(2)}) copy-start(s32[16]{0:T(128)} %lengths_ref.1) | copy-start | bytes 196
  21.7 0.7 %copy-start.8 = (bf16[16,3712]{1,0:T(8,128)(2,1)}, bf16[16,3712]{1,0:T(8,128)(2,1)S(1)}, u32[]{:S(2)}) copy-start(bf16[16,3712]{1,0:T(8,128)(2,1)S(1)} %collective-permute-done.4.refs_5_) | copy-start | bytes 356356
  23.1 0.6 %copy-start.10 = (bf16[16,3712]{1,0:T(8,128)(2,1)}, bf16[16,3712]{1,0:T(8,128)(2,1)S(1)}, u32[]{:S(2)}) copy-start(bf16[16,3712]{1,0:T(8,128)(2,1)S(1)} %collective-permute-done.5.refs_6_) | copy-start | bytes 356356
  24.6 0.7 %copy-start.12 = (bf16[16,3712]{1,0:T(8,128)(2,1)}, bf16[16,3712]{1,0:T(8,128)(2,1)S(1)}, u32[]{:S(2)}) copy-start(bf16[16,3712]{1,0:T(8,128)(2,1)S(1)} %collective-permute-done.6.refs_7_) | copy-start | bytes 356356
  25.3 3.1 %copy-start = (bf16[1,3584,1024]{2,1,0:T(8,128)(2,1)S(1)}, bf16[1,3584,1024]{2,1,0:T(8,128)(2,1)}, u32[]{:S(2)}) copy-start(bf16[1,3584,1024]{2,1,0:T(8,128)(2,1)} %param.12) | copy-start | bytes 22020100
  28.4 0.9 %copy-start.5 = (bf16[16,3712]{1,0:T(8,128)(2,1)S(1)}, bf16[16,3712]{1,0:T(8,128)(2,1)}, u32[]{:S(2)}) copy-start(bf16[16,3712]{1,0:T(8,128)(2,1)} %copy-done.4) | copy-start | bytes 356356
  29.3 0.9 %copy-start.7 = (bf16[16,3712]{1,0:T(8,128)(2,1)S(1)}, bf16[16,3712]{1,0:T(8,128)(2,1)}, u32[]{:S(2)}) copy-start(bf16[16,3712]{1,0:T(8,128)(2,1)} %copy-done.6) | copy-start | bytes 356356
  30.2 0.9 %copy-start.9 = (bf16[16,3712]{1,0:T(8,128)(2,1)S(1)}, bf16[16,3712]{1,0:T(8,128)(2,1)}, u32[]{:S(2)}) copy-start(bf16[16,3712]{1,0:T(8,128)(2,1)} %copy-done.8) | copy-start | bytes 356356
  31.1 0.9 %copy-start.11 = (bf16[16,3712]{1,0:T(8,128)(2,1)S(1)}, bf16[16,3712]{1,0:T(8,128)(2,1)}, u32[]{:S(2)}) copy-start(bf16[16,3712]{1,0:T(8,128)(2,1)} %copy-done.10) | copy-start | bytes 356356
  32.0 0.9 %copy-start.13 = (bf16[16,3712]{1,0:T(8,128)(2,1)S(1)}, bf16[16,3712]{1,0:T(8,128)(2,1)}, u32[]{:S(2)}) copy-start(bf16[16,3712]{1,0:T(8,128)(2,1)} %copy-done.12) | copy-start | bytes 356356
  32.9 19.8 %copy-start.1 = (bf16[16,128,512]{2,1,0:T(8,128)(2,1)S(1)}, bf16[16,128,512]{2,1,0:T(8,128)(2,1)}, u32[]{:S(2)}) copy-start(bf16[16,128,512]{2,1,0:T(8,128)(2,1)} %cl_ref.1) | copy-start | bytes 6291460
  32.9 19.8 %copy-start.2 = (bf16[16,64,512]{2,1,0:T(8,128)(2,1)S(1)}, bf16[16,64,512]{2,1,0:T(8,128)(2,1)}, u32[]{:S(2)}) copy-start(bf16[16,64,512]{2,1,0:T(8,128)(2,1)} %ql_ref.1) | copy-start | bytes 3145732
  40.3 9.3 %collective-permute-start.10 = (bf16[16,1024]{1,0:T(8,128)(2,1)S(1)}, bf16[16,1024]{1,0:T(8,128)(2,1)S(1)}, u32[]{:S(2)}, u32[]{:S(2)}) collective-permute-start(bf16[16,1024]{1,0:T(8,128)(2,1)S(1)} %get-tuple-element.13), channel_id=1, source_target_pairs={{0,12},{2,14},{4,8},{6,10},{8,4},{10,6},{12,0},{14,2},{1,13},{3,15... | collective-permute-start | bytes 98312 | tf_op jit(solution)/shard_map/ppermute | solution.py:195
  42.9 6.8 %collective-permute-start.11 = (bf16[16,1024]{1,0:T(8,128)(2,1)S(1)}, bf16[16,1024]{1,0:T(8,128)(2,1)S(1)}, u32[]{:S(2)}, u32[]{:S(2)}) collective-permute-start(bf16[16,1024]{1,0:T(8,128)(2,1)S(1)} %get-tuple-element.14), channel_id=1, source_target_pairs={{0,2},{2,0},{4,6},{6,4},{8,10},{10,8},{12,14},{14,12},{1,3},{3,1},... | collective-permute-start | bytes 98312 | tf_op jit(solution)/shard_map/ppermute | solution.py:195
  44.3 16.7 %collective-permute-start.12 = (bf16[16,1024]{1,0:T(8,128)(2,1)}, bf16[16,1024]{1,0:T(8,128)(2,1)}, u32[]{:S(2)}, u32[]{:S(2)}) collective-permute-start(bf16[16,1024]{1,0:T(8,128)(2,1)} %get-tuple-element.15), channel_id=1, source_target_pairs={{0,6},{2,4},{4,2},{6,0},{8,14},{10,12},{12,10},{14,8},{1,7},{3,5},... | collective-permute-start | bytes 98312 | tf_op jit(solution)/shard_map/ppermute | solution.py:195
  44.3 16.7 %collective-permute-start.13 = (bf16[16,1024]{1,0:T(8,128)(2,1)}, bf16[16,1024]{1,0:T(8,128)(2,1)}, u32[]{:S(2)}, u32[]{:S(2)}) collective-permute-start(bf16[16,1024]{1,0:T(8,128)(2,1)} %get-tuple-element.16), channel_id=1, source_target_pairs={{0,10},{2,8},{4,14},{6,12},{8,2},{10,0},{12,6},{14,4},{1,11},{3,9}... | collective-permute-start | bytes 98312 | tf_op jit(solution)/shard_map/ppermute | solution.py:195
  46.9 14.1 %collective-permute-start.14 = (bf16[16,1024]{1,0:T(8,128)(2,1)}, bf16[16,1024]{1,0:T(8,128)(2,1)}, u32[]{:S(2)}, u32[]{:S(2)}) collective-permute-start(bf16[16,1024]{1,0:T(8,128)(2,1)} %get-tuple-element.17), channel_id=1, source_target_pairs={{0,14},{2,12},{4,10},{6,8},{8,6},{10,4},{12,2},{14,0},{1,15},{3,13... | collective-permute-start | bytes 98312 | tf_op jit(solution)/shard_map/ppermute | solution.py:195
  49.6 11.4 %collective-permute-start.8 = (bf16[16,1024]{1,0:T(8,128)(2,1)}, bf16[16,1024]{1,0:T(8,128)(2,1)}, u32[]{:S(2)}, u32[]{:S(2)}) collective-permute-start(bf16[16,1024]{1,0:T(8,128)(2,1)} %get-tuple-element.11), channel_id=1, source_target_pairs={{0,4},{2,6},{4,0},{6,2},{8,12},{10,14},{12,8},{14,10},{1,5},{3,7},... | collective-permute-start | bytes 98312 | tf_op jit(solution)/shard_map/ppermute | solution.py:195
  49.6 11.4 %collective-permute-start.9 = (bf16[16,1024]{1,0:T(8,128)(2,1)}, bf16[16,1024]{1,0:T(8,128)(2,1)}, u32[]{:S(2)}, u32[]{:S(2)}) collective-permute-start(bf16[16,1024]{1,0:T(8,128)(2,1)} %get-tuple-element.12), channel_id=1, source_target_pairs={{0,8},{2,10},{4,12},{6,14},{8,0},{10,2},{12,4},{14,6},{1,9},{3,11}... | collective-permute-start | bytes 98312 | tf_op jit(solution)/shard_map/ppermute | solution.py:195
  52.7 1.0 %copy-start.3 = (bf16[16,64,128]{2,1,0:T(8,128)(2,1)S(1)}, bf16[16,64,128]{2,1,0:T(8,128)(2,1)}, u32[]{:S(2)}) copy-start(bf16[16,64,128]{2,1,0:T(8,128)(2,1)} %cr_ref.1) | copy-start | bytes 786436
  (1 other events, 0.6 us)

commit v2 on v1

v2 whole, which is shorter than its diff:
```python
import functools

import jax
import jax.numpy as jnp
from jax import lax
from jax.experimental import pallas as pl
from jax.experimental.pallas import tpu as pltpu
from jax.sharding import PartitionSpec as P

score_scale = 192.0 ** (-0.5)
EXPERT_AXES = ("node", "local", "pair")
LANES = 128
VMEM_LIMIT = 16 * 2**20


def slot_tables(picked, weights, experts, capacity):
    row_count, choose = picked.shape
    flat_picks = picked.reshape(-1)
    matches = (flat_picks[:, None] == jnp.arange(experts, dtype=jnp.int32)[None, :]).astype(
        jnp.int32
    )
    earlier = jnp.cumsum(matches, axis=0) - matches
    position = jnp.sum(earlier * matches, axis=1)
    slot_index = flat_picks * capacity + position
    slot_hits = (
        slot_index[:, None] == jnp.arange(experts * capacity, dtype=jnp.int32)[None, :]
    ).astype(jnp.float32)
    owner = (
        jnp.arange(row_count * choose, dtype=jnp.int32)[:, None] // choose
        == jnp.arange(row_count, dtype=jnp.int32)[None, :]
    ).astype(jnp.float32)
    dispatch = jnp.dot(slot_hits.T, owner, precision=lax.Precision.HIGHEST)
    combine = jnp.dot(
        owner.T,
        slot_hits * weights.astype(jnp.float32).reshape(-1)[:, None],
        precision=lax.Precision.HIGHEST,
    )
    return (dispatch, combine)


def attend_kernel(first, loads, lengths_ref, ql_ref, qr_ref, cl_ref, cr_ref, *refs):
    if loads:
        matrix_hbm, out_ref, matrix_ref, sem = refs
        copy = pltpu.make_async_copy(matrix_hbm, matrix_ref, sem)

        @pl.when(pl.program_id(0) == 0)
        def _():
            copy.start()

    else:
        out_ref = refs[-1]
    rows, heads, _ = ql_ref.shape
    context = cr_ref.shape[2]
    start = first + pl.program_id(0) * rows
    place = lax.broadcasted_iota(jnp.int32, (heads, context), 1)
    scores = []
    for r in range(rows):
        s = lax.dot_general(
            ql_ref[r], cl_ref[r], (((1,), (1,)), ((), ())), preferred_element_type=jnp.float32
        )
        s = s + jnp.dot(qr_ref[r], cr_ref[r], preferred_element_type=jnp.float32)
        scores.append(jnp.where(place < lengths_ref[start + r], s * score_scale, -1e30))
    probs = []
    for s in scores:
        exponent = jnp.exp(s - jnp.max(s, axis=1, keepdims=True))
        probs.append((exponent / jnp.sum(exponent, axis=1, keepdims=True)).astype(jnp.bfloat16))
    for r in range(rows):
        out_ref[r] = jnp.dot(probs[r], cl_ref[r], preferred_element_type=jnp.float32).astype(
            out_ref.dtype
        )
    if loads:

        @pl.when(pl.program_id(0) == pl.num_programs(0) - 1)
        def _():
            copy.wait()


def attend_rows(
    first, count, query_latent, rotary, cache_latent, cache_rope, lengths, so_far=None, matrix=None
):
    row_count, heads, latent = query_latent.shape
    rope, context = cache_rope.shape[1:]
    step = 8 if count % 8 == 0 and first % 8 == 0 else 1

    def block(*tail):
        return pl.BlockSpec((step,) + tail, lambda i, lengths_ref: (first // step + i, 0, 0))

    loads = matrix is not None
    extra = [so_far] if so_far is not None else [in_hbm(matrix)] if loads else []
    out_shape = jax.ShapeDtypeStruct((row_count, heads, latent), jnp.bfloat16)
    out_spec = block(heads, latent)
    if loads:
        out_shape = [out_shape, pltpu.VMEM(matrix.shape, matrix.dtype)]
        out_spec = [out_spec, pl.BlockSpec(memory_space=pltpu.VMEM)]
    return pl.pallas_call(
        functools.partial(attend_kernel, first, loads),
        out_shape=out_shape,
        grid_spec=pltpu.PrefetchScalarGridSpec(
            num_scalar_prefetch=1,
            grid=(count // step,),
            in_specs=[
                block(heads, latent),
                block(heads, rope),
                block(context, latent),
                block(rope, context),
            ]
            + [pl.BlockSpec(memory_space=pl.ANY)] * len(extra),
            out_specs=out_spec,
            scratch_shapes=[pltpu.SemaphoreType.DMA] if loads else [],
        ),
        input_output_aliases={5: 0} if so_far is not None else {},
        compiler_params=pltpu.CompilerParams(vmem_limit_bytes=12 * 2**20),
    )(lengths, in_hbm(query_latent), rotary, in_hbm(cache_latent), in_hbm(cache_rope), *extra)


def in_hbm(value):
    return pltpu.with_memory_space_constraint(value, pltpu.HBM)


def in_vmem(value):
    return pltpu.with_memory_space_constraint(value, pltpu.VMEM)


def expert_by_slots(tokens, expert_ids, combine_weights, expert_weight):
    row_count, model_width = tokens.shape
    choose = expert_ids.shape[1]
    experts = lax.axis_size(EXPERT_AXES)
    capacity = min(row_count, 3 * max(1, (row_count * choose + experts - 1) // experts))
    matrix = expert_weight[0]
    dispatch, combine = slot_tables(expert_ids, combine_weights, experts, capacity)
    outgoing = jnp.dot(
        dispatch.astype(jnp.bfloat16), tokens, preferred_element_type=jnp.float32
    ).astype(jnp.bfloat16)
    outgoing = outgoing.reshape(experts, capacity, model_width)
    received = lax.all_to_all(outgoing, EXPERT_AXES, split_axis=0, concat_axis=0, tiled=True)
    hidden = jnp.dot(received.reshape(-1, model_width), matrix, preferred_element_type=jnp.float32)
    returned = lax.all_to_all(
        jax.nn.silu(hidden).astype(jnp.bfloat16).reshape(received.shape[:-1] + (matrix.shape[1],)),
        EXPERT_AXES,
        split_axis=0,
        concat_axis=0,
        tiled=True,
    )
    returned = returned.reshape(experts * capacity, -1).astype(jnp.float32)
    mixture = jnp.dot(combine, returned, precision=lax.Precision.HIGHEST)
    return mixture.astype(jnp.bfloat16)


def payload_kernel(
    ids_hbm, weights_hbm, tokens_hbm, rope_hbm, out_ref, rope_ref, ids_ref, weights_ref, sems
):
    choose, rows = ids_ref.shape
    width = tokens_hbm.shape[1]
    copies = [
        pltpu.make_async_copy(ids_hbm, ids_ref, sems.at[0]),
        pltpu.make_async_copy(weights_hbm, weights_ref, sems.at[1]),
        pltpu.make_async_copy(tokens_hbm, out_ref.at[:, pl.ds(0, width)], sems.at[2]),
        pltpu.make_async_copy(rope_hbm, rope_ref, sems.at[3]),
    ]
    for copy in copies:
        copy.start()
    copies[0].wait()
    copies[1].wait()
    expert = lax.broadcasted_iota(jnp.int32, (LANES, rows), 0)
    table = jnp.zeros((LANES, rows), jnp.float32)
    ids, weights = ids_ref[...], weights_ref[...].astype(jnp.float32)
    for k in range(choose):
        table = table + jnp.where(expert == ids[k : k + 1], weights[k : k + 1], 0.0)
    eye = (
        lax.broadcasted_iota(jnp.int32, (rows, rows), 0)
        == lax.broadcasted_iota(jnp.int32, (rows, rows), 1)
    ).astype(jnp.bfloat16)
    out_ref[:, width:] = lax.dot_general(
        eye,
        table.astype(jnp.bfloat16),
        (((1,), (1,)), ((), ())),
        preferred_element_type=jnp.float32,
    ).astype(jnp.bfloat16)
    copies[2].wait()
    copies[3].wait()


def make_payload(tokens, expert_ids, combine_weights, query_rope):
    rows, width = tokens.shape
    choose = expert_ids.shape[1]
    return pl.pallas_call(
        payload_kernel,
        out_shape=[
            pltpu.VMEM((rows, width + LANES), jnp.bfloat16),
            pltpu.VMEM(query_rope.shape, query_rope.dtype),
        ],
        in_specs=[pl.BlockSpec(memory_space=pl.ANY)] * 4,
        out_specs=[pl.BlockSpec(memory_space=pltpu.VMEM)] * 2,
        scratch_shapes=[
            pltpu.VMEM((choose, rows), jnp.int32),
            pltpu.VMEM((choose, rows), jnp.bfloat16),
            pltpu.SemaphoreType.DMA((4,)),
        ],
        compiler_params=pltpu.CompilerParams(vmem_limit_bytes=4 * 2**20),
        cost_estimate=pl.CostEstimate(
            flops=0, bytes_accessed=4 * rows * width, transcendentals=0
        ),
    )(in_hbm(expert_ids.T), in_hbm(combine_weights.T), in_hbm(tokens), in_hbm(query_rope))


def expert_kernel(count, *refs):
    here = lax.axis_index(EXPERT_AXES).astype(jnp.int32)
    blocks, (own_ref, other_hbm) = refs[:count], refs[count : count + 2]
    near_ref, far_ref, other_ref, sems = refs[count + 2 :]
    width, hidden = own_ref.shape
    tile = 256
    copies = [
        pltpu.make_async_copy(
            other_hbm.at[:, pl.ds(n, tile)], other_ref.at[:, pl.ds(n, tile)], sems.at[n // tile]
        )
        for n in range(0, hidden, tile)
    ]
    for copy in copies:
        copy.start()
    rows = jnp.concatenate([block[...] for block in blocks], axis=0)
    features, shares = rows[:, :width], rows[:, width:].astype(jnp.float32)
    lane = lax.broadcasted_iota(jnp.int32, shares.shape, 1)
    share = [
        jnp.sum(jnp.where(lane == (here ^ which), shares, 0.0), axis=1, keepdims=True)
        for which in range(2)
    ]

    def term(which, matrix_ref, n):
        value = jnp.dot(features, matrix_ref[:, n : n + tile], preferred_element_type=jnp.float32)
        return share[which] * (value / (1.0 + jnp.exp(-value)))

    half = near_ref.shape[0]
    firsts = [term(0, own_ref, n) for n in range(0, hidden, tile)]
    for n, copy, first in zip(range(0, hidden, tile), copies, firsts):
        copy.wait()
        total = first + term(1, other_ref, n)
        near_ref[:, n : n + tile] = total[:half]
        far_ref[:, n : n + tile] = total[half:].astype(jnp.bfloat16)


def serve(blocks, own, other):
    count = len(blocks)
    rows = blocks[0].shape[0]
    width, hidden = own.shape
    whole = pl.BlockSpec(memory_space=pltpu.VMEM)
    half = count // 2 * rows
    return pl.pallas_call(
        functools.partial(expert_kernel, count),
        out_shape=[
            pltpu.VMEM((half, hidden), jnp.float32),
            pltpu.VMEM((half, hidden), jnp.bfloat16),
        ],
        in_specs=[whole] * (count + 1) + [pl.BlockSpec(memory_space=pl.ANY)],
        out_specs=[whole] * 2,
        scratch_shapes=[
            pltpu.VMEM((width, hidden), jnp.bfloat16),
            pltpu.SemaphoreType.DMA((hidden // 256,)),
        ],
        compiler_params=pltpu.CompilerParams(vmem_limit_bytes=VMEM_LIMIT),
        cost_estimate=pl.CostEstimate(
            flops=4 * count * rows * width * hidden,
            bytes_accessed=4 * width * hidden,
            transcendentals=2 * count * rows * hidden,
        ),
    )(*map(in_vmem, blocks), in_vmem(own), in_hbm(other))


def swap(value, axis, size, mask):
    return lax.ppermute(value, axis, [(i, i ^ mask) for i in range(size)])


def tie(value, *others):
    return lax.optimization_barrier((value,) + others)[0]


def gathered(attention, tokens, expert_ids, combine_weights, expert_weight):
    nodes, locals_, pairs = (lax.axis_size(axis) for axis in EXPERT_AXES)
    rows = tokens.shape[0]
    own = expert_weight[0]
    other = swap(own, "pair", pairs, 1)

    query_latent, query_rope, cache_latent, cache_rope, lengths = attention
    mine, query_rope = make_payload(tokens, expert_ids, combine_weights, query_rope)
    near = {0: mine}
    for n in range(nodes - 1, 0, -1):
        near[n] = swap(mine, "node", nodes, n)
    far = {}
    far[0] = swap(mine, "local", locals_, 1)
    far[1] = swap(mine, ("node", "local"), nodes * locals_, locals_ + 1)
    count, heads, _ = query_latent.shape
    half = count // 2
    rotary = query_rope.reshape(count, heads, cache_rope.shape[1])
    rest = (rotary, cache_latent, cache_rope, lengths)
    attended, own = attend_rows(0, half, tie(query_latent, mine), *rest, matrix=own)
    far[3] = swap(tie(near[3], attended), "local", locals_, 1)
    far[2] = swap(tie(near[2], attended), "local", locals_, 1)

    blocks = [near[n] for n in range(nodes)] + [far[n] for n in range(nodes)]
    kept, sent = serve(blocks, own, other)
    came = swap(sent, "local", locals_, 1)
    attended = attend_rows(half, count - half, tie(query_latent, sent), *rest, attended)
    came = tie(came, attended)
    kept = kept.reshape(nodes, rows, -1)
    came = came.reshape(nodes, rows, -1)
    total = kept[0] + came[0].astype(jnp.float32)
    for n in range(nodes - 1, 0, -1):
        part = (kept[n] + came[n].astype(jnp.float32)).astype(jnp.bfloat16)
        total = total + swap(part, "node", nodes, n).astype(jnp.float32)
    return total.astype(jnp.bfloat16), attended


def body(
    tokens,
    expert_ids,
    combine_weights,
    expert_weight,
    query_latent,
    query_rope,
    cache_latent,
    cache_rope,
    lengths,
):
    sizes = tuple(lax.axis_size(axis) for axis in EXPERT_AXES)
    attention = (query_latent, query_rope, cache_latent, cache_rope, lengths)
    if sizes == (4, 2, 2):
        return gathered(attention, tokens, expert_ids, combine_weights, expert_weight)
    count, heads, _ = query_latent.shape
    rotary = query_rope.reshape(count, heads, cache_rope.shape[1])
    attended = attend_rows(0, count, query_latent, rotary, cache_latent, cache_rope, lengths)
    expert_mix = expert_by_slots(tokens, expert_ids, combine_weights, expert_weight)
    return (expert_mix, attended)


def solution(mesh):
    rows = ("group",) + EXPERT_AXES
    return jax.shard_map(
        body,
        mesh=mesh,
        in_specs=(
            P(rows, None),
            P(rows, None),
            P(rows, None),
            P(EXPERT_AXES, None, None),
            P(rows, None, None),
            P(rows, None),
            P(rows, None, None),
            P(rows, None, None),
            P(rows),
        ),
        out_specs=(P(rows, None), P(rows, None, None)),
        check_vma=False,
    )
```

time: 63 us -> 43.6 us (0.69)
  local copies, waits for them, and re-layouts: 15.2 us -> 0.9 us
  starting transfers between devices: 22.3 us -> 16.8 us
  waiting for transfers between devices: 7.75 us -> 8.66 us
  other arithmetic: 1.56 us -> 0.67 us
  Pallas kernels: 14.9 us -> 15.6 us
    unnamed x36 -> x4, local copies, waits for them, and re-layouts: 14.1 us -> 0.66 us
    ppermute x15 -> x12, starting transfers between devices: 22.3 us -> 16.8 us  [swap(): return lax.ppermute(value, axis, [(i, i ^ mask) for i in range(size)])]
    reshape x1, local copies, waits for them, and re-layouts: 1.18 us -> 0.24 us  [gathered(): rotary = query_rope.reshape(count, heads, cache_rope.shape[1])]
    ppermute x15 -> x12, waiting for transfers between devices: 7.75 us -> 8.66 us  [swap(): return lax.ppermute(value, axis, [(i, i ^ mask) for i in range(size)])]
    convert_element_type x1 -> x2, other arithmetic: 1.48 us -> 0.67 us  [the longest x1 0.64 us: gathered(): return (total.astype(jnp.bfloat16), attended)]
    pallas_call x3 -> x4, Pallas kernels: 14.9 us -> 15.6 us  [the longest x2 9.41 us: attend_rows(): pl.pallas_call(functools.partial(attend_kernel, first, loads), out_shape=...]
  transfers between devices with their start and end apart: 15 -> 12, of which waited for: 4 -> 7; matrix products, arithmetic and copies ran while one was open for 2% -> 1% of each run, Pallas kernels for 12% -> 24%
where the time goes in v2:
time: 43.6 us; the launch traced here: 43.3 us
  starting transfers between devices  16.8 us (39%)
  Pallas kernels  15.6 us (36%)
  waiting for transfers between devices  8.66 us (20%)
  local copies, waits for them, and re-layouts  0.9 us (2%)
  between operations  0.7 us (2%)
  other arithmetic  0.67 us (2%)
    ppermute x12, starting transfers between devices, swap(): return lax.ppermute(value, axis, [(i, i ^ mask) for i in range(size)])  16.8 us
    pallas_call x2, Pallas kernels, attend_rows(): pl.pallas_call(functools.partial(attend_kernel, first, loads), out_shape=...  9.41 us
    ppermute x12, waiting for transfers between devices, swap(): return lax.ppermute(value, axis, [(i, i ^ mask) for i in range(size)])  8.66 us
    pallas_call x1, Pallas kernels, serve(): pl.pallas_call(functools.partial(expert_kernel, count), out_shape=[pltpu....  5.18 us
    pallas_call x1, Pallas kernels, make_payload(): pl.pallas_call(payload_kernel, out_shape=[pltpu.VMEM((rows, width + LANES...  1.02 us
  transfers between devices with their start and end apart: 12, of which 7 were waited for; matrix products, arithmetic and copies ran while one was open for 1% of the time, Pallas kernels for 24%

profile of v2, /device:TPU:0, one launch (start us, length us, event | category | flops | bytes accessed | tf_op | source)
XLA Modules:
  0.0 43.3 jit_solution(7795976488478399321)
XLA Ops:
  0.6 0.5 %collective-permute-start.7 = (bf16[3584,1024]{1,0:T(8,128)(2,1)}, bf16[3584,1024]{1,0:T(8,128)(2,1)}, u32[]{:S(2)}, u32[]{:S(2)}) collective-permute-start(bf16[3584,1024]{1,0:T(8,128)(2,1)} %bitcast.3), channel_id=1, source_target_pairs={{0,1},{1,0},{2,3},{3,2},{4,5},{5,4},{6,7},{7,6},{8,9},{9,8},{10,11... | collective-permute-start | bytes 22020104 | tf_op jit(solution)/shard_map/ppermute | solution.py:269
  1.1 1.0 %shard_map.104 = (bf16[16,3712]{1,0:T(8,128)(2,1)S(1)}, bf16[16,4096]{1,0:T(8,128)(2,1)S(1)}) custom-call(s32[8,16]{1,0:T(8,128)} %bitcast.5, bf16[8,16]{1,0:T(8,128)(2,1)} %bitcast.6, bf16[16,3584]{1,0:T(8,128)(2,1)} %tokens_hbm.1, bf16[16,4096]{1,0:T(8,128)(2,1)} %rope_hbm.1), custom_call_target="tpu_custom_call" | custom-call | bytes 229376 | tf_op jit(solution)/shard_map/pallas_call | solution.py:186
  2.2 4.7 %collective-permute-start.2 = (bf16[16,3712]{1,0:T(8,128)(2,1)S(1)}, bf16[16,3712]{1,0:T(8,128)(2,1)S(1)}, u32[]{:S(2)}, u32[]{:S(2)}) collective-permute-start(bf16[16,3712]{1,0:T(8,128)(2,1)S(1)} %get-tuple-element.13.refs_0_), channel_id=1, source_target_pairs={{0,12},{4,8},{8,4},{12,0},{1,13},{5,9},{9,5},{13,1},{2,14},{6,10},... | collective-permute-start | bytes 356360 | tf_op jit(solution)/shard_map/ppermute | solution.py:269
  6.9 0.0 collective-permute-start.1
  6.9 1.7 %collective-permute-start.4 = (bf16[16,3712]{1,0:T(8,128)(2,1)S(1)}, bf16[16,3712]{1,0:T(8,128)(2,1)S(1)}, u32[]{:S(2)}, u32[]{:S(2)}) collective-permute-start(bf16[16,3712]{1,0:T(8,128)(2,1)S(1)} %get-tuple-element.13.refs_0_), channel_id=1, source_target_pairs={{0,6},{2,4},{4,2},{6,0},{8,14},{10,12},{12,10},{14,8},{1,7},{3,5},... | collective-permute-start | bytes 356360 | tf_op jit(solution)/shard_map/ppermute | solution.py:269
  8.6 0.4 collective-permute-start.3
  9.0 0.2 reshape.25.qr_ref
  9.2 0.0 copy-start
  9.2 0.7 %copy-done = s32[16]{0:T(128)S(1)} copy-done((s32[16]{0:T(128)S(1)}, s32[16]{0:T(128)}, u32[]{:S(2)}) %copy-start) | copy-done | bytes 88
  9.9 5.8 %shard_map.105 = (bf16[16,64,512]{2,1,0:T(8,128)(2,1)}, bf16[3584,1024]{1,0:T(8,128)(2,1)S(1)}) custom-call(s32[16]{0:T(128)S(1)} %copy-done, bf16[16,64,512]{2,1,0:T(8,128)(2,1)} %ql_ref.1, bf16[16,64,64]{2,1,0:T(8,128)(2,1)S(1)} %reshape.25.qr_ref, bf16[16,128,512]{2,1,0:T(8,128)(2,1)} %cl_ref.3, bf16[16,64,128]{2,1,0:T(8,128)(2,1)} %cr_ref.3, ...), custom_call_target="tpu_custom_call" | custom-call | tf_op jit(solution)/shard_map/pallas_call | solution.py:95
  15.7 0.0 collective-permute-done.2.refs_3_
  15.7 1.5 %collective-permute-start = (bf16[16,3712]{1,0:T(8,128)(2,1)S(1)}, bf16[16,3712]{1,0:T(8,128)(2,1)S(1)}, u32[]{:S(2)}, u32[]{:S(2)}) collective-permute-start(bf16[16,3712]{1,0:T(8,128)(2,1)S(1)} %get-tuple-element.13.refs_0_), channel_id=1, source_target_pairs={{0,4},{4,0},{8,12},{12,8},{1,5},{5,1},{9,13},{13,9},{2,6},{6,2},{1... | collective-permute-start | bytes 356360 | tf_op jit(solution)/shard_map/ppermute | solution.py:269
  17.2 0.4 collective-permute-done.1.refs_2_
  17.5 1.5 %collective-permute-start.5 = (bf16[16,3712]{1,0:T(8,128)(2,1)S(1)}, bf16[16,3712]{1,0:T(8,128)(2,1)S(1)}, u32[]{:S(2)}, u32[]{:S(2)}) collective-permute-start(bf16[16,3712]{1,0:T(8,128)(2,1)S(1)} %collective-permute-done.1.refs_2_), channel_id=1, source_target_pairs={{0,2},{2,0},{1,3},{3,1},{4,6},{6,4},{5,7},{7,5},{8,10},{10,8},{9,1... | collective-permute-start | bytes 356360 | tf_op jit(solution)/shard_map/ppermute | solution.py:269
  19.0 0.0 collective-permute-done.4.refs_5_
  19.0 0.5 %collective-permute-start.6 = (bf16[16,3712]{1,0:T(8,128)(2,1)S(1)}, bf16[16,3712]{1,0:T(8,128)(2,1)S(1)}, u32[]{:S(2)}, u32[]{:S(2)}) collective-permute-start(bf16[16,3712]{1,0:T(8,128)(2,1)S(1)} %collective-permute-done.2.refs_3_), channel_id=1, source_target_pairs={{0,2},{2,0},{1,3},{3,1},{4,6},{6,4},{5,7},{7,5},{8,10},{10,8},{9,1... | collective-permute-start | bytes 356360 | tf_op jit(solution)/shard_map/ppermute | solution.py:269
  19.6 0.0 collective-permute-done.3.refs_4_
  19.6 1.0 %collective-permute-done.refs_1_ = bf16[16,3712]{1,0:T(8,128)(2,1)S(1)} collective-permute-done((bf16[16,3712]{1,0:T(8,128)(2,1)S(1)}, bf16[16,3712]{1,0:T(8,128)(2,1)S(1)}, u32[]{:S(2)}, u32[]{:S(2)}) %collective-permute-start) | collective-permute-done | bytes 118816 | tf_op jit(solution)/shard_map/ppermute | solution.py:269
  20.6 3.0 %collective-permute-done.5.refs_6_ = bf16[16,3712]{1,0:T(8,128)(2,1)S(1)} collective-permute-done((bf16[16,3712]{1,0:T(8,128)(2,1)S(1)}, bf16[16,3712]{1,0:T(8,128)(2,1)S(1)}, u32[]{:S(2)}, u32[]{:S(2)}) %collective-permute-start.5) | collective-permute-done | bytes 118816 | tf_op jit(solution)/shard_map/ppermute | solution.py:269
  23.7 1.3 %collective-permute-done.6.refs_7_ = bf16[16,3712]{1,0:T(8,128)(2,1)S(1)} collective-permute-done((bf16[16,3712]{1,0:T(8,128)(2,1)S(1)}, bf16[16,3712]{1,0:T(8,128)(2,1)S(1)}, u32[]{:S(2)}, u32[]{:S(2)}) %collective-permute-start.6) | collective-permute-done | bytes 118816 | tf_op jit(solution)/shard_map/ppermute | solution.py:269
  24.9 0.0 collective-permute-done.7.refs_9_
  24.9 5.2 %shard_map.106 = (f32[64,1024]{1,0:T(8,128)S(1)}, bf16[64,1024]{1,0:T(8,128)(2,1)S(1)}) custom-call(bf16[16,3712]{1,0:T(8,128)(2,1)S(1)} %get-tuple-element.13.refs_0_, bf16[16,3712]{1,0:T(8,128)(2,1)S(1)} %collective-permute-done.refs_1_, bf16[16,3712]{1,0:T(8,128)(2,1)S(1)} %collective-permute-done.1.refs_2_, ...), custom_call_target="tpu_custom_call" | custom-call | flops 1879048192 | bytes 14680064 | tf_op jit(solution)/shard_map/pallas_call | solution.py:247
  30.1 1.6 %collective-permute-start.8 = (bf16[64,1024]{1,0:T(8,128)(2,1)S(1)}, bf16[64,1024]{1,0:T(8,128)(2,1)S(1)}, u32[]{:S(2)}, u32[]{:S(2)}) collective-permute-start(bf16[64,1024]{1,0:T(8,128)(2,1)S(1)} %get-tuple-element.21), channel_id=1, source_target_pairs={{0,2},{2,0},{1,3},{3,1},{4,6},{6,4},{5,7},{7,5},{8,10},{10,8},{9,1... | collective-permute-start | bytes 393224 | tf_op jit(solution)/shard_map/ppermute | solution.py:269
  31.7 3.6 %shard_map.107 = bf16[16,64,512]{2,1,0:T(8,128)(2,1)} custom-call(s32[16]{0:T(128)S(1)} %copy-done.1, bf16[16,64,512]{2,1,0:T(8,128)(2,1)} %ql_ref.1, bf16[16,64,64]{2,1,0:T(8,128)(2,1)S(1)} %reshape.25.qr_ref, bf16[16,128,512]{2,1,0:T(8,128)(2,1)} %cl_ref.3, bf16[16,64,128]{2,1,0:T(8,128)(2,1)} %cr_ref.3, ...), custom_call_target="tpu_custom_call", output_to_operand_aliasing={{}: (5, {})} | custom-call | tf_op jit(solution)/shard_map/pallas_call | solution.py:95
  35.3 0.0 collective-permute-done.8
  35.3 2.5 %collective-permute-start.9 = (bf16[16,1024]{1,0:T(8,128)(2,1)S(1)}, bf16[16,1024]{1,0:T(8,128)(2,1)S(1)}, u32[]{:S(2)}, u32[]{:S(2)}) collective-permute-start(bf16[16,1024]{1,0:T(8,128)(2,1)S(1)} %get-tuple-element.24), channel_id=1, source_target_pairs={{0,12},{4,8},{8,4},{12,0},{1,13},{5,9},{9,5},{13,1},{2,14},{6,10},... | collective-permute-start | bytes 98312 | tf_op jit(solution)/shard_map/ppermute | solution.py:269
  37.8 0.0 collective-permute-start.11
  37.9 1.9 %collective-permute-start.10 = (bf16[16,1024]{1,0:T(8,128)(2,1)S(1)}, bf16[16,1024]{1,0:T(8,128)(2,1)S(1)}, u32[]{:S(2)}, u32[]{:S(2)}) collective-permute-start(bf16[16,1024]{1,0:T(8,128)(2,1)S(1)} %get-tuple-element.26), channel_id=1, source_target_pairs={{0,8},{4,12},{8,0},{12,4},{1,9},{5,13},{9,1},{13,5},{2,10},{6,14},... | collective-permute-start | bytes 98312 | tf_op jit(solution)/shard_map/ppermute | solution.py:269
  39.8 1.6 %collective-permute-done.9 = bf16[16,1024]{1,0:T(8,128)(2,1)S(1)} collective-permute-done((bf16[16,1024]{1,0:T(8,128)(2,1)S(1)}, bf16[16,1024]{1,0:T(8,128)(2,1)S(1)}, u32[]{:S(2)}, u32[]{:S(2)}) %collective-permute-start.9) | collective-permute-done | bytes 32800 | tf_op jit(solution)/shard_map/ppermute | solution.py:269
  41.4 0.4 collective-permute-done.11
  41.8 0.9 %collective-permute-done.10 = bf16[16,1024]{1,0:T(8,128)(2,1)S(1)} collective-permute-done((bf16[16,1024]{1,0:T(8,128)(2,1)S(1)}, bf16[16,1024]{1,0:T(8,128)(2,1)S(1)}, u32[]{:S(2)}, u32[]{:S(2)}) %collective-permute-start.10) | collective-permute-done | bytes 32800 | tf_op jit(solution)/shard_map/ppermute | solution.py:269
  42.7 0.6 %add_convert_fusion = bf16[16,1024]{1,0:T(8,128)(2,1)} fusion(bf16[16,1024]{1,0:T(8,128)(2,1)S(1)} %collective-permute-done.11, bf16[16,1024]{1,0:T(8,128)(2,1)S(1)} %collective-permute-done.10, bf16[16,1024]{1,0:T(8,128)(2,1)S(1)} %collective-permute-done.9, f32[64,1024]{1,0:T(8,128)S(1)} %get-tuple-element.20, bf16[64,1024]{1,0:T(8,128)(2,1)S(1)} %collective-permute-done.8), kind=kLoop, calls=%fused_computation | loop fusion | flops 147456 | bytes 229376 | tf_op jit(solution)/shard_map/convert_element_type | solution.py:309
  (3 shorter events, 0.0 us)
Async XLA Ops:
  0.6 24.3 %collective-permute-start.7 = (bf16[3584,1024]{1,0:T(8,128)(2,1)}, bf16[3584,1024]{1,0:T(8,128)(2,1)}, u32[]{:S(2)}, u32[]{:S(2)}) collective-permute-start(bf16[3584,1024]{1,0:T(8,128)(2,1)} %bitcast.3), channel_id=1, source_target_pairs={{0,1},{1,0},{2,3},{3,2},{4,5},{5,4},{6,7},{7,6},{8,9},{9,8},{10,11... | collective-permute-start | bytes 22020104 | tf_op jit(solution)/shard_map/ppermute | solution.py:269
  2.2 13.5 %collective-permute-start.2 = (bf16[16,3712]{1,0:T(8,128)(2,1)S(1)}, bf16[16,3712]{1,0:T(8,128)(2,1)S(1)}, u32[]{:S(2)}, u32[]{:S(2)}) collective-permute-start(bf16[16,3712]{1,0:T(8,128)(2,1)S(1)} %get-tuple-element.13.refs_0_), channel_id=1, source_target_pairs={{0,12},{4,8},{8,4},{12,0},{1,13},{5,9},{9,5},{13,1},{2,14},{6,10},... | collective-permute-start | bytes 356360 | tf_op jit(solution)/shard_map/ppermute | solution.py:269
  6.9 10.7 %collective-permute-start.1 = (bf16[16,3712]{1,0:T(8,128)(2,1)S(1)}, bf16[16,3712]{1,0:T(8,128)(2,1)S(1)}, u32[]{:S(2)}, u32[]{:S(2)}) collective-permute-start(bf16[16,3712]{1,0:T(8,128)(2,1)S(1)} %get-tuple-element.13.refs_0_), channel_id=1, source_target_pairs={{0,8},{4,12},{8,0},{12,4},{1,9},{5,13},{9,1},{13,5},{2,10},{6,14},... | collective-permute-start | bytes 356360 | tf_op jit(solution)/shard_map/ppermute | solution.py:269
  6.9 12.2 %collective-permute-start.4 = (bf16[16,3712]{1,0:T(8,128)(2,1)S(1)}, bf16[16,3712]{1,0:T(8,128)(2,1)S(1)}, u32[]{:S(2)}, u32[]{:S(2)}) collective-permute-start(bf16[16,3712]{1,0:T(8,128)(2,1)S(1)} %get-tuple-element.13.refs_0_), channel_id=1, source_target_pairs={{0,6},{2,4},{4,2},{6,0},{8,14},{10,12},{12,10},{14,8},{1,7},{3,5},... | collective-permute-start | bytes 356360 | tf_op jit(solution)/shard_map/ppermute | solution.py:269
  8.6 11.0 %collective-permute-start.3 = (bf16[16,3712]{1,0:T(8,128)(2,1)S(1)}, bf16[16,3712]{1,0:T(8,128)(2,1)S(1)}, u32[]{:S(2)}, u32[]{:S(2)}) collective-permute-start(bf16[16,3712]{1,0:T(8,128)(2,1)S(1)} %get-tuple-element.13.refs_0_), channel_id=1, source_target_pairs={{0,2},{2,0},{1,3},{3,1},{4,6},{6,4},{5,7},{7,5},{8,10},{10,8},{9,1... | collective-permute-start | bytes 356360 | tf_op jit(solution)/shard_map/ppermute | solution.py:269
  9.2 0.7 %copy-start = (s32[16]{0:T(128)S(1)}, s32[16]{0:T(128)}, u32[]{:S(2)}) copy-start(s32[16]{0:T(128)} %lengths_ref.3) | copy-start | bytes 196
  15.7 4.9 %collective-permute-start = (bf16[16,3712]{1,0:T(8,128)(2,1)S(1)}, bf16[16,3712]{1,0:T(8,128)(2,1)S(1)}, u32[]{:S(2)}, u32[]{:S(2)}) collective-permute-start(bf16[16,3712]{1,0:T(8,128)(2,1)S(1)} %get-tuple-element.13.refs_0_), channel_id=1, source_target_pairs={{0,4},{4,0},{8,12},{12,8},{1,5},{5,1},{9,13},{13,9},{2,6},{6,2},{1... | collective-permute-start | bytes 356360 | tf_op jit(solution)/shard_map/ppermute | solution.py:269
  17.5 6.1 %collective-permute-start.5 = (bf16[16,3712]{1,0:T(8,128)(2,1)S(1)}, bf16[16,3712]{1,0:T(8,128)(2,1)S(1)}, u32[]{:S(2)}, u32[]{:S(2)}) collective-permute-start(bf16[16,3712]{1,0:T(8,128)(2,1)S(1)} %collective-permute-done.1.refs_2_), channel_id=1, source_target_pairs={{0,2},{2,0},{1,3},{3,1},{4,6},{6,4},{5,7},{7,5},{8,10},{10,8},{9,1... | collective-permute-start | bytes 356360 | tf_op jit(solution)/shard_map/ppermute | solution.py:269
  19.0 5.9 %collective-permute-start.6 = (bf16[16,3712]{1,0:T(8,128)(2,1)S(1)}, bf16[16,3712]{1,0:T(8,128)(2,1)S(1)}, u32[]{:S(2)}, u32[]{:S(2)}) collective-permute-start(bf16[16,3712]{1,0:T(8,128)(2,1)S(1)} %collective-permute-done.2.refs_3_), channel_id=1, source_target_pairs={{0,2},{2,0},{1,3},{3,1},{4,6},{6,4},{5,7},{7,5},{8,10},{10,8},{9,1... | collective-permute-start | bytes 356360 | tf_op jit(solution)/shard_map/ppermute | solution.py:269
  24.9 6.8 %copy-start.1 = (s32[16]{0:T(128)S(1)}, s32[16]{0:T(128)}, u32[]{:S(2)}) copy-start(s32[16]{0:T(128)} %lengths_ref.3) | copy-start | bytes 196
  30.1 5.2 %collective-permute-start.8 = (bf16[64,1024]{1,0:T(8,128)(2,1)S(1)}, bf16[64,1024]{1,0:T(8,128)(2,1)S(1)}, u32[]{:S(2)}, u32[]{:S(2)}) collective-permute-start(bf16[64,1024]{1,0:T(8,128)(2,1)S(1)} %get-tuple-element.21), channel_id=1, source_target_pairs={{0,2},{2,0},{1,3},{3,1},{4,6},{6,4},{5,7},{7,5},{8,10},{10,8},{9,1... | collective-permute-start | bytes 393224 | tf_op jit(solution)/shard_map/ppermute | solution.py:269
  35.3 6.1 %collective-permute-start.9 = (bf16[16,1024]{1,0:T(8,128)(2,1)S(1)}, bf16[16,1024]{1,0:T(8,128)(2,1)S(1)}, u32[]{:S(2)}, u32[]{:S(2)}) collective-permute-start(bf16[16,1024]{1,0:T(8,128)(2,1)S(1)} %get-tuple-element.24), channel_id=1, source_target_pairs={{0,12},{4,8},{8,4},{12,0},{1,13},{5,9},{9,5},{13,1},{2,14},{6,10},... | collective-permute-start | bytes 98312 | tf_op jit(solution)/shard_map/ppermute | solution.py:269
  37.8 3.9 %collective-permute-start.11 = (bf16[16,1024]{1,0:T(8,128)(2,1)S(1)}, bf16[16,1024]{1,0:T(8,128)(2,1)S(1)}, u32[]{:S(2)}, u32[]{:S(2)}) collective-permute-start(bf16[16,1024]{1,0:T(8,128)(2,1)S(1)} %get-tuple-element.25), channel_id=1, source_target_pairs={{0,4},{4,0},{8,12},{12,8},{1,5},{5,1},{9,13},{13,9},{2,6},{6,2},{1... | collective-permute-start | bytes 98312 | tf_op jit(solution)/shard_map/ppermute | solution.py:269
  37.9 4.8 %collective-permute-start.10 = (bf16[16,1024]{1,0:T(8,128)(2,1)S(1)}, bf16[16,1024]{1,0:T(8,128)(2,1)S(1)}, u32[]{:S(2)}, u32[]{:S(2)}) collective-permute-start(bf16[16,1024]{1,0:T(8,128)(2,1)S(1)} %get-tuple-element.26), channel_id=1, source_target_pairs={{0,8},{4,12},{8,0},{12,4},{1,9},{5,13},{9,1},{13,5},{2,10},{6,14},... | collective-permute-start | bytes 98312 | tf_op jit(solution)/shard_map/ppermute | solution.py:269

commit v3 on v2

v3 whole, which is shorter than its diff:
```python
import functools

import jax
import jax.numpy as jnp
from jax import lax
from jax.experimental import pallas as pl
from jax.experimental.pallas import tpu as pltpu
from jax.sharding import PartitionSpec as P

score_scale = 192.0 ** (-0.5)
EXPERT_AXES = ("node", "local", "pair")
LANES = 128
VMEM_LIMIT = 8 * 2**20


def slot_tables(picked, weights, experts, capacity):
    row_count, choose = picked.shape
    flat_picks = picked.reshape(-1)
    matches = (flat_picks[:, None] == jnp.arange(experts, dtype=jnp.int32)[None, :]).astype(
        jnp.int32
    )
    earlier = jnp.cumsum(matches, axis=0) - matches
    position = jnp.sum(earlier * matches, axis=1)
    slot_index = flat_picks * capacity + position
    slot_hits = (
        slot_index[:, None] == jnp.arange(experts * capacity, dtype=jnp.int32)[None, :]
    ).astype(jnp.float32)
    owner = (
        jnp.arange(row_count * choose, dtype=jnp.int32)[:, None] // choose
        == jnp.arange(row_count, dtype=jnp.int32)[None, :]
    ).astype(jnp.float32)
    dispatch = jnp.dot(slot_hits.T, owner, precision=lax.Precision.HIGHEST)
    combine = jnp.dot(
        owner.T,
        slot_hits * weights.astype(jnp.float32).reshape(-1)[:, None],
        precision=lax.Precision.HIGHEST,
    )
    return (dispatch, combine)


def attend_core(first, limits, ql_ref, qr_ref, cl_ref, cr_ref, out_ref, pairs_ref, rotary_ref):
    rows, heads, _ = ql_ref.shape
    rope, context = cr_ref.shape[1:]
    all_rows, width = qr_ref.shape
    place = lax.broadcasted_iota(jnp.int32, (heads, context), 1)
    pairs = width // (2 * rope)
    for p in range(pairs):
        pairs_ref[pl.ds(p * all_rows, all_rows), :] = qr_ref[
            :, p * 2 * rope : (p + 1) * 2 * rope
        ].astype(jnp.float32)
    for r in range(rows):
        both = pairs_ref[pl.ds(first + r, pairs, stride=all_rows), :].astype(jnp.bfloat16)
        for odd in range(2):
            rotary_ref[r, pl.ds(odd, pairs, stride=2), :] = jnp.dot(
                both[:, odd * rope : (odd + 1) * rope],
                cr_ref[r],
                preferred_element_type=jnp.float32,
            )
    scores = []
    for r in range(rows):
        s = lax.dot_general(
            ql_ref[r], cl_ref[r], (((1,), (1,)), ((), ())), preferred_element_type=jnp.float32
        )
        s = (s + rotary_ref[r]) * score_scale
        scores.append(jnp.where(place < limits[r], s, -1e30))
    probs = []
    for s in scores:
        exponent = jnp.exp(s - jnp.max(s, axis=1, keepdims=True))
        probs.append((exponent / jnp.sum(exponent, axis=1, keepdims=True)).astype(jnp.bfloat16))
    for r, p in enumerate(probs):
        out_ref[r] = jnp.dot(p, cl_ref[r], preferred_element_type=jnp.float32).astype(
            out_ref.dtype
        )


def fetch(sources, targets, sems):
    copies = [
        pltpu.make_async_copy(source, target, sems.at[i])
        for i, (source, target) in enumerate(zip(sources, targets))
    ]
    for copy in copies:
        copy.start()
    return copies


def attend_kernel(first, lengths_hbm, ql_hbm, qr_hbm, cl_hbm, cr_hbm, out_hbm, *scratch):
    lengths_ref, ql_ref, qr_ref, cl_ref, cr_ref, out_ref, pairs_ref, rotary_ref, sems = scratch
    rows = ql_ref.shape[0]
    part = pl.ds(first, rows)
    sources = (lengths_hbm, qr_hbm, cr_hbm.at[part], cl_hbm.at[part], ql_hbm.at[part])
    for copy in fetch(sources, (lengths_ref, qr_ref, cr_ref, cl_ref, ql_ref), sems):
        copy.wait()
    limits = [lengths_ref[first + r] for r in range(rows)]
    attend_core(first, limits, ql_ref, qr_ref, cl_ref, cr_ref, out_ref, pairs_ref, rotary_ref)
    for copy in fetch((out_ref,), (out_hbm.at[part],), sems):
        copy.wait()


def staged_kernel(first, limits_ref, ql_ref, qr_ref, cl_ref, cr_ref, so_far, out_hbm, *scratch):
    out_ref, pairs_ref, rotary_ref, sems = scratch
    rows = ql_ref.shape[0]
    limits = [limits_ref[pl.ds(r, 1), :] for r in range(rows)]
    attend_core(first, limits, ql_ref, qr_ref, cl_ref, cr_ref, out_ref, pairs_ref, rotary_ref)
    for copy in fetch((out_ref,), (out_hbm.at[pl.ds(first, rows)],), sems):
        copy.wait()


def attend_cost(count, heads, context, latent, rope):
    return pl.CostEstimate(
        flops=2 * count * heads * context * (2 * latent + rope),
        bytes_accessed=10 * count * latent * (2 * heads + context),
        transcendentals=count * heads * context,
    )


ANYWHERE = pl.BlockSpec(memory_space=pl.ANY)
IN_VMEM = pl.BlockSpec(memory_space=pltpu.VMEM)


def attend_rows(first, count, query_latent, query_rope, cache_latent, cache_rope, lengths):
    row_count, heads, latent = query_latent.shape
    rope, context = cache_rope.shape[1:]
    operands = (lengths, query_latent, query_rope, cache_latent, cache_rope)
    return pl.pallas_call(
        functools.partial(attend_kernel, first),
        out_shape=pltpu.HBM((row_count, heads, latent), jnp.bfloat16),
        in_specs=[ANYWHERE] * 5,
        out_specs=ANYWHERE,
        scratch_shapes=[
            pltpu.SMEM(lengths.shape, lengths.dtype),
            pltpu.VMEM((count, heads, latent), jnp.bfloat16),
            pltpu.VMEM(query_rope.shape, jnp.bfloat16),
            pltpu.VMEM((count, context, latent), jnp.bfloat16),
            pltpu.VMEM((count, rope, context), jnp.bfloat16),
            pltpu.VMEM((count, heads, latent), jnp.bfloat16),
            pltpu.VMEM((row_count * heads // 2, 2 * rope), jnp.float32),
            pltpu.VMEM((count, heads, context), jnp.float32),
            pltpu.SemaphoreType.DMA((5,)),
        ],
        compiler_params=pltpu.CompilerParams(vmem_limit_bytes=(count + 4) * 2**20),
        cost_estimate=attend_cost(count, heads, context, latent, rope),
    )(*map(in_hbm, operands))


def attend_staged(first, staged, so_far):
    limits, query_latent, query_rope, cache_latent, cache_rope = staged
    count, heads, latent = query_latent.shape
    rope, context = cache_rope.shape[1:]
    return pl.pallas_call(
        functools.partial(staged_kernel, first),
        out_shape=pltpu.HBM(so_far.shape, so_far.dtype),
        in_specs=[IN_VMEM] * 5 + [ANYWHERE],
        out_specs=ANYWHERE,
        scratch_shapes=[
            pltpu.VMEM((count, heads, latent), jnp.bfloat16),
            pltpu.VMEM((so_far.shape[0] * heads // 2, 2 * rope), jnp.float32),
            pltpu.VMEM((count, heads, context), jnp.float32),
            pltpu.SemaphoreType.DMA((1,)),
        ],
        input_output_aliases={5: 0},
        compiler_params=pltpu.CompilerParams(vmem_limit_bytes=(count + 4) * 2**20),
        cost_estimate=attend_cost(count, heads, context, latent, rope),
    )(*map(in_vmem, staged), so_far)


def stage_kernel(first, matrix_hbm, lengths_hbm, ql_hbm, qr_hbm, cl_hbm, cr_hbm, *refs):
    matrix_ref, limits_ref, ql_ref, qr_ref, cl_ref, cr_ref, lengths_ref, sems = refs
    rows = ql_ref.shape[0]
    part = pl.ds(first, rows)
    pieces = sems.shape[0] - 5
    step = matrix_hbm.shape[0] // pieces
    cuts = [pl.ds(i * step, step) for i in range(pieces)]
    sources = [lengths_hbm, qr_hbm, cr_hbm.at[part], cl_hbm.at[part], ql_hbm.at[part]]
    targets = [lengths_ref, qr_ref, cr_ref, cl_ref, ql_ref]
    copies = fetch(
        sources + [matrix_hbm.at[cut] for cut in cuts],
        targets + [matrix_ref.at[cut] for cut in cuts],
        sems,
    )
    for i, copy in enumerate(copies):
        copy.wait()
        if i == 0:
            for r in range(rows):
                limits_ref[pl.ds(r, 1), :] = jnp.full(
                    (1, limits_ref.shape[1]), lengths_ref[first + r], jnp.int32
                )


def stage(first, count, matrix, query_latent, query_rope, cache_latent, cache_rope, lengths):
    heads, latent = query_latent.shape[1:]
    rope, context = cache_rope.shape[1:]
    operands = (matrix, lengths, query_latent, query_rope, cache_latent, cache_rope)
    out = pl.pallas_call(
        functools.partial(stage_kernel, first),
        out_shape=[
            pltpu.VMEM(matrix.shape, matrix.dtype),
            pltpu.VMEM((count, context), jnp.int32),
            pltpu.VMEM((count, heads, latent), jnp.bfloat16),
            pltpu.VMEM(query_rope.shape, jnp.bfloat16),
            pltpu.VMEM((count, context, latent), jnp.bfloat16),
            pltpu.VMEM((count, rope, context), jnp.bfloat16),
        ],
        in_specs=[ANYWHERE] * 6,
        out_specs=[IN_VMEM] * 6,
        scratch_shapes=[
            pltpu.SMEM(lengths.shape, lengths.dtype),
            pltpu.SemaphoreType.DMA((5 + (4 if matrix.shape[0] % 64 == 0 else 1),)),
        ],
        compiler_params=pltpu.CompilerParams(vmem_limit_bytes=2**20),
        cost_estimate=pl.CostEstimate(
            flops=0, bytes_accessed=2 * matrix.size, transcendentals=0
        ),
    )(*map(in_hbm, operands))
    return out[0], out[1:]


def in_hbm(value):
    return pltpu.with_memory_space_constraint(value, pltpu.HBM)


def in_vmem(value):
    return pltpu.with_memory_space_constraint(value, pltpu.VMEM)


def expert_by_slots(tokens, expert_ids, combine_weights, expert_weight):
    row_count, model_width = tokens.shape
    choose = expert_ids.shape[1]
    experts = lax.axis_size(EXPERT_AXES)
    capacity = min(row_count, 3 * max(1, (row_count * choose + experts - 1) // experts))
    matrix = expert_weight[0]
    dispatch, combine = slot_tables(expert_ids, combine_weights, experts, capacity)
    outgoing = jnp.dot(
        dispatch.astype(jnp.bfloat16), tokens, preferred_element_type=jnp.float32
    ).astype(jnp.bfloat16)
    outgoing = outgoing.reshape(experts, capacity, model_width)
    received = lax.all_to_all(outgoing, EXPERT_AXES, split_axis=0, concat_axis=0, tiled=True)
    hidden = jnp.dot(received.reshape(-1, model_width), matrix, preferred_element_type=jnp.float32)
    returned = lax.all_to_all(
        jax.nn.silu(hidden).astype(jnp.bfloat16).reshape(received.shape[:-1] + (matrix.shape[1],)),
        EXPERT_AXES,
        split_axis=0,
        concat_axis=0,
        tiled=True,
    )
    returned = returned.reshape(experts * capacity, -1).astype(jnp.float32)
    mixture = jnp.dot(combine, returned, precision=lax.Precision.HIGHEST)
    return mixture.astype(jnp.bfloat16)


def payload_kernel(
    ids_hbm, weights_hbm, tokens_hbm, out_ref, ids_ref, weights_ref, sems
):
    choose, rows = ids_ref.shape
    width = tokens_hbm.shape[1]
    copies = [
        pltpu.make_async_copy(ids_hbm, ids_ref, sems.at[0]),
        pltpu.make_async_copy(weights_hbm, weights_ref, sems.at[1]),
        pltpu.make_async_copy(tokens_hbm, out_ref.at[:, pl.ds(0, width)], sems.at[2]),
    ]
    for copy in copies:
        copy.start()
    copies[0].wait()
    copies[1].wait()
    expert = lax.broadcasted_iota(jnp.int32, (LANES, rows), 0)
    table = jnp.zeros((LANES, rows), jnp.float32)
    ids, weights = ids_ref[...], weights_ref[...].astype(jnp.float32)
    for k in range(choose):
        table = table + jnp.where(expert == ids[k : k + 1], weights[k : k + 1], 0.0)
    eye = (
        lax.broadcasted_iota(jnp.int32, (rows, rows), 0)
        == lax.broadcasted_iota(jnp.int32, (rows, rows), 1)
    ).astype(jnp.bfloat16)
    out_ref[:, width:] = lax.dot_general(
        eye,
        table.astype(jnp.bfloat16),
        (((1,), (1,)), ((), ())),
        preferred_element_type=jnp.float32,
    ).astype(jnp.bfloat16)
    copies[2].wait()


def make_payload(tokens, expert_ids, combine_weights):
    rows, width = tokens.shape
    choose = expert_ids.shape[1]
    return pl.pallas_call(
        payload_kernel,
        out_shape=pltpu.VMEM((rows, width + LANES), jnp.bfloat16),
        in_specs=[pl.BlockSpec(memory_space=pl.ANY)] * 3,
        out_specs=pl.BlockSpec(memory_space=pltpu.VMEM),
        scratch_shapes=[
            pltpu.VMEM((choose, rows), jnp.int32),
            pltpu.VMEM((choose, rows), jnp.bfloat16),
            pltpu.SemaphoreType.DMA((3,)),
        ],
        compiler_params=pltpu.CompilerParams(vmem_limit_bytes=4 * 2**20),
        cost_estimate=pl.CostEstimate(
            flops=0, bytes_accessed=4 * rows * width, transcendentals=0
        ),
    )(in_hbm(expert_ids.T), in_hbm(combine_weights.T), in_hbm(tokens))


def expert_kernel(count, *refs):
    here = lax.axis_index(EXPERT_AXES).astype(jnp.int32)
    blocks, matrices = refs[:count], refs[count : count + 2]
    near_ref, far_ref = refs[count + 2 :]
    width, hidden = matrices[0].shape
    rows = jnp.concatenate([block[...] for block in blocks], axis=0)
    features, shares = rows[:, :width], rows[:, width:].astype(jnp.float32)
    lane = lax.broadcasted_iota(jnp.int32, shares.shape, 1)
    share = [
        jnp.sum(jnp.where(lane == (here ^ which), shares, 0.0), axis=1, keepdims=True)
        for which in range(2)
    ]
    half = near_ref.shape[0]
    tile = 256
    for n in range(0, hidden, tile):
        total = None
        for which, matrix_ref in enumerate(matrices):
            value = jnp.dot(
                features, matrix_ref[:, n : n + tile], preferred_element_type=jnp.float32
            )
            term = share[which] * (value / (1.0 + jnp.exp(-value)))
            total = term if total is None else total + term
        near_ref[:, n : n + tile] = total[:half]
        far_ref[:, n : n + tile] = total[half:].astype(jnp.bfloat16)


def serve(blocks, own, other):
    count = len(blocks)
    rows = blocks[0].shape[0]
    width, hidden = own.shape
    whole = pl.BlockSpec(memory_space=pltpu.VMEM)
    half = count // 2 * rows
    return pl.pallas_call(
        functools.partial(expert_kernel, count),
        out_shape=[
            pltpu.VMEM((half, hidden), jnp.float32),
            pltpu.VMEM((half, hidden), jnp.bfloat16),
        ],
        in_specs=[whole] * (count + 2),
        out_specs=[whole] * 2,
        compiler_params=pltpu.CompilerParams(vmem_limit_bytes=VMEM_LIMIT),
        cost_estimate=pl.CostEstimate(
            flops=4 * count * rows * width * hidden,
            bytes_accessed=4 * width * hidden,
            transcendentals=2 * count * rows * hidden,
        ),
    )(*map(in_vmem, blocks), in_vmem(own), in_vmem(other))


def swap(value, axis, size, mask):
    return lax.ppermute(value, axis, [(i, i ^ mask) for i in range(size)])


def tie(value, *others):
    return lax.optimization_barrier((value,) + others)[0]


def gathered(attention, tokens, expert_ids, combine_weights, expert_weight):
    nodes, locals_, pairs = (lax.axis_size(axis) for axis in EXPERT_AXES)
    rows = tokens.shape[0]
    own = expert_weight[0]
    other = swap(own, "pair", pairs, 1)

    query_latent, query_rope, cache_latent, cache_rope, lengths = attention
    mine = make_payload(tokens, expert_ids, combine_weights)
    near, far = {0: mine}, {}
    near[1] = swap(mine, "node", nodes, 1)
    far[0] = swap(mine, "local", locals_, 1)
    near[2] = swap(mine, "node", nodes, 2)
    count = query_latent.shape[0]
    half = count // 2
    rest = (query_rope, cache_latent, cache_rope, lengths)
    attended = attend_rows(0, half, tie(query_latent, mine), *rest)
    near[1], far[0], near[2], _ = lax.optimization_barrier((near[1], far[0], near[2], attended))
    near[3] = swap(near[2], "node", nodes, 1)
    far[2] = swap(near[2], "local", locals_, 1)
    far[1] = swap(far[0], "node", nodes, 1)
    far[3] = swap(near[3], "local", locals_, 1)
    own, staged = stage(half, count - half, tie(own, near[3]), query_latent, *rest)
    far[1], far[2], far[3], _ = lax.optimization_barrier((far[1], far[2], far[3], own))
    blocks = [near[n] for n in range(nodes)] + [far[n] for n in range(nodes)]
    kept, sent = serve(blocks, own, other)
    came = swap(sent, "local", locals_, 1)
    attended = attend_staged(half, staged, tie(attended, sent))
    came = tie(came, attended)
    kept = kept.reshape(nodes, rows, -1)
    came = came.reshape(nodes, rows, -1)
    total = kept[0] + came[0].astype(jnp.float32)
    for n in (2, 1, 3):
        part = (kept[n] + came[n].astype(jnp.float32)).astype(jnp.bfloat16)
        total = total + swap(part, "node", nodes, n).astype(jnp.float32)
    return total.astype(jnp.bfloat16), attended


def body(
    tokens,
    expert_ids,
    combine_weights,
    expert_weight,
    query_latent,
    query_rope,
    cache_latent,
    cache_rope,
    lengths,
):
    sizes = tuple(lax.axis_size(axis) for axis in EXPERT_AXES)
    attention = (query_latent, query_rope, cache_latent, cache_rope, lengths)
    if sizes == (4, 2, 2):
        return gathered(attention, tokens, expert_ids, combine_weights, expert_weight)
    count = query_latent.shape[0]
    attended = attend_rows(0, count, query_latent, query_rope, cache_latent, cache_rope, lengths)
    expert_mix = expert_by_slots(tokens, expert_ids, combine_weights, expert_weight)
    return (expert_mix, attended)


def solution(mesh):
    rows = ("group",) + EXPERT_AXES
    return jax.shard_map(
        body,
        mesh=mesh,
        in_specs=(
            P(rows, None),
            P(rows, None),
            P(rows, None),
            P(EXPERT_AXES, None, None),
            P(rows, None, None),
            P(rows, None),
            P(rows, None, None),
            P(rows, None, None),
            P(rows),
        ),
        out_specs=(P(rows, None), P(rows, None, None)),
        check_vma=False,
    )
```

time: 43.6 us -> 40.4 us (0.927)
  Pallas kernels: 15.6 us -> 12.4 us
  waiting for transfers between devices: 8.66 us -> 11.6 us
  starting transfers between devices: 16.8 us -> 14.8 us
  local copies, waits for them, and re-layouts: 0.9 us -> 0 us
    ppermute x12, waiting for transfers between devices: 8.66 us -> 11.6 us  [swap(): return lax.ppermute(value, axis, [(i, i ^ mask) for i in range(size)])]
    pallas_call x1, Pallas kernels: 5.18 us -> 2.59 us  [serve(): pl.pallas_call(functools.partial(expert_kernel, count), out_shape=[pltpu....]
    ppermute x12, starting transfers between devices: 16.8 us -> 14.8 us  [swap(): return lax.ppermute(value, axis, [(i, i ^ mask) for i in range(size)])]
    unnamed x4 -> x0, local copies, waits for them, and re-layouts: 0.66 us -> none
    pallas_call x3 -> x4, Pallas kernels: 10.4 us -> 9.84 us  [the longest x1 3.82 us: stage(): pl.pallas_call(functools.partial(stage_kernel, first), out_shape=[pltpu.V...]
  transfers between devices with their start and end apart: 12 -> 12, of which waited for: 7 -> 8; matrix products, arithmetic and copies ran while one was open for 1% -> 0% of each run, Pallas kernels for 24% -> 24%
where the time goes in v3:
time: 40.4 us; the launch traced here: 40.2 us
  starting transfers between devices  14.8 us (37%)
  Pallas kernels  12.4 us (31%)
  waiting for transfers between devices  11.6 us (29%)
  between operations  0.7 us (2%)
  other arithmetic  0.66 us (2%)
    ppermute x12, starting transfers between devices, swap(): return lax.ppermute(value, axis, [(i, i ^ mask) for i in range(size)])  14.8 us
    ppermute x12, waiting for transfers between devices, swap(): return lax.ppermute(value, axis, [(i, i ^ mask) for i in range(size)])  11.6 us
    pallas_call x1, Pallas kernels, stage(): pl.pallas_call(functools.partial(stage_kernel, first), out_shape=[pltpu.V...  3.82 us
    pallas_call x1, Pallas kernels, attend_rows(): pl.pallas_call(functools.partial(attend_kernel, first), out_shape=pltpu.H...  3.29 us
    pallas_call x1, Pallas kernels, serve(): pl.pallas_call(functools.partial(expert_kernel, count), out_shape=[pltpu....  2.59 us
    pallas_call x1, Pallas kernels, attend_staged(): pl.pallas_call(functools.partial(staged_kernel, first), out_shape=pltpu.H...  1.77 us
    pallas_call x1, Pallas kernels, make_payload(): pl.pallas_call(payload_kernel, out_shape=pltpu.VMEM((rows, width + LANES)...  0.96 us
  transfers between devices with their start and end apart: 12, of which 8 were waited for; matrix products, arithmetic and copies ran while one was open for 0% of the time, Pallas kernels for 24%

profile of v3, /device:TPU:0, one launch (start us, length us, event | category | flops | bytes accessed | tf_op | source)
XLA Modules:
  0.0 40.2 jit_solution(4844898959888018180)
XLA Ops:
  0.6 0.5 %collective-permute-start.7 = (bf16[3584,1024]{1,0:T(8,128)(2,1)}, bf16[3584,1024]{1,0:T(8,128)(2,1)S(1)}, u32[]{:S(2)}, u32[]{:S(2)}) collective-permute-start(bf16[3584,1024]{1,0:T(8,128)(2,1)} %bitcast.3), channel_id=1, source_target_pairs={{0,1},{1,0},{2,3},{3,2},{4,5},{5,4},{6,7},{7,6},{8,9},{9,8},{10,11... | collective-permute-start | bytes 22020104 | tf_op jit(solution)/shard_map/ppermute | solution.py:352
  1.1 1.0 %shard_map.104.refs_0_ = bf16[16,3712]{1,0:T(8,128)(2,1)S(1)} custom-call(s32[8,16]{1,0:T(8,128)} %bitcast.5, bf16[8,16]{1,0:T(8,128)(2,1)} %bitcast.6, bf16[16,3584]{1,0:T(8,128)(2,1)} %tokens_hbm.1), custom_call_target="tpu_custom_call" | custom-call | bytes 229376 | tf_op jit(solution)/shard_map/pallas_call | solution.py:285
  2.1 3.7 %collective-permute-start.2 = (bf16[16,3712]{1,0:T(8,128)(2,1)S(1)}, bf16[16,3712]{1,0:T(8,128)(2,1)S(1)}, u32[]{:S(2)}, u32[]{:S(2)}) collective-permute-start(bf16[16,3712]{1,0:T(8,128)(2,1)S(1)} %shard_map.104.refs_0_), channel_id=1, source_target_pairs={{0,8},{4,12},{8,0},{12,4},{1,9},{5,13},{9,1},{13,5},{2,10},{6,14},... | collective-permute-start | bytes 356360 | tf_op jit(solution)/shard_map/ppermute | solution.py:352
  5.8 1.5 %collective-permute-start.1 = (bf16[16,3712]{1,0:T(8,128)(2,1)S(1)}, bf16[16,3712]{1,0:T(8,128)(2,1)S(1)}, u32[]{:S(2)}, u32[]{:S(2)}) collective-permute-start(bf16[16,3712]{1,0:T(8,128)(2,1)S(1)} %shard_map.104.refs_0_), channel_id=1, source_target_pairs={{0,2},{2,0},{1,3},{3,1},{4,6},{6,4},{5,7},{7,5},{8,10},{10,8},{9,1... | collective-permute-start | bytes 356360 | tf_op jit(solution)/shard_map/ppermute | solution.py:352
  7.3 1.6 %collective-permute-start = (bf16[16,3712]{1,0:T(8,128)(2,1)S(1)}, bf16[16,3712]{1,0:T(8,128)(2,1)S(1)}, u32[]{:S(2)}, u32[]{:S(2)}) collective-permute-start(bf16[16,3712]{1,0:T(8,128)(2,1)S(1)} %shard_map.104.refs_0_), channel_id=1, source_target_pairs={{0,4},{4,0},{8,12},{12,8},{1,5},{5,1},{9,13},{13,9},{2,6},{6,2},{1... | collective-permute-start | bytes 356360 | tf_op jit(solution)/shard_map/ppermute | solution.py:352
  8.8 3.3 %shard_map.105.so_far = bf16[16,64,512]{2,1,0:T(8,128)(2,1)} custom-call(s32[16]{0:T(128)} %lengths_hbm.3, bf16[16,64,512]{2,1,0:T(8,128)(2,1)} %ql_hbm.2, bf16[16,4096]{1,0:T(8,128)(2,1)} %qr_hbm.3, bf16[16,128,512]{2,1,0:T(8,128)(2,1)} %cl_hbm.3, bf16[16,64,128]{2,1,0:T(8,128)(2,1)} %cr_hbm.3), custom_call_target="tpu_custom_call" | custom-call | flops 142606336 | bytes 10485760 | tf_op jit(solution)/shard_map/pallas_call | solution.py:124
  12.1 0.2 collective-permute-done.2.refs_2_
  12.3 0.0 collective-permute-done.1.refs_4_
  12.3 1.4 %collective-permute-done.refs_1_ = bf16[16,3712]{1,0:T(8,128)(2,1)S(1)} collective-permute-done((bf16[16,3712]{1,0:T(8,128)(2,1)S(1)}, bf16[16,3712]{1,0:T(8,128)(2,1)S(1)}, u32[]{:S(2)}, u32[]{:S(2)}) %collective-permute-start) | collective-permute-done | bytes 118816 | tf_op jit(solution)/shard_map/ppermute | solution.py:352
  13.7 0.3 collective-permute-start.3
  14.0 1.5 %collective-permute-start.5 = (bf16[16,3712]{1,0:T(8,128)(2,1)S(1)}, bf16[16,3712]{1,0:T(8,128)(2,1)S(1)}, u32[]{:S(2)}, u32[]{:S(2)}) collective-permute-start(bf16[16,3712]{1,0:T(8,128)(2,1)S(1)} %collective-permute-done.2.refs_2_), channel_id=1, source_target_pairs={{0,2},{2,0},{1,3},{3,1},{4,6},{6,4},{5,7},{7,5},{8,10},{10,8},{9,1... | collective-permute-start | bytes 356360 | tf_op jit(solution)/shard_map/ppermute | solution.py:352
  15.5 0.8 %collective-permute-start.4 = (bf16[16,3712]{1,0:T(8,128)(2,1)S(1)}, bf16[16,3712]{1,0:T(8,128)(2,1)S(1)}, u32[]{:S(2)}, u32[]{:S(2)}) collective-permute-start(bf16[16,3712]{1,0:T(8,128)(2,1)S(1)} %collective-permute-done.1.refs_4_), channel_id=1, source_target_pairs={{0,4},{4,0},{8,12},{12,8},{1,5},{5,1},{9,13},{13,9},{2,6},{6,2},{1... | collective-permute-start | bytes 356360 | tf_op jit(solution)/shard_map/ppermute | solution.py:352
  16.3 3.4 %collective-permute-done.3.refs_3_ = bf16[16,3712]{1,0:T(8,128)(2,1)S(1)} collective-permute-done((bf16[16,3712]{1,0:T(8,128)(2,1)S(1)}, bf16[16,3712]{1,0:T(8,128)(2,1)S(1)}, u32[]{:S(2)}, u32[]{:S(2)}) %collective-permute-start.3) | collective-permute-done | bytes 118816 | tf_op jit(solution)/shard_map/ppermute | solution.py:352
  19.8 0.3 collective-permute-start.6
  20.1 3.8 %shard_map.106 = (bf16[3584,1024]{1,0:T(8,128)(2,1)S(1)}, s32[8,128]{1,0:T(8,128)S(1)}, bf16[8,64,512]{2,1,0:T(8,128)(2,1)S(1)}, bf16[16,4096]{1,0:T(8,128)(2,1)...) custom-call(bf16[3584,1024]{1,0:T(8,128)(2,1)} %bitcast.4, s32[16]{0:T(128)} %lengths_hbm.3, ...), custom_call_target="tpu_custom_call" | custom-call | bytes 7340032 | tf_op jit(solution)/shard_map/pallas_call | solution.py:193
  23.9 0.0 collective-permute-done.4.refs_5_
  23.9 0.0 collective-permute-done.5.refs_6_
  23.9 0.7 %collective-permute-done.6.refs_7_ = bf16[16,3712]{1,0:T(8,128)(2,1)S(1)} collective-permute-done((bf16[16,3712]{1,0:T(8,128)(2,1)S(1)}, bf16[16,3712]{1,0:T(8,128)(2,1)S(1)}, u32[]{:S(2)}, u32[]{:S(2)}) %collective-permute-start.6) | collective-permute-done | bytes 118816 | tf_op jit(solution)/shard_map/ppermute | solution.py:352
  24.6 0.0 collective-permute-done.7.refs_9_
  24.6 2.6 %shard_map.107 = (f32[64,1024]{1,0:T(8,128)S(1)}, bf16[64,1024]{1,0:T(8,128)(2,1)S(1)}) custom-call(bf16[16,3712]{1,0:T(8,128)(2,1)S(1)} %shard_map.104.refs_0_, bf16[16,3712]{1,0:T(8,128)(2,1)S(1)} %collective-permute-done.refs_1_, bf16[16,3712]{1,0:T(8,128)(2,1)S(1)} %collective-permute-done.2.refs_2_, ...), custom_call_target="tpu_custom_call" | custom-call | flops 1879048192 | bytes 14680064 | tf_op jit(solution)/shard_map/pallas_call | solution.py:334
  27.2 1.1 %collective-permute-start.8 = (bf16[64,1024]{1,0:T(8,128)(2,1)S(1)}, bf16[64,1024]{1,0:T(8,128)(2,1)S(1)}, u32[]{:S(2)}, u32[]{:S(2)}) collective-permute-start(bf16[64,1024]{1,0:T(8,128)(2,1)S(1)} %get-tuple-element.30), channel_id=1, source_target_pairs={{0,2},{2,0},{1,3},{3,1},{4,6},{6,4},{5,7},{7,5},{8,10},{10,8},{9,1... | collective-permute-start | bytes 393224 | tf_op jit(solution)/shard_map/ppermute | solution.py:352
  28.3 1.8 %shard_map.108 = bf16[16,64,512]{2,1,0:T(8,128)(2,1)} custom-call(s32[8,128]{1,0:T(8,128)S(1)} %get-tuple-element.31.limits_ref, bf16[8,64,512]{2,1,0:T(8,128)(2,1)S(1)} %get-tuple-element.32.ql_ref, bf16[16,4096]{1,0:T(8,128)(2,1)S(1)} %get-tuple-element.33.qr_ref, ...), custom_call_target="tpu_custom_call", output_to_operand_aliasing={{}: (5, {})} | custom-call | flops 142606336 | bytes 10485760 | tf_op jit(solution)/shard_map/pallas_call | solution.py:149
  30.1 2.1 %collective-permute-done.8 = bf16[64,1024]{1,0:T(8,128)(2,1)S(1)} collective-permute-done((bf16[64,1024]{1,0:T(8,128)(2,1)S(1)}, bf16[64,1024]{1,0:T(8,128)(2,1)S(1)}, u32[]{:S(2)}, u32[]{:S(2)}) %collective-permute-start.8) | collective-permute-done | bytes 131104 | tf_op jit(solution)/shard_map/ppermute | solution.py:352
  32.3 1.2 %collective-permute-start.9 = (bf16[16,1024]{1,0:T(8,128)(2,1)S(1)}, bf16[16,1024]{1,0:T(8,128)(2,1)S(1)}, u32[]{:S(2)}, u32[]{:S(2)}) collective-permute-start(bf16[16,1024]{1,0:T(8,128)(2,1)S(1)} %get-tuple-element.38), channel_id=1, source_target_pairs={{0,8},{4,12},{8,0},{12,4},{1,9},{5,13},{9,1},{13,5},{2,10},{6,14},... | collective-permute-start | bytes 98312 | tf_op jit(solution)/shard_map/ppermute | solution.py:352
  33.4 2.1 %collective-permute-start.11 = (bf16[16,1024]{1,0:T(8,128)(2,1)S(1)}, bf16[16,1024]{1,0:T(8,128)(2,1)S(1)}, u32[]{:S(2)}, u32[]{:S(2)}) collective-permute-start(bf16[16,1024]{1,0:T(8,128)(2,1)S(1)} %get-tuple-element.39), channel_id=1, source_target_pairs={{0,12},{4,8},{8,4},{12,0},{1,13},{5,9},{9,5},{13,1},{2,14},{6,10},... | collective-permute-start | bytes 98312 | tf_op jit(solution)/shard_map/ppermute | solution.py:352
  35.6 0.3 collective-permute-start.10
  35.8 1.3 %collective-permute-done.9 = bf16[16,1024]{1,0:T(8,128)(2,1)S(1)} collective-permute-done((bf16[16,1024]{1,0:T(8,128)(2,1)S(1)}, bf16[16,1024]{1,0:T(8,128)(2,1)S(1)}, u32[]{:S(2)}, u32[]{:S(2)}) %collective-permute-start.9) | collective-permute-done | bytes 32800 | tf_op jit(solution)/shard_map/ppermute | solution.py:352
  37.2 2.1 %collective-permute-done.11 = bf16[16,1024]{1,0:T(8,128)(2,1)S(1)} collective-permute-done((bf16[16,1024]{1,0:T(8,128)(2,1)S(1)}, bf16[16,1024]{1,0:T(8,128)(2,1)S(1)}, u32[]{:S(2)}, u32[]{:S(2)}) %collective-permute-start.11) | collective-permute-done | bytes 32800 | tf_op jit(solution)/shard_map/ppermute | solution.py:352
  39.2 0.3 collective-permute-done.10
  39.6 0.6 %add_convert_fusion = bf16[16,1024]{1,0:T(8,128)(2,1)} fusion(bf16[16,1024]{1,0:T(8,128)(2,1)S(1)} %collective-permute-done.11, bf16[16,1024]{1,0:T(8,128)(2,1)S(1)} %collective-permute-done.10, bf16[16,1024]{1,0:T(8,128)(2,1)S(1)} %collective-permute-done.9, f32[64,1024]{1,0:T(8,128)S(1)} %get-tuple-element.29, bf16[64,1024]{1,0:T(8,128)(2,1)S(1)} %collective-permute-done.8), kind=kLoop, calls=%fused_computation | loop fusion | flops 147456 | bytes 229376 | tf_op jit(solution)/shard_map/convert_element_type | solution.py:393
  (1 shorter events, 0.0 us)
Async XLA Ops:
  0.6 24.0 %collective-permute-start.7 = (bf16[3584,1024]{1,0:T(8,128)(2,1)}, bf16[3584,1024]{1,0:T(8,128)(2,1)S(1)}, u32[]{:S(2)}, u32[]{:S(2)}) collective-permute-start(bf16[3584,1024]{1,0:T(8,128)(2,1)} %bitcast.3), channel_id=1, source_target_pairs={{0,1},{1,0},{2,3},{3,2},{4,5},{5,4},{6,7},{7,6},{8,9},{9,8},{10,11... | collective-permute-start | bytes 22020104 | tf_op jit(solution)/shard_map/ppermute | solution.py:352
  2.1 10.2 %collective-permute-start.2 = (bf16[16,3712]{1,0:T(8,128)(2,1)S(1)}, bf16[16,3712]{1,0:T(8,128)(2,1)S(1)}, u32[]{:S(2)}, u32[]{:S(2)}) collective-permute-start(bf16[16,3712]{1,0:T(8,128)(2,1)S(1)} %shard_map.104.refs_0_), channel_id=1, source_target_pairs={{0,8},{4,12},{8,0},{12,4},{1,9},{5,13},{9,1},{13,5},{2,10},{6,14},... | collective-permute-start | bytes 356360 | tf_op jit(solution)/shard_map/ppermute | solution.py:352
  5.8 6.5 %collective-permute-start.1 = (bf16[16,3712]{1,0:T(8,128)(2,1)S(1)}, bf16[16,3712]{1,0:T(8,128)(2,1)S(1)}, u32[]{:S(2)}, u32[]{:S(2)}) collective-permute-start(bf16[16,3712]{1,0:T(8,128)(2,1)S(1)} %shard_map.104.refs_0_), channel_id=1, source_target_pairs={{0,2},{2,0},{1,3},{3,1},{4,6},{6,4},{5,7},{7,5},{8,10},{10,8},{9,1... | collective-permute-start | bytes 356360 | tf_op jit(solution)/shard_map/ppermute | solution.py:352
  7.3 6.5 %collective-permute-start = (bf16[16,3712]{1,0:T(8,128)(2,1)S(1)}, bf16[16,3712]{1,0:T(8,128)(2,1)S(1)}, u32[]{:S(2)}, u32[]{:S(2)}) collective-permute-start(bf16[16,3712]{1,0:T(8,128)(2,1)S(1)} %shard_map.104.refs_0_), channel_id=1, source_target_pairs={{0,4},{4,0},{8,12},{12,8},{1,5},{5,1},{9,13},{13,9},{2,6},{6,2},{1... | collective-permute-start | bytes 356360 | tf_op jit(solution)/shard_map/ppermute | solution.py:352
  13.7 6.1 %collective-permute-start.3 = (bf16[16,3712]{1,0:T(8,128)(2,1)S(1)}, bf16[16,3712]{1,0:T(8,128)(2,1)S(1)}, u32[]{:S(2)}, u32[]{:S(2)}) collective-permute-start(bf16[16,3712]{1,0:T(8,128)(2,1)S(1)} %collective-permute-done.2.refs_2_), channel_id=1, source_target_pairs={{0,4},{4,0},{8,12},{12,8},{1,5},{5,1},{9,13},{13,9},{2,6},{6,2},{1... | collective-permute-start | bytes 356360 | tf_op jit(solution)/shard_map/ppermute | solution.py:352
  14.0 9.9 %collective-permute-start.5 = (bf16[16,3712]{1,0:T(8,128)(2,1)S(1)}, bf16[16,3712]{1,0:T(8,128)(2,1)S(1)}, u32[]{:S(2)}, u32[]{:S(2)}) collective-permute-start(bf16[16,3712]{1,0:T(8,128)(2,1)S(1)} %collective-permute-done.2.refs_2_), channel_id=1, source_target_pairs={{0,2},{2,0},{1,3},{3,1},{4,6},{6,4},{5,7},{7,5},{8,10},{10,8},{9,1... | collective-permute-start | bytes 356360 | tf_op jit(solution)/shard_map/ppermute | solution.py:352
  15.5 8.4 %collective-permute-start.4 = (bf16[16,3712]{1,0:T(8,128)(2,1)S(1)}, bf16[16,3712]{1,0:T(8,128)(2,1)S(1)}, u32[]{:S(2)}, u32[]{:S(2)}) collective-permute-start(bf16[16,3712]{1,0:T(8,128)(2,1)S(1)} %collective-permute-done.1.refs_4_), channel_id=1, source_target_pairs={{0,4},{4,0},{8,12},{12,8},{1,5},{5,1},{9,13},{13,9},{2,6},{6,2},{1... | collective-permute-start | bytes 356360 | tf_op jit(solution)/shard_map/ppermute | solution.py:352
  19.8 4.8 %collective-permute-start.6 = (bf16[16,3712]{1,0:T(8,128)(2,1)S(1)}, bf16[16,3712]{1,0:T(8,128)(2,1)S(1)}, u32[]{:S(2)}, u32[]{:S(2)}) collective-permute-start(bf16[16,3712]{1,0:T(8,128)(2,1)S(1)} %collective-permute-done.3.refs_3_), channel_id=1, source_target_pairs={{0,2},{2,0},{1,3},{3,1},{4,6},{6,4},{5,7},{7,5},{8,10},{10,8},{9,1... | collective-permute-start | bytes 356360 | tf_op jit(solution)/shard_map/ppermute | solution.py:352
  27.2 5.0 %collective-permute-start.8 = (bf16[64,1024]{1,0:T(8,128)(2,1)S(1)}, bf16[64,1024]{1,0:T(8,128)(2,1)S(1)}, u32[]{:S(2)}, u32[]{:S(2)}) collective-permute-start(bf16[64,1024]{1,0:T(8,128)(2,1)S(1)} %get-tuple-element.30), channel_id=1, source_target_pairs={{0,2},{2,0},{1,3},{3,1},{4,6},{6,4},{5,7},{7,5},{8,10},{10,8},{9,1... | collective-permute-start | bytes 393224 | tf_op jit(solution)/shard_map/ppermute | solution.py:352
  32.3 4.9 %collective-permute-start.9 = (bf16[16,1024]{1,0:T(8,128)(2,1)S(1)}, bf16[16,1024]{1,0:T(8,128)(2,1)S(1)}, u32[]{:S(2)}, u32[]{:S(2)}) collective-permute-start(bf16[16,1024]{1,0:T(8,128)(2,1)S(1)} %get-tuple-element.38), channel_id=1, source_target_pairs={{0,8},{4,12},{8,0},{12,4},{1,9},{5,13},{9,1},{13,5},{2,10},{6,14},... | collective-permute-start | bytes 98312 | tf_op jit(solution)/shard_map/ppermute | solution.py:352
  33.4 5.8 %collective-permute-start.11 = (bf16[16,1024]{1,0:T(8,128)(2,1)S(1)}, bf16[16,1024]{1,0:T(8,128)(2,1)S(1)}, u32[]{:S(2)}, u32[]{:S(2)}) collective-permute-start(bf16[16,1024]{1,0:T(8,128)(2,1)S(1)} %get-tuple-element.39), channel_id=1, source_target_pairs={{0,12},{4,8},{8,4},{12,0},{1,13},{5,9},{9,5},{13,1},{2,14},{6,10},... | collective-permute-start | bytes 98312 | tf_op jit(solution)/shard_map/ppermute | solution.py:352
  35.6 4.0 %collective-permute-start.10 = (bf16[16,1024]{1,0:T(8,128)(2,1)S(1)}, bf16[16,1024]{1,0:T(8,128)(2,1)S(1)}, u32[]{:S(2)}, u32[]{:S(2)}) collective-permute-start(bf16[16,1024]{1,0:T(8,128)(2,1)S(1)} %get-tuple-element.40), channel_id=1, source_target_pairs={{0,4},{4,0},{8,12},{12,8},{1,5},{5,1},{9,13},{13,9},{2,6},{6,2},{1... | collective-permute-start | bytes 98312 | tf_op jit(solution)/shard_map/ppermute | solution.py:352

commit v4 on v3

--- a/solution.py
+++ b/solution.py
@@ -83,16 +83,27 @@
     return copies
 
 
-def attend_kernel(first, lengths_hbm, ql_hbm, qr_hbm, cl_hbm, cr_hbm, out_hbm, *scratch):
-    lengths_ref, ql_ref, qr_ref, cl_ref, cr_ref, out_ref, pairs_ref, rotary_ref, sems = scratch
-    rows = ql_ref.shape[0]
-    part = pl.ds(first, rows)
-    sources = (lengths_hbm, qr_hbm, cr_hbm.at[part], cl_hbm.at[part], ql_hbm.at[part])
-    for copy in fetch(sources, (lengths_ref, qr_ref, cr_ref, cl_ref, ql_ref), sems):
+def attend_kernel(split, lengths_hbm, ql_hbm, qr_hbm, cl_hbm, cr_hbm, out_hbm, *refs):
+    limits_ref, ql_late, qr_ref, cl_late, cr_late = refs[:5]
+    lengths_ref, ql_ref, cl_ref, cr_ref, out_ref, pairs_ref, rotary_ref, sems, late_sems = refs[5:]
+    part, late = pl.ds(0, split), pl.ds(split, ql_late.shape[0])
+    copies = fetch(
+        (lengths_hbm, qr_hbm, cr_hbm.at[part], cl_hbm.at[part], ql_hbm.at[part]),
+        (lengths_ref, qr_ref, cr_ref, cl_ref, ql_ref),
+        sems,
+    )
+    late_copies = fetch(
+        (cr_hbm.at[late], cl_hbm.at[late], ql_hbm.at[late]), (cr_late, cl_late, ql_late), late_sems
+    )
+    for copy in copies:
         copy.wait()
-    limits = [lengths_ref[first + r] for r in range(rows)]
-    attend_core(first, limits, ql_ref, qr_ref, cl_ref, cr_ref, out_ref, pairs_ref, rotary_ref)
-    for copy in fetch((out_ref,), (out_hbm.at[part],), sems):
+    for r in range(limits_ref.shape[0]):
+        limits_ref[pl.ds(r, 1), :] = jnp.full(
+            (1, limits_ref.shape[1]), lengths_ref[split + r], jnp.int32
+        )
+    limits = [lengths_ref[r] for r in range(split)]
+    attend_core(0, limits, ql_ref, qr_ref, cl_ref, cr_ref, out_ref, pairs_ref, rotary_ref)
+    for copy in fetch((out_ref,), (out_hbm.at[part],), sems) + late_copies:
         copy.wait()
 
 
@@ -117,29 +128,45 @@
 IN_VMEM = pl.BlockSpec(memory_space=pltpu.VMEM)
 
 
-def attend_rows(first, count, query_latent, query_rope, cache_latent, cache_rope, lengths):
+def attend_first(split, query_latent, query_rope, cache_latent, cache_rope, lengths):
     row_count, heads, latent = query_latent.shape
     rope, context = cache_rope.shape[1:]
     operands = (lengths, query_latent, query_rope, cache_latent, cache_rope)
-    return pl.pallas_call(
-        functools.partial(attend_kernel, first),
-        out_shape=pltpu.HBM((row_count, heads, latent), jnp.bfloat16),
-        in_specs=[ANYWHERE] * 5,
-        out_specs=ANYWHERE,
-        scratch_shapes=[
-            pltpu.SMEM(lengths.shape, lengths.dtype),
+    late = row_count - split
+
+    def held(count):
+        return [
             pltpu.VMEM((count, heads, latent), jnp.bfloat16),
-            pltpu.VMEM(query_rope.shape, jnp.bfloat16),
             pltpu.VMEM((count, context, latent), jnp.bfloat16),
             pltpu.VMEM((count, rope, context), jnp.bfloat16),
-            pltpu.VMEM((count, heads, latent), jnp.bfloat16),
+        ]
+
+    ql_late, cl_late, cr_late = held(late)
+    out = pl.pallas_call(
+        functools.partial(attend_kernel, split),
+        out_shape=[
+            pltpu.HBM((row_count, heads, latent), jnp.bfloat16),
+            pltpu.VMEM((late, context), jnp.int32),
+            ql_late,
+            pltpu.VMEM(query_rope.shape, jnp.bfloat16),
+            cl_late,
+            cr_late,
+        ],
+        in_specs=[ANYWHERE] * 5,
+        out_specs=[ANYWHERE] + [IN_VMEM] * 5,
+        scratch_shapes=[pltpu.SMEM(lengths.shape, lengths.dtype)]
+        + held(split)
+        + [
+            pltpu.VMEM((split, heads, latent), jnp.bfloat16),
             pltpu.VMEM((row_count * heads // 2, 2 * rope), jnp.float32),
-            pltpu.VMEM((count, heads, context), jnp.float32),
+            pltpu.VMEM((split, heads, context), jnp.float32),
             pltpu.SemaphoreType.DMA((5,)),
+            pltpu.SemaphoreType.DMA((3,)),
         ],
-        compiler_params=pltpu.CompilerParams(vmem_limit_bytes=(count + 4) * 2**20),
-        cost_estimate=attend_cost(count, heads, context, latent, rope),
+        compiler_params=pltpu.CompilerParams(vmem_limit_bytes=(row_count + 4) * 2**20),
+        cost_estimate=attend_cost(split, heads, context, latent, rope),
     )(*map(in_hbm, operands))
+    return out[0], out[1:]
 
 
 def attend_staged(first, staged, so_far):
@@ -163,55 +190,27 @@
     )(*map(in_vmem, staged), so_far)
 
 
-def stage_kernel(first, matrix_hbm, lengths_hbm, ql_hbm, qr_hbm, cl_hbm, cr_hbm, *refs):
-    matrix_ref, limits_ref, ql_ref, qr_ref, cl_ref, cr_ref, lengths_ref, sems = refs
-    rows = ql_ref.shape[0]
-    part = pl.ds(first, rows)
-    pieces = sems.shape[0] - 5
-    step = matrix_hbm.shape[0] // pieces
-    cuts = [pl.ds(i * step, step) for i in range(pieces)]
-    sources = [lengths_hbm, qr_hbm, cr_hbm.at[part], cl_hbm.at[part], ql_hbm.at[part]]
-    targets = [lengths_ref, qr_ref, cr_ref, cl_ref, ql_ref]
-    copies = fetch(
-        sources + [matrix_hbm.at[cut] for cut in cuts],
-        targets + [matrix_ref.at[cut] for cut in cuts],
-        sems,
-    )
-    for i, copy in enumerate(copies):
+def load_kernel(source_hbm, target_ref, sems):
+    step = source_hbm.shape[0] // sems.shape[0]
+    cuts = [pl.ds(i * step, step) for i in range(sems.shape[0])]
+    for copy in fetch(
+        [source_hbm.at[cut] for cut in cuts], [target_ref.at[cut] for cut in cuts], sems
+    ):
         copy.wait()
-        if i == 0:
-            for r in range(rows):
-                limits_ref[pl.ds(r, 1), :] = jnp.full(
-                    (1, limits_ref.shape[1]), lengths_ref[first + r], jnp.int32
-                )
-
-
-def stage(first, count, matrix, query_latent, query_rope, cache_latent, cache_rope, lengths):
-    heads, latent = query_latent.shape[1:]
-    rope, context = cache_rope.shape[1:]
-    operands = (matrix, lengths, query_latent, query_rope, cache_latent, cache_rope)
-    out = pl.pallas_call(
-        functools.partial(stage_kernel, first),
-        out_shape=[
-            pltpu.VMEM(matrix.shape, matrix.dtype),
-            pltpu.VMEM((count, context), jnp.int32),
-            pltpu.VMEM((count, heads, latent), jnp.bfloat16),
-            pltpu.VMEM(query_rope.shape, jnp.bfloat16),
-            pltpu.VMEM((count, context, latent), jnp.bfloat16),
-            pltpu.VMEM((count, rope, context), jnp.bfloat16),
-        ],
-        in_specs=[ANYWHERE] * 6,
-        out_specs=[IN_VMEM] * 6,
-        scratch_shapes=[
-            pltpu.SMEM(lengths.shape, lengths.dtype),
-            pltpu.SemaphoreType.DMA((5 + (4 if matrix.shape[0] % 64 == 0 else 1),)),
-        ],
+
+
+def load(matrix):
+    return pl.pallas_call(
+        load_kernel,
+        out_shape=pltpu.VMEM(matrix.shape, matrix.dtype),
+        in_specs=[ANYWHERE],
+        out_specs=IN_VMEM,
+        scratch_shapes=[pltpu.SemaphoreType.DMA((4 if matrix.shape[0] % 64 == 0 else 1,))],
         compiler_params=pltpu.CompilerParams(vmem_limit_bytes=2**20),
         cost_estimate=pl.CostEstimate(
             flops=0, bytes_accessed=2 * matrix.size, transcendentals=0
         ),
-    )(*map(in_hbm, operands))
-    return out[0], out[1:]
+    )(in_hbm(matrix))
 
 
 def in_hbm(value):
@@ -371,13 +370,13 @@
     count = query_latent.shape[0]
     half = count // 2
     rest = (query_rope, cache_latent, cache_rope, lengths)
-    attended = attend_rows(0, half, tie(query_latent, mine), *rest)
+    attended, staged = attend_first(half, tie(query_latent, mine), *rest)
     near[1], far[0], near[2], _ = lax.optimization_barrier((near[1], far[0], near[2], attended))
     near[3] = swap(near[2], "node", nodes, 1)
     far[2] = swap(near[2], "local", locals_, 1)
     far[1] = swap(far[0], "node", nodes, 1)
     far[3] = swap(near[3], "local", locals_, 1)
-    own, staged = stage(half, count - half, tie(own, near[3]), query_latent, *rest)
+    own = load(tie(own, near[3]))
     far[1], far[2], far[3], _ = lax.optimization_barrier((far[1], far[2], far[3], own))
     blocks = [near[n] for n in range(nodes)] + [far[n] for n in range(nodes)]
     kept, sent = serve(blocks, own, other)
@@ -408,8 +407,9 @@
     attention = (query_latent, query_rope, cache_latent, cache_rope, lengths)
     if sizes == (4, 2, 2):
         return gathered(attention, tokens, expert_ids, combine_weights, expert_weight)
-    count = query_latent.shape[0]
-    attended = attend_rows(0, count, query_latent, query_rope, cache_latent, cache_rope, lengths)
+    half = query_latent.shape[0] // 2
+    attended, staged = attend_first(half, *attention)
+    attended = attend_staged(half, staged, attended)
     expert_mix = expert_by_slots(tokens, expert_ids, combine_weights, expert_weight)
     return (expert_mix, attended)
 

time: 40.4 us -> 39.8 us (0.985)
  starting transfers between devices: 14.8 us -> 14.2 us
    ppermute x12, starting transfers between devices: 14.8 us -> 14.2 us  [swap(): return lax.ppermute(value, axis, [(i, i ^ mask) for i in range(size)])]
  transfers between devices with their start and end apart: 12 -> 12, of which waited for: 8 -> 7; matrix products, arithmetic and copies ran while one was open for 0% -> 0% of each run, Pallas kernels for 24% -> 24%
where the time goes in v4:
time: 39.8 us; the launch traced here: 39.7 us
  starting transfers between devices  14.2 us (36%)
  Pallas kernels  12.2 us (31%)
  waiting for transfers between devices  11.9 us (30%)
  between operations  0.71 us (2%)
  other arithmetic  0.67 us (2%)
    ppermute x12, starting transfers between devices, swap(): return lax.ppermute(value, axis, [(i, i ^ mask) for i in range(size)])  14.2 us
    ppermute x12, waiting for transfers between devices, swap(): return lax.ppermute(value, axis, [(i, i ^ mask) for i in range(size)])  11.9 us
    pallas_call x1, Pallas kernels, attend_first(): pl.pallas_call(functools.partial(attend_kernel, split), out_shape=[pltpu....  3.71 us
    pallas_call x1, Pallas kernels, load(): pl.pallas_call(load_kernel, out_shape=pltpu.VMEM(matrix.shape, matrix.dty...  3.18 us
    pallas_call x1, Pallas kernels, serve(): pl.pallas_call(functools.partial(expert_kernel, count), out_shape=[pltpu....  2.6 us
    pallas_call x1, Pallas kernels, attend_staged(): pl.pallas_call(functools.partial(staged_kernel, first), out_shape=pltpu.H...  1.77 us
    pallas_call x1, Pallas kernels, make_payload(): pl.pallas_call(payload_kernel, out_shape=pltpu.VMEM((rows, width + LANES)...  0.96 us
  transfers between devices with their start and end apart: 12, of which 7 were waited for; matrix products, arithmetic and copies ran while one was open for 0% of the time, Pallas kernels for 24%

profile of v4, /device:TPU:0, one launch (start us, length us, event | category | flops | bytes accessed | tf_op | source)
XLA Modules:
  0.0 39.7 jit_solution(13826304287274536247)
XLA Ops:
  0.6 0.5 %collective-permute-start.7 = (bf16[3584,1024]{1,0:T(8,128)(2,1)}, bf16[3584,1024]{1,0:T(8,128)(2,1)S(1)}, u32[]{:S(2)}, u32[]{:S(2)}) collective-permute-start(bf16[3584,1024]{1,0:T(8,128)(2,1)} %bitcast.3), channel_id=1, source_target_pairs={{0,1},{1,0},{2,3},{3,2},{4,5},{5,4},{6,7},{7,6},{8,9},{9,8},{10,11... | collective-permute-start | bytes 22020104 | tf_op jit(solution)/shard_map/ppermute | solution.py:351
  1.1 1.0 %shard_map.104.refs_0_ = bf16[16,3712]{1,0:T(8,128)(2,1)S(1)} custom-call(s32[8,16]{1,0:T(8,128)} %bitcast.5, bf16[8,16]{1,0:T(8,128)(2,1)} %bitcast.6, bf16[16,3584]{1,0:T(8,128)(2,1)} %tokens_hbm.1), custom_call_target="tpu_custom_call" | custom-call | bytes 229376 | tf_op jit(solution)/shard_map/pallas_call | solution.py:284
  2.1 3.7 %collective-permute-start.2 = (bf16[16,3712]{1,0:T(8,128)(2,1)S(1)}, bf16[16,3712]{1,0:T(8,128)(2,1)S(1)}, u32[]{:S(2)}, u32[]{:S(2)}) collective-permute-start(bf16[16,3712]{1,0:T(8,128)(2,1)S(1)} %shard_map.104.refs_0_), channel_id=1, source_target_pairs={{0,8},{4,12},{8,0},{12,4},{1,9},{5,13},{9,1},{13,5},{2,10},{6,14},... | collective-permute-start | bytes 356360 | tf_op jit(solution)/shard_map/ppermute | solution.py:351
  5.8 1.5 %collective-permute-start.1 = (bf16[16,3712]{1,0:T(8,128)(2,1)S(1)}, bf16[16,3712]{1,0:T(8,128)(2,1)S(1)}, u32[]{:S(2)}, u32[]{:S(2)}) collective-permute-start(bf16[16,3712]{1,0:T(8,128)(2,1)S(1)} %shard_map.104.refs_0_), channel_id=1, source_target_pairs={{0,2},{2,0},{1,3},{3,1},{4,6},{6,4},{5,7},{7,5},{8,10},{10,8},{9,1... | collective-permute-start | bytes 356360 | tf_op jit(solution)/shard_map/ppermute | solution.py:351
  7.3 1.6 %collective-permute-start = (bf16[16,3712]{1,0:T(8,128)(2,1)S(1)}, bf16[16,3712]{1,0:T(8,128)(2,1)S(1)}, u32[]{:S(2)}, u32[]{:S(2)}) collective-permute-start(bf16[16,3712]{1,0:T(8,128)(2,1)S(1)} %shard_map.104.refs_0_), channel_id=1, source_target_pairs={{0,4},{4,0},{8,12},{12,8},{1,5},{5,1},{9,13},{13,9},{2,6},{6,2},{1... | collective-permute-start | bytes 356360 | tf_op jit(solution)/shard_map/ppermute | solution.py:351
  8.8 3.7 %shard_map.105 = (bf16[16,64,512]{2,1,0:T(8,128)(2,1)}, s32[8,128]{1,0:T(8,128)S(1)}, bf16[8,64,512]{2,1,0:T(8,128)(2,1)S(1)}, bf16[16,4096]{1,0:T(8,128)(2,1)S(...) custom-call(s32[16]{0:T(128)} %lengths_hbm.1, bf16[16,64,512]{2,1,0:T(8,128)(2,1)} %ql_hbm, ...), custom_call_target="tpu_custom_call" | custom-call | flops 142606336 | bytes 10485760 | tf_op jit(solution)/shard_map/pallas_call | solution.py:145
  12.6 0.0 collective-permute-done.2.refs_2_
  12.6 0.0 collective-permute-done.1.refs_4_
  12.6 1.1 %collective-permute-done.refs_1_ = bf16[16,3712]{1,0:T(8,128)(2,1)S(1)} collective-permute-done((bf16[16,3712]{1,0:T(8,128)(2,1)S(1)}, bf16[16,3712]{1,0:T(8,128)(2,1)S(1)}, u32[]{:S(2)}, u32[]{:S(2)}) %collective-permute-start) | collective-permute-done | bytes 118816 | tf_op jit(solution)/shard_map/ppermute | solution.py:351
  13.7 0.3 collective-permute-start.3
  14.0 1.5 %collective-permute-start.5 = (bf16[16,3712]{1,0:T(8,128)(2,1)S(1)}, bf16[16,3712]{1,0:T(8,128)(2,1)S(1)}, u32[]{:S(2)}, u32[]{:S(2)}) collective-permute-start(bf16[16,3712]{1,0:T(8,128)(2,1)S(1)} %collective-permute-done.2.refs_2_), channel_id=1, source_target_pairs={{0,2},{2,0},{1,3},{3,1},{4,6},{6,4},{5,7},{7,5},{8,10},{10,8},{9,1... | collective-permute-start | bytes 356360 | tf_op jit(solution)/shard_map/ppermute | solution.py:351
  15.5 0.8 %collective-permute-start.4 = (bf16[16,3712]{1,0:T(8,128)(2,1)S(1)}, bf16[16,3712]{1,0:T(8,128)(2,1)S(1)}, u32[]{:S(2)}, u32[]{:S(2)}) collective-permute-start(bf16[16,3712]{1,0:T(8,128)(2,1)S(1)} %collective-permute-done.1.refs_4_), channel_id=1, source_target_pairs={{0,4},{4,0},{8,12},{12,8},{1,5},{5,1},{9,13},{13,9},{2,6},{6,2},{1... | collective-permute-start | bytes 356360 | tf_op jit(solution)/shard_map/ppermute | solution.py:351
  16.3 3.4 %collective-permute-done.3.refs_3_ = bf16[16,3712]{1,0:T(8,128)(2,1)S(1)} collective-permute-done((bf16[16,3712]{1,0:T(8,128)(2,1)S(1)}, bf16[16,3712]{1,0:T(8,128)(2,1)S(1)}, u32[]{:S(2)}, u32[]{:S(2)}) %collective-permute-start.3) | collective-permute-done | bytes 118816 | tf_op jit(solution)/shard_map/ppermute | solution.py:351
  19.8 0.3 collective-permute-start.6
  20.1 3.2 %shard_map.106.refs_8_ = bf16[3584,1024]{1,0:T(8,128)(2,1)S(1)} custom-call(bf16[3584,1024]{1,0:T(8,128)(2,1)} %bitcast.4), custom_call_target="tpu_custom_call" | custom-call | bytes 7340032 | tf_op jit(solution)/shard_map/pallas_call | solution.py:203
  23.3 0.0 collective-permute-done.4.refs_5_
  23.3 0.0 collective-permute-done.5.refs_6_
  23.3 1.3 %collective-permute-done.6.refs_7_ = bf16[16,3712]{1,0:T(8,128)(2,1)S(1)} collective-permute-done((bf16[16,3712]{1,0:T(8,128)(2,1)S(1)}, bf16[16,3712]{1,0:T(8,128)(2,1)S(1)}, u32[]{:S(2)}, u32[]{:S(2)}) %collective-permute-start.6) | collective-permute-done | bytes 118816 | tf_op jit(solution)/shard_map/ppermute | solution.py:351
  24.6 0.0 collective-permute-done.7.refs_9_
  24.6 2.6 %shard_map.107 = (f32[64,1024]{1,0:T(8,128)S(1)}, bf16[64,1024]{1,0:T(8,128)(2,1)S(1)}) custom-call(bf16[16,3712]{1,0:T(8,128)(2,1)S(1)} %shard_map.104.refs_0_, bf16[16,3712]{1,0:T(8,128)(2,1)S(1)} %collective-permute-done.refs_1_, bf16[16,3712]{1,0:T(8,128)(2,1)S(1)} %collective-permute-done.2.refs_2_, ...), custom_call_target="tpu_custom_call" | custom-call | flops 1879048192 | bytes 14680064 | tf_op jit(solution)/shard_map/pallas_call | solution.py:333
  27.2 0.5 %collective-permute-start.8 = (bf16[64,1024]{1,0:T(8,128)(2,1)S(1)}, bf16[64,1024]{1,0:T(8,128)(2,1)S(1)}, u32[]{:S(2)}, u32[]{:S(2)}) collective-permute-start(bf16[64,1024]{1,0:T(8,128)(2,1)S(1)} %get-tuple-element.30), channel_id=1, source_target_pairs={{0,2},{2,0},{1,3},{3,1},{4,6},{6,4},{5,7},{7,5},{8,10},{10,8},{9,1... | collective-permute-start | bytes 393224 | tf_op jit(solution)/shard_map/ppermute | solution.py:351
  27.7 1.8 %shard_map.108 = bf16[16,64,512]{2,1,0:T(8,128)(2,1)} custom-call(s32[8,128]{1,0:T(8,128)S(1)} %get-tuple-element.31.limits_ref, bf16[8,64,512]{2,1,0:T(8,128)(2,1)S(1)} %get-tuple-element.32.ql_ref, bf16[16,4096]{1,0:T(8,128)(2,1)S(1)} %get-tuple-element.33.qr_ref, ...), custom_call_target="tpu_custom_call", output_to_operand_aliasing={{}: (5, {})} | custom-call | flops 142606336 | bytes 10485760 | tf_op jit(solution)/shard_map/pallas_call | solution.py:176
  29.5 2.8 %collective-permute-done.8 = bf16[64,1024]{1,0:T(8,128)(2,1)S(1)} collective-permute-done((bf16[64,1024]{1,0:T(8,128)(2,1)S(1)}, bf16[64,1024]{1,0:T(8,128)(2,1)S(1)}, u32[]{:S(2)}, u32[]{:S(2)}) %collective-permute-start.8) | collective-permute-done | bytes 131104 | tf_op jit(solution)/shard_map/ppermute | solution.py:351
  32.3 0.7 %collective-permute-start.9 = (bf16[16,1024]{1,0:T(8,128)(2,1)S(1)}, bf16[16,1024]{1,0:T(8,128)(2,1)S(1)}, u32[]{:S(2)}, u32[]{:S(2)}) collective-permute-start(bf16[16,1024]{1,0:T(8,128)(2,1)S(1)} %get-tuple-element.38), channel_id=1, source_target_pairs={{0,8},{4,12},{8,0},{12,4},{1,9},{5,13},{9,1},{13,5},{2,10},{6,14},... | collective-permute-start | bytes 98312 | tf_op jit(solution)/shard_map/ppermute | solution.py:351
  32.9 2.1 %collective-permute-start.11 = (bf16[16,1024]{1,0:T(8,128)(2,1)S(1)}, bf16[16,1024]{1,0:T(8,128)(2,1)S(1)}, u32[]{:S(2)}, u32[]{:S(2)}) collective-permute-start(bf16[16,1024]{1,0:T(8,128)(2,1)S(1)} %get-tuple-element.39), channel_id=1, source_target_pairs={{0,12},{4,8},{8,4},{12,0},{1,13},{5,9},{9,5},{13,1},{2,14},{6,10},... | collective-permute-start | bytes 98312 | tf_op jit(solution)/shard_map/ppermute | solution.py:351
  35.0 0.8 %collective-permute-start.10 = (bf16[16,1024]{1,0:T(8,128)(2,1)S(1)}, bf16[16,1024]{1,0:T(8,128)(2,1)S(1)}, u32[]{:S(2)}, u32[]{:S(2)}) collective-permute-start(bf16[16,1024]{1,0:T(8,128)(2,1)S(1)} %get-tuple-element.40), channel_id=1, source_target_pairs={{0,4},{4,0},{8,12},{12,8},{1,5},{5,1},{9,13},{13,9},{2,6},{6,2},{1... | collective-permute-start | bytes 98312 | tf_op jit(solution)/shard_map/ppermute | solution.py:351
  35.8 1.4 %collective-permute-done.9 = bf16[16,1024]{1,0:T(8,128)(2,1)S(1)} collective-permute-done((bf16[16,1024]{1,0:T(8,128)(2,1)S(1)}, bf16[16,1024]{1,0:T(8,128)(2,1)S(1)}, u32[]{:S(2)}, u32[]{:S(2)}) %collective-permute-start.9) | collective-permute-done | bytes 32800 | tf_op jit(solution)/shard_map/ppermute | solution.py:351
  37.3 1.4 %collective-permute-done.11 = bf16[16,1024]{1,0:T(8,128)(2,1)S(1)} collective-permute-done((bf16[16,1024]{1,0:T(8,128)(2,1)S(1)}, bf16[16,1024]{1,0:T(8,128)(2,1)S(1)}, u32[]{:S(2)}, u32[]{:S(2)}) %collective-permute-start.11) | collective-permute-done | bytes 32800 | tf_op jit(solution)/shard_map/ppermute | solution.py:351
  38.7 0.3 collective-permute-done.10
  39.0 0.6 %add_convert_fusion = bf16[16,1024]{1,0:T(8,128)(2,1)} fusion(bf16[16,1024]{1,0:T(8,128)(2,1)S(1)} %collective-permute-done.11, bf16[16,1024]{1,0:T(8,128)(2,1)S(1)} %collective-permute-done.10, bf16[16,1024]{1,0:T(8,128)(2,1)S(1)} %collective-permute-done.9, f32[64,1024]{1,0:T(8,128)S(1)} %get-tuple-element.29, bf16[64,1024]{1,0:T(8,128)(2,1)S(1)} %collective-permute-done.8), kind=kLoop, calls=%fused_computation | loop fusion | flops 147456 | bytes 229376 | tf_op jit(solution)/shard_map/convert_element_type | solution.py:392
  (1 shorter events, 0.0 us)
Async XLA Ops:
  0.6 24.0 %collective-permute-start.7 = (bf16[3584,1024]{1,0:T(8,128)(2,1)}, bf16[3584,1024]{1,0:T(8,128)(2,1)S(1)}, u32[]{:S(2)}, u32[]{:S(2)}) collective-permute-start(bf16[3584,1024]{1,0:T(8,128)(2,1)} %bitcast.3), channel_id=1, source_target_pairs={{0,1},{1,0},{2,3},{3,2},{4,5},{5,4},{6,7},{7,6},{8,9},{9,8},{10,11... | collective-permute-start | bytes 22020104 | tf_op jit(solution)/shard_map/ppermute | solution.py:351
  2.1 10.5 %collective-permute-start.2 = (bf16[16,3712]{1,0:T(8,128)(2,1)S(1)}, bf16[16,3712]{1,0:T(8,128)(2,1)S(1)}, u32[]{:S(2)}, u32[]{:S(2)}) collective-permute-start(bf16[16,3712]{1,0:T(8,128)(2,1)S(1)} %shard_map.104.refs_0_), channel_id=1, source_target_pairs={{0,8},{4,12},{8,0},{12,4},{1,9},{5,13},{9,1},{13,5},{2,10},{6,14},... | collective-permute-start | bytes 356360 | tf_op jit(solution)/shard_map/ppermute | solution.py:351
  5.8 6.8 %collective-permute-start.1 = (bf16[16,3712]{1,0:T(8,128)(2,1)S(1)}, bf16[16,3712]{1,0:T(8,128)(2,1)S(1)}, u32[]{:S(2)}, u32[]{:S(2)}) collective-permute-start(bf16[16,3712]{1,0:T(8,128)(2,1)S(1)} %shard_map.104.refs_0_), channel_id=1, source_target_pairs={{0,2},{2,0},{1,3},{3,1},{4,6},{6,4},{5,7},{7,5},{8,10},{10,8},{9,1... | collective-permute-start | bytes 356360 | tf_op jit(solution)/shard_map/ppermute | solution.py:351
  7.3 6.5 %collective-permute-start = (bf16[16,3712]{1,0:T(8,128)(2,1)S(1)}, bf16[16,3712]{1,0:T(8,128)(2,1)S(1)}, u32[]{:S(2)}, u32[]{:S(2)}) collective-permute-start(bf16[16,3712]{1,0:T(8,128)(2,1)S(1)} %shard_map.104.refs_0_), channel_id=1, source_target_pairs={{0,4},{4,0},{8,12},{12,8},{1,5},{5,1},{9,13},{13,9},{2,6},{6,2},{1... | collective-permute-start | bytes 356360 | tf_op jit(solution)/shard_map/ppermute | solution.py:351
  13.7 6.1 %collective-permute-start.3 = (bf16[16,3712]{1,0:T(8,128)(2,1)S(1)}, bf16[16,3712]{1,0:T(8,128)(2,1)S(1)}, u32[]{:S(2)}, u32[]{:S(2)}) collective-permute-start(bf16[16,3712]{1,0:T(8,128)(2,1)S(1)} %collective-permute-done.2.refs_2_), channel_id=1, source_target_pairs={{0,4},{4,0},{8,12},{12,8},{1,5},{5,1},{9,13},{13,9},{2,6},{6,2},{1... | collective-permute-start | bytes 356360 | tf_op jit(solution)/shard_map/ppermute | solution.py:351
  14.0 9.3 %collective-permute-start.5 = (bf16[16,3712]{1,0:T(8,128)(2,1)S(1)}, bf16[16,3712]{1,0:T(8,128)(2,1)S(1)}, u32[]{:S(2)}, u32[]{:S(2)}) collective-permute-start(bf16[16,3712]{1,0:T(8,128)(2,1)S(1)} %collective-permute-done.2.refs_2_), channel_id=1, source_target_pairs={{0,2},{2,0},{1,3},{3,1},{4,6},{6,4},{5,7},{7,5},{8,10},{10,8},{9,1... | collective-permute-start | bytes 356360 | tf_op jit(solution)/shard_map/ppermute | solution.py:351
  15.5 7.8 %collective-permute-start.4 = (bf16[16,3712]{1,0:T(8,128)(2,1)S(1)}, bf16[16,3712]{1,0:T(8,128)(2,1)S(1)}, u32[]{:S(2)}, u32[]{:S(2)}) collective-permute-start(bf16[16,3712]{1,0:T(8,128)(2,1)S(1)} %collective-permute-done.1.refs_4_), channel_id=1, source_target_pairs={{0,4},{4,0},{8,12},{12,8},{1,5},{5,1},{9,13},{13,9},{2,6},{6,2},{1... | collective-permute-start | bytes 356360 | tf_op jit(solution)/shard_map/ppermute | solution.py:351
  19.8 4.8 %collective-permute-start.6 = (bf16[16,3712]{1,0:T(8,128)(2,1)S(1)}, bf16[16,3712]{1,0:T(8,128)(2,1)S(1)}, u32[]{:S(2)}, u32[]{:S(2)}) collective-permute-start(bf16[16,3712]{1,0:T(8,128)(2,1)S(1)} %collective-permute-done.3.refs_3_), channel_id=1, source_target_pairs={{0,2},{2,0},{1,3},{3,1},{4,6},{6,4},{5,7},{7,5},{8,10},{10,8},{9,1... | collective-permute-start | bytes 356360 | tf_op jit(solution)/shard_map/ppermute | solution.py:351
  27.2 5.0 %collective-permute-start.8 = (bf16[64,1024]{1,0:T(8,128)(2,1)S(1)}, bf16[64,1024]{1,0:T(8,128)(2,1)S(1)}, u32[]{:S(2)}, u32[]{:S(2)}) collective-permute-start(bf16[64,1024]{1,0:T(8,128)(2,1)S(1)} %get-tuple-element.30), channel_id=1, source_target_pairs={{0,2},{2,0},{1,3},{3,1},{4,6},{6,4},{5,7},{7,5},{8,10},{10,8},{9,1... | collective-permute-start | bytes 393224 | tf_op jit(solution)/shard_map/ppermute | solution.py:351
  32.3 5.0 %collective-permute-start.9 = (bf16[16,1024]{1,0:T(8,128)(2,1)S(1)}, bf16[16,1024]{1,0:T(8,128)(2,1)S(1)}, u32[]{:S(2)}, u32[]{:S(2)}) collective-permute-start(bf16[16,1024]{1,0:T(8,128)(2,1)S(1)} %get-tuple-element.38), channel_id=1, source_target_pairs={{0,8},{4,12},{8,0},{12,4},{1,9},{5,13},{9,1},{13,5},{2,10},{6,14},... | collective-permute-start | bytes 98312 | tf_op jit(solution)/shard_map/ppermute | solution.py:351
  32.9 5.7 %collective-permute-start.11 = (bf16[16,1024]{1,0:T(8,128)(2,1)S(1)}, bf16[16,1024]{1,0:T(8,128)(2,1)S(1)}, u32[]{:S(2)}, u32[]{:S(2)}) collective-permute-start(bf16[16,1024]{1,0:T(8,128)(2,1)S(1)} %get-tuple-element.39), channel_id=1, source_target_pairs={{0,12},{4,8},{8,4},{12,0},{1,13},{5,9},{9,5},{13,1},{2,14},{6,10},... | collective-permute-start | bytes 98312 | tf_op jit(solution)/shard_map/ppermute | solution.py:351
  35.0 4.0 %collective-permute-start.10 = (bf16[16,1024]{1,0:T(8,128)(2,1)S(1)}, bf16[16,1024]{1,0:T(8,128)(2,1)S(1)}, u32[]{:S(2)}, u32[]{:S(2)}) collective-permute-start(bf16[16,1024]{1,0:T(8,128)(2,1)S(1)} %get-tuple-element.40), channel_id=1, source_target_pairs={{0,4},{4,0},{8,12},{12,8},{1,5},{5,1},{9,13},{13,9},{2,6},{6,2},{1... | collective-permute-start | bytes 98312 | tf_op jit(solution)/shard_map/ppermute | solution.py:351

commit v5 on v4

--- a/solution.py
+++ b/solution.py
@@ -301,7 +301,7 @@
 def expert_kernel(count, *refs):
     here = lax.axis_index(EXPERT_AXES).astype(jnp.int32)
     blocks, matrices = refs[:count], refs[count : count + 2]
-    near_ref, far_ref = refs[count + 2 :]
+    kept_ref, *sent_refs = refs[count + 2 :]
     width, hidden = matrices[0].shape
     rows = jnp.concatenate([block[...] for block in blocks], axis=0)
     features, shares = rows[:, :width], rows[:, width:].astype(jnp.float32)
@@ -310,7 +310,7 @@
         jnp.sum(jnp.where(lane == (here ^ which), shares, 0.0), axis=1, keepdims=True)
         for which in range(2)
     ]
-    half = near_ref.shape[0]
+    step = kept_ref.shape[0]
     tile = 256
     for n in range(0, hidden, tile):
         total = None
@@ -320,8 +320,9 @@
             )
             term = share[which] * (value / (1.0 + jnp.exp(-value)))
             total = term if total is None else total + term
-        near_ref[:, n : n + tile] = total[:half]
-        far_ref[:, n : n + tile] = total[half:].astype(jnp.bfloat16)
+        kept_ref[:, n : n + tile] = total[:step]
+        for i, sent_ref in enumerate(sent_refs, 1):
+            sent_ref[:, n : n + tile] = total[i * step : (i + 1) * step].astype(jnp.bfloat16)
 
 
 def serve(blocks, own, other):
@@ -329,15 +330,15 @@
     rows = blocks[0].shape[0]
     width, hidden = own.shape
     whole = pl.BlockSpec(memory_space=pltpu.VMEM)
-    half = count // 2 * rows
+    pair = 2 * rows
     return pl.pallas_call(
         functools.partial(expert_kernel, count),
         out_shape=[
-            pltpu.VMEM((half, hidden), jnp.float32),
-            pltpu.VMEM((half, hidden), jnp.bfloat16),
-        ],
+            pltpu.VMEM((pair, hidden), jnp.float32),
+        ]
+        + [pltpu.VMEM((pair, hidden), jnp.bfloat16)] * (count // 2 - 1),
         in_specs=[whole] * (count + 2),
-        out_specs=[whole] * 2,
+        out_specs=[whole] * (count // 2),
         compiler_params=pltpu.CompilerParams(vmem_limit_bytes=VMEM_LIMIT),
         cost_estimate=pl.CostEstimate(
             flops=4 * count * rows * width * hidden,
@@ -378,17 +379,16 @@
     far[3] = swap(near[3], "local", locals_, 1)
     own = load(tie(own, near[3]))
     far[1], far[2], far[3], _ = lax.optimization_barrier((far[1], far[2], far[3], own))
-    blocks = [near[n] for n in range(nodes)] + [far[n] for n in range(nodes)]
-    kept, sent = serve(blocks, own, other)
-    came = swap(sent, "local", locals_, 1)
-    attended = attend_staged(half, staged, tie(attended, sent))
-    came = tie(came, attended)
-    kept = kept.reshape(nodes, rows, -1)
-    came = came.reshape(nodes, rows, -1)
-    total = kept[0] + came[0].astype(jnp.float32)
-    for n in (2, 1, 3):
-        part = (kept[n] + came[n].astype(jnp.float32)).astype(jnp.bfloat16)
-        total = total + swap(part, "node", nodes, n).astype(jnp.float32)
+    blocks = [block for n in range(nodes) for block in (near[n], far[n])]
+    total, *sent = serve(blocks, own, other)
+    came = [swap(sent[n - 1], "node", nodes, n) for n in (2, 3, 1)]
+    attended = attend_staged(half, staged, tie(attended, *sent))
+    came = lax.optimization_barrier(came + [attended])
+    attended = came.pop()
+    for value in came:
+        total = total + value.astype(jnp.float32)
+    came = swap(total[rows:].astype(jnp.bfloat16), "local", locals_, 1)
+    total = total[:rows] + came.astype(jnp.float32)
     return total.astype(jnp.bfloat16), attended
 
 

time: 39.8 us -> 39.5 us (level)
  waiting for transfers between devices: 11.9 us -> 10.4 us
  starting transfers between devices: 14.2 us -> 15.3 us
    ppermute x12, waiting for transfers between devices: 11.9 us -> 10.4 us  [swap(): return lax.ppermute(value, axis, [(i, i ^ mask) for i in range(size)])]
    ppermute x12, starting transfers between devices: 14.2 us -> 15.3 us  [swap(): return lax.ppermute(value, axis, [(i, i ^ mask) for i in range(size)])]
where the time goes in v5:
time: 39.5 us; the launch traced here: 39.3 us
  starting transfers between devices  15.3 us (39%)
  Pallas kernels  12.2 us (31%)
  waiting for transfers between devices  10.4 us (26%)
  between operations  0.72 us (2%)
  other arithmetic  0.66 us (2%)
    ppermute x12, starting transfers between devices, swap(): return lax.ppermute(value, axis, [(i, i ^ mask) for i in range(size)])  15.3 us
    ppermute x12, waiting for transfers between devices, swap(): return lax.ppermute(value, axis, [(i, i ^ mask) for i in range(size)])  10.4 us
    pallas_call x1, Pallas kernels, attend_first(): pl.pallas_call(functools.partial(attend_kernel, split), out_shape=[pltpu....  3.71 us
    pallas_call x1, Pallas kernels, load(): pl.pallas_call(load_kernel, out_shape=pltpu.VMEM(matrix.shape, matrix.dty...  3.18 us
    pallas_call x1, Pallas kernels, serve(): pl.pallas_call(functools.partial(expert_kernel, count), out_shape=[pltpu....  2.57 us
    pallas_call x1, Pallas kernels, attend_staged(): pl.pallas_call(functools.partial(staged_kernel, first), out_shape=pltpu.H...  1.77 us
    pallas_call x1, Pallas kernels, make_payload(): pl.pallas_call(payload_kernel, out_shape=pltpu.VMEM((rows, width + LANES)...  0.96 us
  transfers between devices with their start and end apart: 12, of which 7 were waited for; matrix products, arithmetic and copies ran while one was open for 0% of the time, Pallas kernels for 24%

profile of v5, /device:TPU:0, one launch (start us, length us, event | category | flops | bytes accessed | tf_op | source)
XLA Modules:
  0.0 39.3 jit_solution(8178454609851617256)
XLA Ops:
  0.6 0.5 %collective-permute-start.7 = (bf16[3584,1024]{1,0:T(8,128)(2,1)}, bf16[3584,1024]{1,0:T(8,128)(2,1)S(1)}, u32[]{:S(2)}, u32[]{:S(2)}) collective-permute-start(bf16[3584,1024]{1,0:T(8,128)(2,1)} %bitcast.3), channel_id=1, source_target_pairs={{0,1},{1,0},{2,3},{3,2},{4,5},{5,4},{6,7},{7,6},{8,9},{9,8},{10,11... | collective-permute-start | bytes 22020104 | tf_op jit(solution)/shard_map/ppermute | solution.py:352
  1.1 1.0 %shard_map.104.refs_0_ = bf16[16,3712]{1,0:T(8,128)(2,1)S(1)} custom-call(s32[8,16]{1,0:T(8,128)} %bitcast.5, bf16[8,16]{1,0:T(8,128)(2,1)} %bitcast.6, bf16[16,3584]{1,0:T(8,128)(2,1)} %tokens_hbm.1), custom_call_target="tpu_custom_call" | custom-call | bytes 229376 | tf_op jit(solution)/shard_map/pallas_call | solution.py:284
  2.1 3.7 %collective-permute-start.2 = (bf16[16,3712]{1,0:T(8,128)(2,1)S(1)}, bf16[16,3712]{1,0:T(8,128)(2,1)S(1)}, u32[]{:S(2)}, u32[]{:S(2)}) collective-permute-start(bf16[16,3712]{1,0:T(8,128)(2,1)S(1)} %shard_map.104.refs_0_), channel_id=1, source_target_pairs={{0,8},{4,12},{8,0},{12,4},{1,9},{5,13},{9,1},{13,5},{2,10},{6,14},... | collective-permute-start | bytes 356360 | tf_op jit(solution)/shard_map/ppermute | solution.py:352
  5.8 1.5 %collective-permute-start.1 = (bf16[16,3712]{1,0:T(8,128)(2,1)S(1)}, bf16[16,3712]{1,0:T(8,128)(2,1)S(1)}, u32[]{:S(2)}, u32[]{:S(2)}) collective-permute-start(bf16[16,3712]{1,0:T(8,128)(2,1)S(1)} %shard_map.104.refs_0_), channel_id=1, source_target_pairs={{0,2},{2,0},{1,3},{3,1},{4,6},{6,4},{5,7},{7,5},{8,10},{10,8},{9,1... | collective-permute-start | bytes 356360 | tf_op jit(solution)/shard_map/ppermute | solution.py:352
  7.3 1.6 %collective-permute-start = (bf16[16,3712]{1,0:T(8,128)(2,1)S(1)}, bf16[16,3712]{1,0:T(8,128)(2,1)S(1)}, u32[]{:S(2)}, u32[]{:S(2)}) collective-permute-start(bf16[16,3712]{1,0:T(8,128)(2,1)S(1)} %shard_map.104.refs_0_), channel_id=1, source_target_pairs={{0,4},{4,0},{8,12},{12,8},{1,5},{5,1},{9,13},{13,9},{2,6},{6,2},{1... | collective-permute-start | bytes 356360 | tf_op jit(solution)/shard_map/ppermute | solution.py:352
  8.8 3.7 %shard_map.105 = (bf16[16,64,512]{2,1,0:T(8,128)(2,1)}, s32[8,128]{1,0:T(8,128)S(1)}, bf16[8,64,512]{2,1,0:T(8,128)(2,1)S(1)}, bf16[16,4096]{1,0:T(8,128)(2,1)S(...) custom-call(s32[16]{0:T(128)} %lengths_hbm.1, bf16[16,64,512]{2,1,0:T(8,128)(2,1)} %ql_hbm, ...), custom_call_target="tpu_custom_call" | custom-call | flops 142606336 | bytes 10485760 | tf_op jit(solution)/shard_map/pallas_call | solution.py:145
  12.6 0.0 collective-permute-done.2.refs_4_
  12.6 0.0 collective-permute-done.1.refs_1_
  12.6 1.1 %collective-permute-done.refs_2_ = bf16[16,3712]{1,0:T(8,128)(2,1)S(1)} collective-permute-done((bf16[16,3712]{1,0:T(8,128)(2,1)S(1)}, bf16[16,3712]{1,0:T(8,128)(2,1)S(1)}, u32[]{:S(2)}, u32[]{:S(2)}) %collective-permute-start) | collective-permute-done | bytes 118816 | tf_op jit(solution)/shard_map/ppermute | solution.py:352
  13.7 0.3 collective-permute-start.5
  14.0 1.5 %collective-permute-start.4 = (bf16[16,3712]{1,0:T(8,128)(2,1)S(1)}, bf16[16,3712]{1,0:T(8,128)(2,1)S(1)}, u32[]{:S(2)}, u32[]{:S(2)}) collective-permute-start(bf16[16,3712]{1,0:T(8,128)(2,1)S(1)} %collective-permute-done.2.refs_4_), channel_id=1, source_target_pairs={{0,2},{2,0},{1,3},{3,1},{4,6},{6,4},{5,7},{7,5},{8,10},{10,8},{9,1... | collective-permute-start | bytes 356360 | tf_op jit(solution)/shard_map/ppermute | solution.py:352
  15.5 0.8 %collective-permute-start.3 = (bf16[16,3712]{1,0:T(8,128)(2,1)S(1)}, bf16[16,3712]{1,0:T(8,128)(2,1)S(1)}, u32[]{:S(2)}, u32[]{:S(2)}) collective-permute-start(bf16[16,3712]{1,0:T(8,128)(2,1)S(1)} %collective-permute-done.1.refs_1_), channel_id=1, source_target_pairs={{0,4},{4,0},{8,12},{12,8},{1,5},{5,1},{9,13},{13,9},{2,6},{6,2},{1... | collective-permute-start | bytes 356360 | tf_op jit(solution)/shard_map/ppermute | solution.py:352
  16.3 3.4 %collective-permute-done.5.refs_6_ = bf16[16,3712]{1,0:T(8,128)(2,1)S(1)} collective-permute-done((bf16[16,3712]{1,0:T(8,128)(2,1)S(1)}, bf16[16,3712]{1,0:T(8,128)(2,1)S(1)}, u32[]{:S(2)}, u32[]{:S(2)}) %collective-permute-start.5) | collective-permute-done | bytes 118816 | tf_op jit(solution)/shard_map/ppermute | solution.py:352
  19.8 0.3 collective-permute-start.6
  20.1 3.2 %shard_map.106.refs_8_ = bf16[3584,1024]{1,0:T(8,128)(2,1)S(1)} custom-call(bf16[3584,1024]{1,0:T(8,128)(2,1)} %bitcast.4), custom_call_target="tpu_custom_call" | custom-call | bytes 7340032 | tf_op jit(solution)/shard_map/pallas_call | solution.py:203
  23.3 0.0 collective-permute-done.3.refs_3_
  23.3 0.0 collective-permute-done.4.refs_5_
  23.3 1.3 %collective-permute-done.6.refs_7_ = bf16[16,3712]{1,0:T(8,128)(2,1)S(1)} collective-permute-done((bf16[16,3712]{1,0:T(8,128)(2,1)S(1)}, bf16[16,3712]{1,0:T(8,128)(2,1)S(1)}, u32[]{:S(2)}, u32[]{:S(2)}) %collective-permute-start.6) | collective-permute-done | bytes 118816 | tf_op jit(solution)/shard_map/ppermute | solution.py:352
  24.6 0.0 collective-permute-done.7.refs_9_
  24.6 2.6 %shard_map.107 = (f32[32,1024]{1,0:T(8,128)S(1)}, bf16[32,1024]{1,0:T(8,128)(2,1)S(1)}, bf16[32,1024]{1,0:T(8,128)(2,1)S(1)}, bf16[32,1024]{1,0:T(8,128)(2,1)S(1)}) custom-call(bf16[16,3712]{1,0:T(8,128)(2,1)S(1)} %shard_map.104.refs_0_, bf16[16,3712]{1,0:T(8,128)(2,1)S(1)} %collective-permute-done.1.refs_1_, ...), custom_call_target="tpu_custom_call" | custom-call | flops 1879048192 | bytes 14680064 | tf_op jit(solution)/shard_map/pallas_call | solution.py:334
  27.2 0.7 %collective-permute-start.8 = (bf16[32,1024]{1,0:T(8,128)(2,1)S(1)}, bf16[32,1024]{1,0:T(8,128)(2,1)S(1)}, u32[]{:S(2)}, u32[]{:S(2)}) collective-permute-start(bf16[32,1024]{1,0:T(8,128)(2,1)S(1)} %get-tuple-element.35), channel_id=1, source_target_pairs={{0,8},{4,12},{8,0},{12,4},{1,9},{5,13},{9,1},{13,5},{2,10},{6,14},... | collective-permute-start | bytes 196616 | tf_op jit(solution)/shard_map/ppermute | solution.py:352
  27.9 2.1 %collective-permute-start.9 = (bf16[32,1024]{1,0:T(8,128)(2,1)S(1)}, bf16[32,1024]{1,0:T(8,128)(2,1)S(1)}, u32[]{:S(2)}, u32[]{:S(2)}) collective-permute-start(bf16[32,1024]{1,0:T(8,128)(2,1)S(1)} %get-tuple-element.36), channel_id=1, source_target_pairs={{0,12},{4,8},{8,4},{12,0},{1,13},{5,9},{9,5},{13,1},{2,14},{6,10},... | collective-permute-start | bytes 196616 | tf_op jit(solution)/shard_map/ppermute | solution.py:352
  29.9 0.8 %collective-permute-start.10 = (bf16[32,1024]{1,0:T(8,128)(2,1)S(1)}, bf16[32,1024]{1,0:T(8,128)(2,1)S(1)}, u32[]{:S(2)}, u32[]{:S(2)}) collective-permute-start(bf16[32,1024]{1,0:T(8,128)(2,1)S(1)} %get-tuple-element.37), channel_id=1, source_target_pairs={{0,4},{4,0},{8,12},{12,8},{1,5},{5,1},{9,13},{13,9},{2,6},{6,2},{1... | collective-permute-start | bytes 196616 | tf_op jit(solution)/shard_map/ppermute | solution.py:352
  30.8 1.8 %shard_map.108 = bf16[16,64,512]{2,1,0:T(8,128)(2,1)} custom-call(s32[8,128]{1,0:T(8,128)S(1)} %get-tuple-element.38.limits_ref, bf16[8,64,512]{2,1,0:T(8,128)(2,1)S(1)} %get-tuple-element.39.ql_ref, bf16[16,4096]{1,0:T(8,128)(2,1)S(1)} %get-tuple-element.40.qr_ref, ...), custom_call_target="tpu_custom_call", output_to_operand_aliasing={{}: (5, {})} | custom-call | flops 142606336 | bytes 10485760 | tf_op jit(solution)/shard_map/pallas_call | solution.py:176
  32.5 0.5 %collective-permute-done.8 = bf16[32,1024]{1,0:T(8,128)(2,1)S(1)} collective-permute-done((bf16[32,1024]{1,0:T(8,128)(2,1)S(1)}, bf16[32,1024]{1,0:T(8,128)(2,1)S(1)}, u32[]{:S(2)}, u32[]{:S(2)}) %collective-permute-start.8) | collective-permute-done | bytes 65568 | tf_op jit(solution)/shard_map/ppermute | solution.py:352
  33.0 1.1 %collective-permute-done.9 = bf16[32,1024]{1,0:T(8,128)(2,1)S(1)} collective-permute-done((bf16[32,1024]{1,0:T(8,128)(2,1)S(1)}, bf16[32,1024]{1,0:T(8,128)(2,1)S(1)}, u32[]{:S(2)}, u32[]{:S(2)}) %collective-permute-start.9) | collective-permute-done | bytes 65568 | tf_op jit(solution)/shard_map/ppermute | solution.py:352
  34.0 0.6 %collective-permute-done.10 = bf16[32,1024]{1,0:T(8,128)(2,1)S(1)} collective-permute-done((bf16[32,1024]{1,0:T(8,128)(2,1)S(1)}, bf16[32,1024]{1,0:T(8,128)(2,1)S(1)}, u32[]{:S(2)}, u32[]{:S(2)}) %collective-permute-start.10) | collective-permute-done | bytes 65568 | tf_op jit(solution)/shard_map/ppermute | solution.py:352
  34.7 1.6 %collective-permute-start.11 = (bf16[16,1024]{1,0:T(8,128)(2,1)S(1)}, bf16[16,1024]{1,0:T(8,128)(2,1)S(1)}, u32[]{:S(2)}, u32[]{:S(2)}) collective-permute-start(bf16[16,1024]{1,0:T(8,128)(2,1)S(1)} %slice.15), channel_id=1, source_target_pairs={{0,2},{2,0},{1,3},{3,1},{4,6},{6,4},{5,7},{7,5},{8,10},{10,8},{9,1... | collective-permute-start | bytes 98312 | tf_op jit(solution)/shard_map/ppermute | solution.py:352
  36.3 2.4 %collective-permute-done.11 = bf16[16,1024]{1,0:T(8,128)(2,1)S(1)} collective-permute-done((bf16[16,1024]{1,0:T(8,128)(2,1)S(1)}, bf16[16,1024]{1,0:T(8,128)(2,1)S(1)}, u32[]{:S(2)}, u32[]{:S(2)}) %collective-permute-start.11) | collective-permute-done | bytes 32800 | tf_op jit(solution)/shard_map/ppermute | solution.py:352
  38.7 0.6 %fusion = bf16[16,1024]{1,0:T(8,128)(2,1)} fusion(f32[32,1024]{1,0:T(8,128)S(1)} %convert_add_fusion, bf16[16,1024]{1,0:T(8,128)(2,1)S(1)} %collective-permute-done.11), kind=kLoop, calls=%fused_computation.3 | loop fusion | flops 49152 | bytes 131072 | tf_op jit(solution)/shard_map/convert_element_type | solution.py:392
  (2 shorter events, 0.0 us)
Async XLA Ops:
  0.6 24.0 %collective-permute-start.7 = (bf16[3584,1024]{1,0:T(8,128)(2,1)}, bf16[3584,1024]{1,0:T(8,128)(2,1)S(1)}, u32[]{:S(2)}, u32[]{:S(2)}) collective-permute-start(bf16[3584,1024]{1,0:T(8,128)(2,1)} %bitcast.3), channel_id=1, source_target_pairs={{0,1},{1,0},{2,3},{3,2},{4,5},{5,4},{6,7},{7,6},{8,9},{9,8},{10,11... | collective-permute-start | bytes 22020104 | tf_op jit(solution)/shard_map/ppermute | solution.py:352
  2.1 10.5 %collective-permute-start.2 = (bf16[16,3712]{1,0:T(8,128)(2,1)S(1)}, bf16[16,3712]{1,0:T(8,128)(2,1)S(1)}, u32[]{:S(2)}, u32[]{:S(2)}) collective-permute-start(bf16[16,3712]{1,0:T(8,128)(2,1)S(1)} %shard_map.104.refs_0_), channel_id=1, source_target_pairs={{0,8},{4,12},{8,0},{12,4},{1,9},{5,13},{9,1},{13,5},{2,10},{6,14},... | collective-permute-start | bytes 356360 | tf_op jit(solution)/shard_map/ppermute | solution.py:352
  5.8 6.8 %collective-permute-start.1 = (bf16[16,3712]{1,0:T(8,128)(2,1)S(1)}, bf16[16,3712]{1,0:T(8,128)(2,1)S(1)}, u32[]{:S(2)}, u32[]{:S(2)}) collective-permute-start(bf16[16,3712]{1,0:T(8,128)(2,1)S(1)} %shard_map.104.refs_0_), channel_id=1, source_target_pairs={{0,2},{2,0},{1,3},{3,1},{4,6},{6,4},{5,7},{7,5},{8,10},{10,8},{9,1... | collective-permute-start | bytes 356360 | tf_op jit(solution)/shard_map/ppermute | solution.py:352
  7.3 6.5 %collective-permute-start = (bf16[16,3712]{1,0:T(8,128)(2,1)S(1)}, bf16[16,3712]{1,0:T(8,128)(2,1)S(1)}, u32[]{:S(2)}, u32[]{:S(2)}) collective-permute-start(bf16[16,3712]{1,0:T(8,128)(2,1)S(1)} %shard_map.104.refs_0_), channel_id=1, source_target_pairs={{0,4},{4,0},{8,12},{12,8},{1,5},{5,1},{9,13},{13,9},{2,6},{6,2},{1... | collective-permute-start | bytes 356360 | tf_op jit(solution)/shard_map/ppermute | solution.py:352
  13.7 6.1 %collective-permute-start.5 = (bf16[16,3712]{1,0:T(8,128)(2,1)S(1)}, bf16[16,3712]{1,0:T(8,128)(2,1)S(1)}, u32[]{:S(2)}, u32[]{:S(2)}) collective-permute-start(bf16[16,3712]{1,0:T(8,128)(2,1)S(1)} %collective-permute-done.2.refs_4_), channel_id=1, source_target_pairs={{0,4},{4,0},{8,12},{12,8},{1,5},{5,1},{9,13},{13,9},{2,6},{6,2},{1... | collective-permute-start | bytes 356360 | tf_op jit(solution)/shard_map/ppermute | solution.py:352
  14.0 9.3 %collective-permute-start.4 = (bf16[16,3712]{1,0:T(8,128)(2,1)S(1)}, bf16[16,3712]{1,0:T(8,128)(2,1)S(1)}, u32[]{:S(2)}, u32[]{:S(2)}) collective-permute-start(bf16[16,3712]{1,0:T(8,128)(2,1)S(1)} %collective-permute-done.2.refs_4_), channel_id=1, source_target_pairs={{0,2},{2,0},{1,3},{3,1},{4,6},{6,4},{5,7},{7,5},{8,10},{10,8},{9,1... | collective-permute-start | bytes 356360 | tf_op jit(solution)/shard_map/ppermute | solution.py:352
  15.5 7.8 %collective-permute-start.3 = (bf16[16,3712]{1,0:T(8,128)(2,1)S(1)}, bf16[16,3712]{1,0:T(8,128)(2,1)S(1)}, u32[]{:S(2)}, u32[]{:S(2)}) collective-permute-start(bf16[16,3712]{1,0:T(8,128)(2,1)S(1)} %collective-permute-done.1.refs_1_), channel_id=1, source_target_pairs={{0,4},{4,0},{8,12},{12,8},{1,5},{5,1},{9,13},{13,9},{2,6},{6,2},{1... | collective-permute-start | bytes 356360 | tf_op jit(solution)/shard_map/ppermute | solution.py:352
  19.8 4.8 %collective-permute-start.6 = (bf16[16,3712]{1,0:T(8,128)(2,1)S(1)}, bf16[16,3712]{1,0:T(8,128)(2,1)S(1)}, u32[]{:S(2)}, u32[]{:S(2)}) collective-permute-start(bf16[16,3712]{1,0:T(8,128)(2,1)S(1)} %collective-permute-done.5.refs_6_), channel_id=1, source_target_pairs={{0,2},{2,0},{1,3},{3,1},{4,6},{6,4},{5,7},{7,5},{8,10},{10,8},{9,1... | collective-permute-start | bytes 356360 | tf_op jit(solution)/shard_map/ppermute | solution.py:352
  27.2 5.8 %collective-permute-start.8 = (bf16[32,1024]{1,0:T(8,128)(2,1)S(1)}, bf16[32,1024]{1,0:T(8,128)(2,1)S(1)}, u32[]{:S(2)}, u32[]{:S(2)}) collective-permute-start(bf16[32,1024]{1,0:T(8,128)(2,1)S(1)} %get-tuple-element.35), channel_id=1, source_target_pairs={{0,8},{4,12},{8,0},{12,4},{1,9},{5,13},{9,1},{13,5},{2,10},{6,14},... | collective-permute-start | bytes 196616 | tf_op jit(solution)/shard_map/ppermute | solution.py:352
  27.9 6.2 %collective-permute-start.9 = (bf16[32,1024]{1,0:T(8,128)(2,1)S(1)}, bf16[32,1024]{1,0:T(8,128)(2,1)S(1)}, u32[]{:S(2)}, u32[]{:S(2)}) collective-permute-start(bf16[32,1024]{1,0:T(8,128)(2,1)S(1)} %get-tuple-element.36), channel_id=1, source_target_pairs={{0,12},{4,8},{8,4},{12,0},{1,13},{5,9},{9,5},{13,1},{2,14},{6,10},... | collective-permute-start | bytes 196616 | tf_op jit(solution)/shard_map/ppermute | solution.py:352
  29.9 4.7 %collective-permute-start.10 = (bf16[32,1024]{1,0:T(8,128)(2,1)S(1)}, bf16[32,1024]{1,0:T(8,128)(2,1)S(1)}, u32[]{:S(2)}, u32[]{:S(2)}) collective-permute-start(bf16[32,1024]{1,0:T(8,128)(2,1)S(1)} %get-tuple-element.37), channel_id=1, source_target_pairs={{0,4},{4,0},{8,12},{12,8},{1,5},{5,1},{9,13},{13,9},{2,6},{6,2},{1... | collective-permute-start | bytes 196616 | tf_op jit(solution)/shard_map/ppermute | solution.py:352
  34.7 4.0 %collective-permute-start.11 = (bf16[16,1024]{1,0:T(8,128)(2,1)S(1)}, bf16[16,1024]{1,0:T(8,128)(2,1)S(1)}, u32[]{:S(2)}, u32[]{:S(2)}) collective-permute-start(bf16[16,1024]{1,0:T(8,128)(2,1)S(1)} %slice.15), channel_id=1, source_target_pairs={{0,2},{2,0},{1,3},{3,1},{4,6},{6,4},{5,7},{7,5},{8,10},{10,8},{9,1... | collective-permute-start | bytes 98312 | tf_op jit(solution)/shard_map/ppermute | solution.py:352
